TPU v7x, 512 devices: a whole 4x4x16 slice. The times are simulated.
512 devices in a mesh: row: 128 (over x, z, y_hi), ch: 4 (over y_lo, core).
Axes of the slice: x: 4, y: 4 (y_hi: 2, y_lo: 2; y = y_hi * 2 + y_lo), z: 16, core: 2. Of those that a mesh axis runs over, the one named last changes fastest.
Arguments:
- pair_rep: bfloat16 [128, 128, 128], P('ch', 'row'), may hold values from -6 to 6
- residue_mask: int32 [128], replicated, may hold values 0 or 1
- chain_ids: int32 [128], replicated, may hold values from 0 to 3, never falling along the last dimension, each value on 1 to 64 neighbouring positions
- in_gain: float32 [2, 128], replicated, may hold values from 0.5 to 1.5
- in_bias: float32 [2, 128], replicated, may hold values from -3 to 3
- w_proj: bfloat16 [2, 128, 4, 128], P(None, None, None, 'ch'), may hold values from -0.5 to 0.5
- w_gate: bfloat16 [2, 128, 128], P(None, None, 'ch'), may hold values from -0.5 to 0.5
- pair_bias: float32 [2, 128], P(None, 'ch'), may hold values from -4 to 4
- out_gain: float32 [2, 128], P(None, 'ch'), may hold values from 0.5 to 1.5
- out_bias: float32 [2, 128], P(None, 'ch'), may hold values from -3 to 3
- w_out: bfloat16 [2, 128, 128], P(None, 'ch'), may hold values from -0.5 to 0.5
Outputs:
- pair_out: bfloat16 [128, 128, 128], P('ch', 'row')
Inputs may be any that keep to these rules, and one draw needn't show every extreme that they name: `chain_ids`: chain numbers never fall along the residues; each chain has 1 to 64 residues.
All inputs are finite; a program needn't handle non-finite values.
Results may differ from a plain program's by a relative error of at most 0.013.
Values may be sent and summed in bfloat16 or wider, within the bound.
No kernel may reach another device: no remote copies, remote signals or barrier semaphores. Data moves between devices by JAX's collectives and lax.ppermute only.
A program may use at most 64 MiB of HBM per device.

v0:
```python
import jax
import jax.numpy as jnp
from jax import lax
from jax.sharding import PartitionSpec as P

epsilon = 1e-05


def in_order(tiles, dim):
    tiles = jnp.moveaxis(tiles, 0, dim)
    dims = tiles.shape
    return tiles.reshape(*dims[:dim], dims[dim] * dims[dim + 1], *dims[dim + 2 :])


def from_everyone(x, axis):
    devices = lax.axis_size(axis)
    return lax.all_to_all(jnp.broadcast_to(x[None], (devices, *x.shape)), axis, 0, 0, tiled=True)


def gathered_copies(x, axis, dim):
    return in_order(from_everyone(x, axis), dim)


def of_everyone(x, axis):
    return from_everyone(x, axis).sum(axis=0)


def together(arrays, axis):
    ends = [0]
    for a in arrays:
        ends.append(ends[-1] + a.size)
    so_far = of_everyone(jnp.concatenate([a.ravel() for a in arrays]), axis)
    return tuple((so_far[b:e].reshape(a.shape) for a, b, e in zip(arrays, ends, ends[1:])))


def in_blocks(x, dim, devices):
    before, after = (x.shape[:dim], x.shape[dim + 1 :])
    return jnp.moveaxis(x.reshape(*before, devices, -1, *after), dim, 0)


def sum_at_owner(x, axis, dim):
    devices = lax.axis_size(axis)
    tiles = lax.all_to_all(in_blocks(x, dim, devices), axis, 0, 0, tiled=True)
    return jnp.sum(tiles.astype(jnp.float32), axis=0)


def sent_together(arrays, axis, split_dim, concat_dim, along):
    widths = [a.shape[along] for a in arrays]
    both = jnp.concatenate(arrays, axis=along)
    result = lax.all_to_all(both, axis, split_axis=split_dim, concat_axis=concat_dim, tiled=True)
    return tuple(jnp.split(result, [sum(widths[:k]) for k in range(1, len(widths))], axis=along))


def channel_norm(values, norm_gain, norm_bias):
    mean_val = jnp.mean(values, axis=0)
    variance = jnp.mean(values * values, axis=0) - mean_val * mean_val
    return (values - mean_val) * lax.rsqrt(variance + epsilon) * norm_gain[
        :, None, None
    ] + norm_bias[:, None, None]


def prepare(
    pair_local, layer, in_gain, in_bias, w_proj, w_gate, pair_bias, mask_rows, mask_cols, same_chain
):
    full_pair = gathered_copies(pair_local, "ch", 0)
    normed = channel_norm(full_pair.astype(jnp.float32), in_gain[layer], in_bias[layer]).astype(
        jnp.bfloat16
    )
    projected = jnp.einsum(
        "cij,cpd->pdij", normed, w_proj[layer], preferred_element_type=jnp.float32
    )
    pair_mask = mask_rows[:, None] * mask_cols[None, :]
    first_arm = (jax.nn.sigmoid(projected[0]) * projected[1] * pair_mask).astype(jnp.bfloat16)
    second_arm = (jax.nn.sigmoid(projected[2]) * projected[3] * pair_mask).astype(jnp.bfloat16)
    logits = jnp.einsum("cij,cd->dij", normed, w_gate[layer], preferred_element_type=jnp.float32)
    logits = logits + pair_bias[layer][:, None, None] * same_chain[None]
    return (first_arm, second_arm, jax.nn.sigmoid(logits))


def finish(product_sum, gating, layer, out_gain, out_bias, w_out):
    totals = together(
        (jnp.sum(product_sum, axis=0), jnp.sum(product_sum * product_sum, axis=0)), "ch"
    )
    channels = product_sum.shape[0] * lax.axis_size("ch")
    mean_val = totals[0] / channels
    variance = totals[1] / channels - mean_val * mean_val
    scaled = (product_sum - mean_val) * lax.rsqrt(variance + epsilon)
    normed = (scaled * out_gain[layer][:, None, None] + out_bias[layer][:, None, None]).astype(
        jnp.bfloat16
    )
    columns = w_out[layer]
    mixed = sum_at_owner(
        jnp.einsum("dij,dc->cij", normed, columns, preferred_element_type=jnp.float32).astype(
            jnp.bfloat16
        ),
        "ch",
        0,
    )
    return gating * mixed


def to_owner(first_arm, second_arm):
    first_quarter, second_quarter = sent_together((first_arm, second_arm), "ch", 2, 0, 1)
    return sent_together((first_quarter, second_quarter), "row", 0, 1, 2)


def to_rows(owned):
    blocks = lax.all_to_all(owned, "row", split_axis=1, concat_axis=0, tiled=True)
    return lax.all_to_all(blocks, "ch", split_axis=0, concat_axis=2, tiled=True)


def body(
    pair_rep,
    residue_mask,
    chain_ids,
    in_gain,
    in_bias,
    w_proj,
    w_gate,
    pair_bias,
    out_gain,
    out_bias,
    w_out,
):
    rows_here = pair_rep.shape[1]
    row_start = lax.axis_index("row") * rows_here
    mask_cols = residue_mask.astype(jnp.float32)
    mask_rows = lax.dynamic_slice_in_dim(mask_cols, row_start, rows_here)
    chain_rows = lax.dynamic_slice_in_dim(chain_ids, row_start, rows_here)
    same_chain = (chain_rows[:, None] == chain_ids[None, :]).astype(jnp.float32)
    first_arm, second_arm, gating = prepare(
        pair_rep, 0, in_gain, in_bias, w_proj, w_gate, pair_bias, mask_rows, mask_cols, same_chain
    )
    first_own, second_own = to_owner(first_arm, second_arm)
    partial_sum = jnp.einsum(
        "dik,djk->dij", first_own, second_own, preferred_element_type=jnp.float32
    )
    owned_sum = sum_at_owner(partial_sum.astype(jnp.bfloat16), "ch", 2)
    product_sum = to_rows(owned_sum)
    middle = (
        pair_rep.astype(jnp.float32) + finish(product_sum, gating, 0, out_gain, out_bias, w_out)
    ).astype(jnp.bfloat16)
    in_first, in_second, in_gating = prepare(
        middle, 1, in_gain, in_bias, w_proj, w_gate, pair_bias, mask_rows, mask_cols, same_chain
    )
    left_own, right_own = to_owner(in_first, in_second)
    owned_product = jnp.einsum(
        "dki,dkj->dij",
        gathered_copies(left_own, "ch", 2),
        right_own,
        preferred_element_type=jnp.float32,
    )
    in_product = to_rows(owned_product)
    update = finish(in_product, in_gating, 1, out_gain, out_bias, w_out)
    return (middle.astype(jnp.float32) + update).astype(jnp.bfloat16)


def solution(mesh):
    return jax.shard_map(
        body,
        mesh=mesh,
        in_specs=(
            P("ch", "row", None),
            P(),
            P(),
            P(),
            P(),
            P(None, None, None, "ch"),
            P(None, None, "ch"),
            P(None, "ch"),
            P(None, "ch"),
            P(None, "ch"),
            P(None, "ch", None),
        ),
        out_specs=P("ch", "row", None),
        check_vma=False,
    )
```

profile of v0, /device:TPU:1, one launch (start us, length us, event | category | flops | bytes accessed | tf_op | source)
XLA Modules:
  0.0 200.2 jit_solution(12180103836867893405)
XLA Ops:
  0.0 1.3 broadcast_in_dim.17
  1.3 10.1 %all-to-all-start = ((bf16[4,32,1,128]{3,1,2,0:T(8,128)(2,1)}), bf16[4,32,1,128]{3,1,2,0:T(8,128)(2,1)S(1)}, u32[]{:S(2)}, u32[]{:S(2)}) async-start(bf16[4,32,1,128]{3,1,2,0:T(8,128)(2,1)} %broadcast_in_dim.17), calls=%async_computation | async-start | bytes 65536 | tf_op jit(solution)/shard_map/all_to_all | solution.py:17
  15.2 6.2 %all_to_all.162 = bf16[4,2,1024]{2,1,0:T(2,128)(2,1)S(1)} all-to-all(bf16[4,2,1024]{2,1,0:T(2,128)(2,1)S(1)} %reshape.1148), channel_id=1, replica_groups=mesh['row'=128,'ch'=4] {'ch'}, dimensions={0} | all-to-all | bytes 32768 | tf_op jit(solution)/shard_map/all_to_all | solution.py:50
  21.9 32.3 %all_to_all.163 = bf16[128,1,64]{2,1,0:T(2,128)(2,1)S(1)} all-to-all(bf16[128,1,64]{2,1,0:T(2,128)(2,1)S(1)} %copy.83), channel_id=1, replica_groups=mesh['row'=128,'ch'=4] {'row'}, dimensions={0} | all-to-all | bytes 32768 | tf_op jit(solution)/shard_map/all_to_all | solution.py:50
  54.5 7.7 %all_to_all.164 = bf16[4,1,128,32]{2,3,1,0:T(8,128)(2,1)S(1)} all-to-all(bf16[4,1,128,32]{2,3,1,0:T(8,128)(2,1)S(1)} %bitcast.246), channel_id=1, replica_groups=mesh['row'=128,'ch'=4] {'ch'}, dimensions={0} | all-to-all | bytes 65536 | tf_op jit(solution)/shard_map/all_to_all | solution.py:43
  62.3 21.3 %all_to_all.165 = f32[1,128,32]{2,0,1:T(1,128)S(1)} all-to-all(f32[1,128,32]{2,0,1:T(1,128)S(1)} %copy.86), channel_id=1, replica_groups=mesh['row'=128,'ch'=4] {'row'}, dimensions={1} | all-to-all | bytes 32768 | tf_op jit(solution)/shard_map/all_to_all | solution.py:108
  85.6 5.5 %all-to-all-start.5 = ((f32[4,1,1024]{2,1,0:T(1,128)}), f32[4,1,1024]{2,1,0:T(1,128)S(1)}, u32[]{:S(2)}, u32[]{:S(2)}) async-start(f32[4,1,1024]{2,1,0:T(1,128)} %reshape.1150), calls=%async_computation.5 | async-start | bytes 32768 | tf_op jit(solution)/shard_map/all_to_all | solution.py:109
  91.1 3.1 %all-to-all-done.5 = f32[4,1,1024]{2,1,0:T(1,128)S(1)} async-done(((f32[4,1,1024]{2,1,0:T(1,128)}), f32[4,1,1024]{2,1,0:T(1,128)S(1)}, u32[]{:S(2)}, u32[]{:S(2)}) %all-to-all-start.5) | async-done | bytes 16416 | tf_op jit(solution)/shard_map/all_to_all | solution.py:109
  96.2 4.1 %all-to-all-start.6 = ((f32[4,1,256]{2,1,0:T(1,128)}), f32[4,1,256]{2,1,0:T(1,128)S(1)}, u32[]{:S(2)}, u32[]{:S(2)}) async-start(f32[4,1,256]{2,1,0:T(1,128)} %broadcast_in_dim.18), calls=%async_computation.6 | async-start | bytes 8192 | tf_op jit(solution)/shard_map/all_to_all | solution.py:17
  101.8 1.6 all-to-all-done.6
  103.4 0.8 convolution_convert_fusion.1
  104.3 3.9 %all-to-all-start.7 = ((bf16[4,32,1,128]{3,1,2,0:T(8,128)(2,1)}), bf16[4,32,1,128]{3,1,2,0:T(8,128)(2,1)S(1)}, u32[]{:S(2)}, u32[]{:S(2)}) async-start(bf16[4,32,1,128]{3,1,2,0:T(8,128)(2,1)} %bitcast.36), calls=%async_computation.7 | async-start | bytes 65536 | tf_op jit(solution)/shard_map/all_to_all | solution.py:43
  108.9 2.5 %all-to-all-done.7 = bf16[4,32,1,128]{3,1,2,0:T(8,128)(2,1)S(1)} async-done(((bf16[4,32,1,128]{3,1,2,0:T(8,128)(2,1)}), bf16[4,32,1,128]{3,1,2,0:T(8,128)(2,1)S(1)}, u32[]{:S(2)}, u32[]{:S(2)}) %all-to-all-start.7) | async-done | bytes 32800 | tf_op jit(solution)/shard_map/all_to_all | solution.py:43
  111.7 6.3 %all_to_all.166 = bf16[4,32,1,128]{3,1,2,0:T(8,128)(2,1)S(1)} all-to-all(bf16[4,32,1,128]{3,1,2,0:T(8,128)(2,1)S(1)} %broadcast_in_dim.20), channel_id=1, replica_groups=mesh['row'=128,'ch'=4] {'ch'}, dimensions={0} | all-to-all | bytes 65536 | tf_op jit(solution)/shard_map/all_to_all | solution.py:17
  118.5 6.2 %all_to_all.167 = bf16[4,2,1024]{2,1,0:T(2,128)(2,1)S(1)} all-to-all(bf16[4,2,1024]{2,1,0:T(2,128)(2,1)S(1)} %reshape.1152), channel_id=1, replica_groups=mesh['row'=128,'ch'=4] {'ch'}, dimensions={0} | all-to-all | bytes 32768 | tf_op jit(solution)/shard_map/all_to_all | solution.py:50
  125.2 21.3 %all_to_all.168 = bf16[128,1,64]{2,1,0:T(2,128)(2,1)S(1)} all-to-all(bf16[128,1,64]{2,1,0:T(2,128)(2,1)S(1)} %copy.96), channel_id=1, replica_groups=mesh['row'=128,'ch'=4] {'row'}, dimensions={0} | all-to-all | bytes 32768 | tf_op jit(solution)/shard_map/all_to_all | solution.py:50
  146.6 7.6 %all_to_all.169 = bf16[4,1,128,32]{2,3,1,0:T(8,128)(2,1)S(1)} all-to-all(bf16[4,1,128,32]{2,3,1,0:T(8,128)(2,1)S(1)} %broadcast_in_dim.22), channel_id=1, replica_groups=mesh['row'=128,'ch'=4] {'ch'}, dimensions={0} | all-to-all | bytes 65536 | tf_op jit(solution)/shard_map/all_to_all | solution.py:17
  154.4 21.3 %all_to_all.170 = f32[1,128,32]{2,0,1:T(1,128)S(1)} all-to-all(f32[1,128,32]{2,0,1:T(1,128)S(1)} %bitcast.238), channel_id=1, replica_groups=mesh['row'=128,'ch'=4] {'row'}, dimensions={1} | all-to-all | bytes 32768 | tf_op jit(solution)/shard_map/all_to_all | solution.py:108
  175.6 0.8 reduce.23
  176.5 7.6 %all_to_all.171 = f32[4,1,1024]{2,1,0:T(1,128)S(1)} all-to-all(f32[4,1,1024]{2,1,0:T(1,128)S(1)} %reshape.1154), channel_id=1, replica_groups=mesh['row'=128,'ch'=4] {'ch'}, dimensions={0} | all-to-all | bytes 32768 | tf_op jit(solution)/shard_map/all_to_all | solution.py:109
  185.8 3.9 %all-to-all-start.14 = ((f32[4,1,256]{2,1,0:T(1,128)}), f32[4,1,256]{2,1,0:T(1,128)S(1)}, u32[]{:S(2)}, u32[]{:S(2)}) async-start(f32[4,1,256]{2,1,0:T(1,128)} %broadcast_in_dim.23), calls=%async_computation.14 | async-start | bytes 8192 | tf_op jit(solution)/shard_map/all_to_all | solution.py:17
  189.9 3.0 %all-to-all-done.14 = f32[4,1,256]{2,1,0:T(1,128)S(1)} async-done(((f32[4,1,256]{2,1,0:T(1,128)}), f32[4,1,256]{2,1,0:T(1,128)S(1)}, u32[]{:S(2)}, u32[]{:S(2)}) %all-to-all-start.14) | async-done | bytes 4128 | tf_op jit(solution)/shard_map/all_to_all | solution.py:17
  193.1 6.2 %all_to_all.172 = bf16[4,32,1,128]{3,1,2,0:T(8,128)(2,1)S(1)} all-to-all(bf16[4,32,1,128]{3,1,2,0:T(8,128)(2,1)S(1)} %bitcast.245), channel_id=1, replica_groups=mesh['row'=128,'ch'=4] {'ch'}, dimensions={0} | all-to-all | bytes 65536 | tf_op jit(solution)/shard_map/all_to_all | solution.py:43
  199.4 0.8 fusion.16
  (100 shorter events, 14.2 us)
Async XLA Ops:
  0.0 11.4 %copy-start = (bf16[2,128,4,32]{1,3,2,0:T(8,128)(2,1)S(1)}, bf16[2,128,4,32]{1,3,2,0:T(8,128)(2,1)}, u32[]{:S(2)}) copy-start(bf16[2,128,4,32]{1,3,2,0:T(8,128)(2,1)} %param.16) | copy-start | bytes 196612
  1.3 13.3 %all-to-all-start = ((bf16[4,32,1,128]{3,1,2,0:T(8,128)(2,1)}), bf16[4,32,1,128]{3,1,2,0:T(8,128)(2,1)S(1)}, u32[]{:S(2)}, u32[]{:S(2)}) async-start(bf16[4,32,1,128]{3,1,2,0:T(8,128)(2,1)} %broadcast_in_dim.17), calls=%async_computation | async-start | bytes 65536 | tf_op jit(solution)/shard_map/all_to_all | solution.py:17
  11.5 0.7 copy-start.4
  11.5 0.7 copy-start.9
  12.1 0.7 copy-start.3
  85.6 5.5 %copy-start.5 = (f32[2,32]{1,0:T(2,128)S(1)}, f32[2,32]{1,0:T(2,128)}, u32[]{:S(2)}) copy-start(f32[2,32]{1,0:T(2,128)} %param.20) | copy-start | bytes 772
  85.6 5.5 %copy-start.6 = (f32[2,32]{1,0:T(2,128)S(1)}, f32[2,32]{1,0:T(2,128)}, u32[]{:S(2)}) copy-start(f32[2,32]{1,0:T(2,128)} %param.19) | copy-start | bytes 772
  85.6 8.6 %all-to-all-start.5 = ((f32[4,1,1024]{2,1,0:T(1,128)}), f32[4,1,1024]{2,1,0:T(1,128)S(1)}, u32[]{:S(2)}, u32[]{:S(2)}) async-start(f32[4,1,1024]{2,1,0:T(1,128)} %reshape.1150), calls=%async_computation.5 | async-start | bytes 32768 | tf_op jit(solution)/shard_map/all_to_all | solution.py:109
  96.2 4.1 %copy-start.2 = (f32[2,32]{1,0:T(2,128)S(1)}, f32[2,32]{1,0:T(2,128)}, u32[]{:S(2)}) copy-start(f32[2,32]{1,0:T(2,128)} %param.18) | copy-start | bytes 772
  96.2 7.2 %all-to-all-start.6 = ((f32[4,1,256]{2,1,0:T(1,128)}), f32[4,1,256]{2,1,0:T(1,128)S(1)}, u32[]{:S(2)}, u32[]{:S(2)}) async-start(f32[4,1,256]{2,1,0:T(1,128)} %broadcast_in_dim.18), calls=%async_computation.6 | async-start | bytes 8192 | tf_op jit(solution)/shard_map/all_to_all | solution.py:17
  100.3 0.7 copy-start.10
  101.7 1.7 copy-start.7
  104.3 7.1 %all-to-all-start.7 = ((bf16[4,32,1,128]{3,1,2,0:T(8,128)(2,1)}), bf16[4,32,1,128]{3,1,2,0:T(8,128)(2,1)S(1)}, u32[]{:S(2)}, u32[]{:S(2)}) async-start(bf16[4,32,1,128]{3,1,2,0:T(8,128)(2,1)} %bitcast.36), calls=%async_computation.7 | async-start | bytes 65536 | tf_op jit(solution)/shard_map/all_to_all | solution.py:43
  108.9 2.5 %copy-start.1 = (bf16[32,1,128]{2,0,1:T(8,128)(2,1)S(1)}, bf16[32,1,128]{2,0,1:T(8,128)(2,1)}, u32[]{:S(2)}) copy-start(bf16[32,1,128]{2,0,1:T(8,128)(2,1)} %param.11) | copy-start | bytes 24580
  108.9 2.5 %copy-start.8 = (bf16[2,128,32]{1,2,0:T(8,128)(2,1)S(1)}, bf16[2,128,32]{1,2,0:T(8,128)(2,1)}, u32[]{:S(2)}) copy-start(bf16[2,128,32]{1,2,0:T(8,128)(2,1)} %param.17) | copy-start | bytes 49156
  185.8 7.0 %all-to-all-start.14 = ((f32[4,1,256]{2,1,0:T(1,128)}), f32[4,1,256]{2,1,0:T(1,128)S(1)}, u32[]{:S(2)}, u32[]{:S(2)}) async-start(f32[4,1,256]{2,1,0:T(1,128)} %broadcast_in_dim.23), calls=%async_computation.14 | async-start | bytes 8192 | tf_op jit(solution)/shard_map/all_to_all | solution.py:17
where the time goes:
time: 201 us; the launch traced here: 200 us
  blocking collectives  144 us (72%)
  starting transfers between devices  27.5 us (14%)
  waiting for transfers between devices  10.7 us (5%)
  local copies, waits for them, and re-layouts  9.85 us (5%)
  other arithmetic  4.72 us (2%)
  matrix products  2.92 us (1%)
    all_to_all x4, blocking collectives, sent_together(): lax.all_to_all(both, axis, split_axis=split_dim, concat_axis=concat_dim,...  66.1 us
    all_to_all x2, blocking collectives, to_rows(): lax.all_to_all(owned, 'row', split_axis=1, concat_axis=0, tiled=True)  42.5 us
    all_to_all x3, starting transfers between devices, from_everyone(): lax.all_to_all(jnp.broadcast_to(x[None], (devices, *x.shape)), axis, 0, 0...  18.1 us
    all_to_all x2, blocking collectives, from_everyone(): lax.all_to_all(jnp.broadcast_to(x[None], (devices, *x.shape)), axis, 0, 0...  13.9 us
    all_to_all x2, blocking collectives, sum_at_owner(): tiles = lax.all_to_all(in_blocks(x, dim, devices), axis, 0, 0, tiled=True)  13.9 us
    all_to_all x1, blocking collectives, to_rows(): return lax.all_to_all(blocks, 'ch', split_axis=0, concat_axis=2, tiled=True)  7.58 us
    all_to_all x1, starting transfers between devices, to_rows(): return lax.all_to_all(blocks, 'ch', split_axis=0, concat_axis=2, tiled=True)  5.46 us
    all_to_all x3, waiting for transfers between devices, from_everyone(): lax.all_to_all(jnp.broadcast_to(x[None], (devices, *x.shape)), axis, 0, 0...  5.1 us
  transfers between devices with their start and end apart: 5, of which 5 were waited for; matrix products, arithmetic and copies ran while one was open for 1% of the time, Pallas kernels for 0%

commit v1 on v0

v1 whole, which is shorter than its diff:
```python
import jax
import jax.numpy as jnp
from jax import lax
from jax.sharding import Mesh, PartitionSpec as P

epsilon = 1e-05
bf16 = jnp.bfloat16
f32 = jnp.float32
ROW = ("x", "z", "yh")
PLANE = ("x", "yh", "ch")


def norm(v, gain, bias):
    mean = jnp.mean(v, axis=0)
    var = jnp.mean(v * v, axis=0) - mean * mean
    return ((v - mean) * lax.rsqrt(var + epsilon) * gain[:, None] + bias[:, None]).astype(bf16)


def body(pair_rep, residue_mask, chain_ids, in_gain, in_bias, w_proj, w_gate, pair_bias, out_gain, out_bias, w_out):
    ix, iz, iyh, q = (lax.axis_index(a) for a in ("x", "z", "yh", "ch"))
    row = (ix * 16 + iz) * 2 + iyh
    me = ix * 8 + iyh * 4 + q
    mask = residue_mask.astype(f32)
    zfull = lax.all_gather(pair_rep[:, 0, :], "ch", axis=0, tiled=True)
    wp1 = lax.all_gather(w_proj[1], "ch", axis=2, tiled=True)
    wg = lax.all_gather(w_gate, "ch", axis=2, tiled=True)
    wo = lax.all_gather(w_out, "ch", axis=0)
    pbias = lax.all_gather(pair_bias, "ch", axis=1, tiled=True)
    og = lax.all_gather(out_gain, "ch", axis=0)
    ob = lax.all_gather(out_bias, "ch", axis=0)

    n0 = norm(zfull.astype(f32), in_gain[0], in_bias[0])
    p0 = jnp.einsum("ck,cpd->pdk", n0, w_proj[0], preferred_element_type=f32)
    pm = mask[row] * mask
    left = (jax.nn.sigmoid(p0[0]) * p0[1] * pm).astype(bf16).reshape(8, 4, 128)
    right = (jax.nn.sigmoid(p0[2]) * p0[3] * pm).astype(bf16).reshape(8, 4, 128)
    zt = lax.dynamic_index_in_dim(zfull.T.reshape(4, 8, 4, 128), q, 2, keepdims=False)
    zt = zt.transpose(1, 0, 2)
    send = jnp.stack([left, right, zt], axis=1).reshape(4, 1, 2, 3, 4, 128)
    send = jnp.broadcast_to(send, (4, 16, 2, 3, 4, 128)).reshape(128, 3, 4, 128)
    got = lax.all_to_all(send, ROW, 0, 0, tiled=True)

    x0 = jnp.einsum("jdk,idk->dji", got[:, 1], got[:, 0], preferred_element_type=f32).astype(bf16)
    x0 = x0.reshape(4, 4, 32, 128).transpose(2, 0, 1, 3).reshape(32, 4, 512)
    x0 = lax.all_to_all(x0, PLANE, 0, 0, tiled=True).reshape(128, 512).astype(f32)

    def reorder(w):
        return w.reshape(4, 8, 4, *w.shape[2:]).swapaxes(0, 1).reshape(128, *w.shape[2:])

    cols = jnp.arange(4) * 32 + me
    same = (chain_ids[cols][:, None] == chain_ids[None, :]).astype(f32).reshape(512)
    pm1 = (mask[cols][:, None] * mask[None, :]).reshape(512)
    xn = norm(x0, reorder(og[:, 0]), reorder(ob[:, 0]))
    y = jnp.einsum("dp,dc->cp", xn, reorder(wo[:, 0]), preferred_element_type=f32)
    zp = got[:, 2].transpose(2, 1, 0).reshape(128, 512).astype(f32)
    nz = norm(zp, in_gain[0], in_bias[0])
    gate = jax.nn.sigmoid(
        jnp.einsum("cp,cd->dp", nz, wg[0], preferred_element_type=f32) + pbias[0][:, None] * same
    )
    z1 = (zp + gate * y).astype(bf16)
    n1 = norm(z1.astype(f32), in_gain[1], in_bias[1])
    p1 = jnp.einsum("cp,cxd->xdp", n1, wp1, preferred_element_type=f32)
    left1 = (jax.nn.sigmoid(p1[0]) * p1[1] * pm1).astype(bf16)
    right1 = (jax.nn.sigmoid(p1[2]) * p1[3] * pm1).astype(bf16)
    gate1 = jax.nn.sigmoid(
        jnp.einsum("cp,cd->dp", n1, wg[1], preferred_element_type=f32) + pbias[1][:, None] * same
    ).astype(bf16)
    zg = jnp.stack([z1, gate1]).reshape(2, 4, 32, 4, 4, 16, 2)
    zg = lax.dynamic_index_in_dim(zg, iz, 5, keepdims=False)
    zg = zg.transpose(4, 5, 1, 0, 3, 2).reshape(32, 4, 64)
    send = jnp.concatenate(
        [left1.reshape(32, 4, 512), right1.reshape(32, 4, 512), zg, jnp.zeros((32, 4, 64), bf16)], axis=2
    )
    got = lax.all_to_all(send, PLANE, 0, 0, tiled=True)
    l1 = lax.dynamic_slice_in_dim(got[:, :, :512], iz * 2, 2, 0).reshape(2, 4, 4, 128)
    r1 = got[:, :, 512:1024].reshape(32, 4, 4, 128)
    x1 = jnp.einsum("ydxk,mdtk->xydtm", l1, r1, preferred_element_type=f32).astype(bf16)
    x1 = jnp.broadcast_to(x1.reshape(8, 1, 4, 128), (8, 4, 4, 128)).reshape(32, 4, 128)
    x1 = lax.all_to_all(x1, PLANE, 0, 0, tiled=True).reshape(128, 128).astype(f32)
    xn = norm(x1, og[:, 1].reshape(128), ob[:, 1].reshape(128))
    wo1 = lax.dynamic_slice_in_dim(wo[:, 1].reshape(128, 128), q * 32, 32, 1)
    y = jnp.einsum("dp,dc->cp", xn, wo1, preferred_element_type=f32)
    zg = got[:, :, 1024:1088].reshape(32, 2, 4, 32).transpose(1, 3, 2, 0).reshape(2, 32, 128).astype(f32)
    return (zg[0] + zg[1] * y).astype(bf16)[:, None, :]


def solution(mesh):
    fine = Mesh(mesh.devices.reshape(4, 16, 2, 4), ("x", "z", "yh", "ch"))
    return jax.shard_map(
        body,
        mesh=fine,
        in_specs=(
            P("ch", ROW, None),
            P(),
            P(),
            P(),
            P(),
            P(None, None, None, "ch"),
            P(None, None, "ch"),
            P(None, "ch"),
            P(None, "ch"),
            P(None, "ch"),
            P(None, "ch", None),
        ),
        out_specs=P("ch", ROW, None),
        check_vma=False,
    )
```

time: 201 us -> 115 us (0.57)
  blocking collectives: 144 us -> 43.4 us
  waiting for transfers between devices: 10.7 us -> 23.1 us
  starting transfers between devices: 27.5 us -> 31.2 us
  other arithmetic: 4.72 us -> 2.11 us
    all_to_all x11 -> x0, blocking collectives: 144 us -> none  [the longest x4 66.1 us: sent_together(): lax.all_to_all(both, axis, split_axis=split_dim, concat_axis=concat_dim,...]
    all_gather x0 -> x7, blocking collectives: none -> 43.4 us  [the longest x1 12 us: body(): zfull = lax.all_gather(pair_rep[:, 0, :], 'ch', axis=0, tiled=True)]
    all_to_all x5 -> x4, waiting for transfers between devices: 10.7 us -> 23.1 us  [the longest x1 9.26 us: body(): got = lax.all_to_all(send, PLANE, 0, 0, tiled=True)]
    all_to_all x5 -> x4, starting transfers between devices: 27.5 us -> 31.2 us  [the longest x1 16.8 us: body(): got = lax.all_to_all(send, ROW, 0, 0, tiled=True)]
    all_to_all x4 -> x0, other arithmetic: 2.94 us -> none  [the longest x2 1.59 us: to_rows(): lax.all_to_all(owned, 'row', split_axis=1, concat_axis=0, tiled=True)]
  transfers between devices with their start and end apart: 5 -> 4, of which waited for: 5 -> 3; matrix products, arithmetic and copies ran while one was open for 1% -> 3% of each run, Pallas kernels for 0% -> 0%
where the time goes in v1:
time: 115 us; the launch traced here: 114 us
  blocking collectives  43.4 us (38%)
  starting transfers between devices  31.2 us (27%)
  waiting for transfers between devices  23.1 us (20%)
  local copies, waits for them, and re-layouts  11.3 us (10%)
  matrix products  2.72 us (2%)
  other arithmetic  2.11 us (2%)
    all_to_all x1, starting transfers between devices, body(): got = lax.all_to_all(send, ROW, 0, 0, tiled=True)  16.8 us
    all_gather x1, blocking collectives, body(): zfull = lax.all_gather(pair_rep[:, 0, :], 'ch', axis=0, tiled=True)  12 us
    all_to_all x1, waiting for transfers between devices, body(): got = lax.all_to_all(send, PLANE, 0, 0, tiled=True)  9.26 us
    all_to_all x1, waiting for transfers between devices, body(): lax.all_to_all(x0, PLANE, 0, 0, tiled=True).reshape(128, 512).astype(f32)  7.1 us
    all_to_all x1, starting transfers between devices, body(): lax.all_to_all(x0, PLANE, 0, 0, tiled=True).reshape(128, 512).astype(f32)  6.93 us
    all_to_all x1, waiting for transfers between devices, body(): lax.all_to_all(x1, PLANE, 0, 0, tiled=True).reshape(128, 128).astype(f32)  6.79 us
    all_gather x1, blocking collectives, body(): wp1 = lax.all_gather(w_proj[1], 'ch', axis=2, tiled=True)  5.42 us
    all_gather x1, blocking collectives, body(): og = lax.all_gather(out_gain, 'ch', axis=0)  5.33 us
  transfers between devices with their start and end apart: 4, of which 3 were waited for; matrix products, arithmetic and copies ran while one was open for 3% of the time, Pallas kernels for 0%

profile of v1, /device:TPU:1, one launch (start us, length us, event | category | flops | bytes accessed | tf_op | source)
XLA Modules:
  0.0 114.4 jit_solution(8791381486831941029)
XLA Ops:
  0.0 0.7 copy-done.10
  1.2 0.6 broadcast_multiply_fusion.3
  1.9 12.0 %all-gather = bf16[128,1,128]{2,0,1:T(8,128)(2,1)S(1)} all-gather(bf16[32,1,128]{2,0,1:T(8,128)(2,1)S(1)} %copy-done.4), channel_id=2, replica_groups=mesh['x'=4,'z'=16,'yh'=2,'ch'=4] {'ch'}, dimensions={0}, use_global_device_ids=true | all-gather | bytes 40960 | tf_op jit(solution)/shard_map/all_gather | solution.py:24
  14.2 0.6 copy-done.8
  15.3 0.8 broadcast_in_dim.13
  16.1 16.8 %all-to-all-start = ((bf16[128,3,4,128]{3,2,1,0:T(4,128)(2,1)}), bf16[128,3,4,128]{3,2,1,0:T(4,128)(2,1)S(1)}, u32[]{:S(2)}, u32[]{:S(2)}) async-start(bf16[128,3,4,128]{3,2,1,0:T(4,128)(2,1)} %bitcast.16), calls=%async_computation | async-start | bytes 786432 | tf_op jit(solution)/shard_map/all_to_all | solution.py:41
  32.9 0.7 copy-done.5
  33.6 5.3 %all-gather.6 = f32[4,2,32]{2,1,0:T(2,128)S(1)} all-gather(f32[1,2,32]{2,1,0:T(2,128)S(1)} %bitcast.200), channel_id=3, replica_groups=mesh['x'=4,'z'=16,'yh'=2,'ch'=4] {'ch'}, dimensions={0}, use_global_device_ids=true | all-gather | bytes 1280 | tf_op jit(solution)/shard_map/all_gather | solution.py:29
  38.9 0.7 copy-done.6
  39.6 5.1 %all-gather.7 = f32[4,2,32]{2,1,0:T(2,128)S(1)} all-gather(f32[1,2,32]{2,1,0:T(2,128)S(1)} %bitcast.201), channel_id=4, replica_groups=mesh['x'=4,'z'=16,'yh'=2,'ch'=4] {'ch'}, dimensions={0}, use_global_device_ids=true | all-gather | bytes 1280 | tf_op jit(solution)/shard_map/all_gather | solution.py:30
  46.2 5.1 %all-gather.5 = f32[4,32,2]{1,2,0:T(2,128)S(1)} all-gather(f32[1,32,2]{1,2,0:T(2,128)S(1)} %bitcast.202), channel_id=1, replica_groups=mesh['x'=4,'z'=16,'yh'=2,'ch'=4] {'ch'}, dimensions={0}, use_global_device_ids=true | all-gather | bytes 1280 | tf_op jit(solution)/shard_map/all_gather | solution.py:28
  51.4 5.3 %all-gather.3 = bf16[8,32,128]{2,1,0:T(8,128)(2,1)S(1)} all-gather(bf16[2,32,128]{2,1,0:T(8,128)(2,1)S(1)} %copy-done.2), channel_id=5, replica_groups=mesh['x'=4,'z'=16,'yh'=2,'ch'=4] {'ch'}, dimensions={0}, use_global_device_ids=true | all-gather | bytes 81920 | tf_op jit(solution)/shard_map/all_gather | solution.py:27
  56.7 0.7 copy-done.3
  57.4 5.2 %all_gather.31 = bf16[2,128,128]{1,2,0:T(8,128)(2,1)S(1)} all-gather(bf16[2,128,32]{1,2,0:T(8,128)(2,1)S(1)} %copy-done.3), channel_id=1, replica_groups=mesh['x'=4,'z'=16,'yh'=2,'ch'=4] {'ch'}, dimensions={2}, use_global_device_ids=true | all-gather | bytes 81920 | tf_op jit(solution)/shard_map/all_gather | solution.py:26
  62.6 5.4 %all-gather.4 = bf16[1,128,4,128]{1,3,2,0:T(8,128)(2,1)S(1)} all-gather(bf16[1,128,4,32]{1,3,2,0:T(8,128)(2,1)S(1)} %get-tuple-element.33), channel_id=6, replica_groups=mesh['x'=4,'z'=16,'yh'=2,'ch'=4] {'ch'}, dimensions={3}, use_global_device_ids=true | all-gather | bytes 163840 | tf_op jit(solution)/shard_map/all_gather | solution.py:25
  68.9 0.7 copy.181
  69.7 6.9 %all-to-all-start.1 = ((bf16[32,4,512]{2,1,0:T(4,128)(2,1)}), bf16[32,4,512]{2,1,0:T(4,128)(2,1)S(1)}, u32[]{:S(2)}, u32[]{:S(2)}) async-start(bf16[32,4,512]{2,1,0:T(4,128)(2,1)} %copy.181), calls=%async_computation.1 | async-start | bytes 262144 | tf_op jit(solution)/shard_map/all_to_all | solution.py:45
  77.2 7.1 %all-to-all-done.1 = bf16[32,4,512]{2,1,0:T(4,128)(2,1)S(1)} async-done(((bf16[32,4,512]{2,1,0:T(4,128)(2,1)}), bf16[32,4,512]{2,1,0:T(4,128)(2,1)S(1)}, u32[]{:S(2)}, u32[]{:S(2)}) %all-to-all-start.1) | async-done | bytes 131104 | tf_op jit(solution)/shard_map/all_to_all | solution.py:45
  87.0 1.0 concatenate.5
  88.0 3.9 %all-to-all-start.2 = ((bf16[32,4,1152]{2,1,0:T(4,128)(2,1)}), bf16[32,4,1152]{2,1,0:T(4,128)(2,1)S(1)}, u32[]{:S(2)}, u32[]{:S(2)}) async-start(bf16[32,4,1152]{2,1,0:T(4,128)(2,1)} %concatenate.5), calls=%async_computation.2 | async-start | bytes 589824 | tf_op jit(solution)/shard_map/all_to_all | solution.py:74
  92.0 9.3 %all-to-all-done.2 = bf16[32,4,1152]{2,1,0:T(4,128)(2,1)S(1)} async-done(((bf16[32,4,1152]{2,1,0:T(4,128)(2,1)}), bf16[32,4,1152]{2,1,0:T(4,128)(2,1)S(1)}, u32[]{:S(2)}, u32[]{:S(2)}) %all-to-all-start.2) | async-done | bytes 294944 | tf_op jit(solution)/shard_map/all_to_all | solution.py:74
  102.5 3.6 %all-to-all-start.3 = ((bf16[32,4,128]{2,1,0:T(4,128)(2,1)}), bf16[32,4,128]{2,1,0:T(4,128)(2,1)S(1)}, u32[]{:S(2)}, u32[]{:S(2)}) async-start(bf16[32,4,128]{2,1,0:T(4,128)(2,1)} %bitcast.64), calls=%async_computation.3 | async-start | bytes 65536 | tf_op jit(solution)/shard_map/all_to_all | solution.py:79
  106.7 6.8 %all-to-all-done.3 = bf16[32,4,128]{2,1,0:T(4,128)(2,1)S(1)} async-done(((bf16[32,4,128]{2,1,0:T(4,128)(2,1)}), bf16[32,4,128]{2,1,0:T(4,128)(2,1)S(1)}, u32[]{:S(2)}, u32[]{:S(2)}) %all-to-all-start.3) | async-done | bytes 32800 | tf_op jit(solution)/shard_map/all_to_all | solution.py:79
  113.6 0.9 fusion.17
  (98 shorter events, 8.8 us)
Async XLA Ops:
  0.0 0.7 copy-start.10
  0.0 1.9 %copy-start.4 = (bf16[32,1,128]{2,0,1:T(8,128)(2,1)S(1)}, bf16[32,1,128]{2,0,1:T(8,128)(2,1)}, u32[]{:S(2)}) copy-start(bf16[32,1,128]{2,0,1:T(8,128)(2,1)} %param.11) | copy-start | bytes 24580
  1.9 12.3 %copy-start.1 = (bf16[2,128,4,32]{1,3,2,0:T(8,128)(2,1)S(1)}, bf16[2,128,4,32]{1,3,2,0:T(8,128)(2,1)}, u32[]{:S(2)}) copy-start(bf16[2,128,4,32]{1,3,2,0:T(8,128)(2,1)} %param.16) | copy-start | bytes 196612
  14.2 0.7 copy-start.8
  14.2 0.7 copy-start.9
  16.1 52.0 %all-to-all-start = ((bf16[128,3,4,128]{3,2,1,0:T(4,128)(2,1)}), bf16[128,3,4,128]{3,2,1,0:T(4,128)(2,1)S(1)}, u32[]{:S(2)}, u32[]{:S(2)}) async-start(bf16[128,3,4,128]{3,2,1,0:T(4,128)(2,1)} %bitcast.16), calls=%async_computation | async-start | bytes 786432 | tf_op jit(solution)/shard_map/all_to_all | solution.py:41
  32.9 0.7 copy-start.5
  38.9 0.7 copy-start.6
  44.9 0.7 copy-start
  45.5 0.7 copy-start.7
  46.2 5.2 %copy-start.2 = (bf16[2,32,128]{2,1,0:T(8,128)(2,1)S(1)}, bf16[2,32,128]{2,1,0:T(8,128)(2,1)}, u32[]{:S(2)}) copy-start(bf16[2,32,128]{2,1,0:T(8,128)(2,1)} %param.21) | copy-start | bytes 49156
  56.7 0.7 copy-start.3
  69.7 14.6 %all-to-all-start.1 = ((bf16[32,4,512]{2,1,0:T(4,128)(2,1)}), bf16[32,4,512]{2,1,0:T(4,128)(2,1)S(1)}, u32[]{:S(2)}, u32[]{:S(2)}) async-start(bf16[32,4,512]{2,1,0:T(4,128)(2,1)} %copy.181), calls=%async_computation.1 | async-start | bytes 262144 | tf_op jit(solution)/shard_map/all_to_all | solution.py:45
  88.0 13.3 %all-to-all-start.2 = ((bf16[32,4,1152]{2,1,0:T(4,128)(2,1)}), bf16[32,4,1152]{2,1,0:T(4,128)(2,1)S(1)}, u32[]{:S(2)}, u32[]{:S(2)}) async-start(bf16[32,4,1152]{2,1,0:T(4,128)(2,1)} %concatenate.5), calls=%async_computation.2 | async-start | bytes 589824 | tf_op jit(solution)/shard_map/all_to_all | solution.py:74
  102.5 11.0 %all-to-all-start.3 = ((bf16[32,4,128]{2,1,0:T(4,128)(2,1)}), bf16[32,4,128]{2,1,0:T(4,128)(2,1)S(1)}, u32[]{:S(2)}, u32[]{:S(2)}) async-start(bf16[32,4,128]{2,1,0:T(4,128)(2,1)} %bitcast.64), calls=%async_computation.3 | async-start | bytes 65536 | tf_op jit(solution)/shard_map/all_to_all | solution.py:79

commit v2 on v1

--- a/solution.py
+++ b/solution.py
@@ -20,15 +20,11 @@
     ix, iz, iyh, q = (lax.axis_index(a) for a in ("x", "z", "yh", "ch"))
     row = (ix * 16 + iz) * 2 + iyh
     me = ix * 8 + iyh * 4 + q
+    zfull = lax.all_gather(pair_rep[:, 0, :], "ch", axis=0, tiled=True)
+    zfull, residue_mask, chain_ids, in_gain, in_bias = lax.optimization_barrier(
+        (zfull, residue_mask, chain_ids, in_gain, in_bias)
+    )
     mask = residue_mask.astype(f32)
-    zfull = lax.all_gather(pair_rep[:, 0, :], "ch", axis=0, tiled=True)
-    wp1 = lax.all_gather(w_proj[1], "ch", axis=2, tiled=True)
-    wg = lax.all_gather(w_gate, "ch", axis=2, tiled=True)
-    wo = lax.all_gather(w_out, "ch", axis=0)
-    pbias = lax.all_gather(pair_bias, "ch", axis=1, tiled=True)
-    og = lax.all_gather(out_gain, "ch", axis=0)
-    ob = lax.all_gather(out_bias, "ch", axis=0)
-
     n0 = norm(zfull.astype(f32), in_gain[0], in_bias[0])
     p0 = jnp.einsum("ck,cpd->pdk", n0, w_proj[0], preferred_element_type=f32)
     pm = mask[row] * mask
@@ -39,6 +35,16 @@
     send = jnp.stack([left, right, zt], axis=1).reshape(4, 1, 2, 3, 4, 128)
     send = jnp.broadcast_to(send, (4, 16, 2, 3, 4, 128)).reshape(128, 3, 4, 128)
     got = lax.all_to_all(send, ROW, 0, 0, tiled=True)
+
+    w_gate2 = w_gate.transpose(1, 0, 2).reshape(2, 64, 64).transpose(1, 0, 2).reshape(64, 128)
+    packed = jnp.concatenate([w_proj[1].reshape(128, 128), w_gate2, w_out.reshape(64, 128)], axis=0)
+    packed = lax.all_gather(packed, "ch", axis=0)
+    small = lax.all_gather(jnp.concatenate([pair_bias, out_gain, out_bias], axis=0), "ch", axis=0)
+    wp1 = packed[:, :128].reshape(4, 128, 4, 32).transpose(1, 2, 0, 3).reshape(128, 4, 128)
+    wg = packed[:, 128:192].reshape(4, 64, 2, 2, 32).transpose(3, 2, 1, 0, 4).reshape(2, 128, 128)
+    wo = packed[:, 192:].reshape(4, 2, 32, 128)
+    pbias = small[:, 0:2].transpose(1, 0, 2).reshape(2, 128)
+    og, ob = small[:, 2:4], small[:, 4:6]
 
     x0 = jnp.einsum("jdk,idk->dji", got[:, 1], got[:, 0], preferred_element_type=f32).astype(bf16)
     x0 = x0.reshape(4, 4, 32, 128).transpose(2, 0, 1, 3).reshape(32, 4, 512)

time: 115 us -> 109 us (0.948)
  blocking collectives: 43.4 us -> 23.7 us
  waiting for transfers between devices: 23.1 us -> 33.9 us
  local copies, waits for them, and re-layouts: 11.3 us -> 12.5 us
    all_gather x6 -> x2, blocking collectives: 31.4 us -> 11.9 us  [the longest x1 6.42 us: body(): packed = lax.all_gather(packed, 'ch', axis=0)]
    all_to_all x1, waiting for transfers between devices: 0.01 us -> 10.7 us  [body(): got = lax.all_to_all(send, ROW, 0, 0, tiled=True)]
    unnamed x24 -> x23, local copies, waits for them, and re-layouts: 3.52 us -> 3.48 us
  transfers between devices with their start and end apart: 4 -> 4, of which waited for: 3 -> 4; matrix products, arithmetic and copies ran while one was open for 3% -> 4% of each run, Pallas kernels for 0% -> 0%
where the time goes in v2:
time: 109 us; the launch traced here: 108 us
  waiting for transfers between devices  33.9 us (31%)
  starting transfers between devices  32.3 us (30%)
  blocking collectives  23.7 us (22%)
  local copies, waits for them, and re-layouts  12.5 us (11%)
  matrix products  2.7 us (2%)
  other arithmetic  2.21 us (2%)
    all_to_all x1, starting transfers between devices, body(): got = lax.all_to_all(send, ROW, 0, 0, tiled=True)  16.9 us
    all_gather x1, blocking collectives, body(): zfull = lax.all_gather(pair_rep[:, 0, :], 'ch', axis=0, tiled=True)  11.9 us
    all_to_all x1, waiting for transfers between devices, body(): got = lax.all_to_all(send, ROW, 0, 0, tiled=True)  10.7 us
    all_to_all x1, waiting for transfers between devices, body(): got = lax.all_to_all(send, PLANE, 0, 0, tiled=True)  9.26 us
    all_to_all x1, starting transfers between devices, body(): lax.all_to_all(x0, PLANE, 0, 0, tiled=True).reshape(128, 512).astype(f32)  7.85 us
    all_to_all x1, waiting for transfers between devices, body(): lax.all_to_all(x0, PLANE, 0, 0, tiled=True).reshape(128, 512).astype(f32)  7.1 us
    all_to_all x1, waiting for transfers between devices, body(): lax.all_to_all(x1, PLANE, 0, 0, tiled=True).reshape(128, 128).astype(f32)  6.79 us
    all_gather x1, blocking collectives, body(): packed = lax.all_gather(packed, 'ch', axis=0)  6.42 us
  transfers between devices with their start and end apart: 4, of which 4 were waited for; matrix products, arithmetic and copies ran while one was open for 4% of the time, Pallas kernels for 0%

profile of v2, /device:TPU:1, one launch (start us, length us, event | category | flops | bytes accessed | tf_op | source)
XLA Modules:
  0.0 107.9 jit_solution(16931430102296169060)
XLA Ops:
  0.0 0.7 copy-done.4
  0.7 11.9 %all-gather.1 = bf16[128,1,128]{2,0,1:T(8,128)(2,1)S(1)} all-gather(bf16[32,1,128]{2,0,1:T(8,128)(2,1)S(1)} %copy-done.4), channel_id=3, replica_groups=mesh['x'=4,'z'=16,'yh'=2,'ch'=4] {'ch'}, dimensions={0}, use_global_device_ids=true | all-gather | bytes 40960 | tf_op jit(solution)/shard_map/all_gather | solution.py:23
  12.7 0.7 copy-done.10
  13.9 0.6 broadcast_multiply_fusion.3
  14.8 0.6 copy-done.8
  15.8 0.8 broadcast_in_dim.13
  16.7 16.9 %all-to-all-start = ((bf16[128,3,4,128]{3,2,1,0:T(4,128)(2,1)}), bf16[128,3,4,128]{3,2,1,0:T(4,128)(2,1)S(1)}, u32[]{:S(2)}, u32[]{:S(2)}) async-start(bf16[128,3,4,128]{3,2,1,0:T(4,128)(2,1)} %bitcast.25), calls=%async_computation | async-start | bytes 786432 | tf_op jit(solution)/shard_map/all_to_all | solution.py:37
  33.6 0.7 copy-done.5
  34.3 5.4 %all-gather.3 = f32[4,6,32]{2,1,0:T(8,128)S(1)} all-gather(f32[1,6,32]{2,1,0:T(8,128)S(1)} %maximum_bitcast_fusion.1), channel_id=4, replica_groups=mesh['x'=4,'z'=16,'yh'=2,'ch'=4] {'ch'}, dimensions={0}, use_global_device_ids=true | all-gather | bytes 3840 | tf_op jit(solution)/shard_map/all_gather | solution.py:42
  40.0 0.6 gather_fusion.1
  40.6 0.6 gather_fusion
  41.4 0.7 copy-done.3
  42.3 6.4 %all-gather = bf16[1024,128]{0,1:T(8,128)(2,1)S(1)} all-gather(bf16[256,128]{0,1:T(8,128)(2,1)S(1)} %pad_maximum_fusion), channel_id=2, replica_groups=mesh['x'=4,'z'=16,'yh'=2,'ch'=4] {'ch'}, dimensions={0}, use_global_device_ids=true | all-gather | bytes 327680 | tf_op jit(solution)/shard_map/all_gather | solution.py:41
  50.0 10.7 %all-to-all-done = bf16[128,3,4,128]{3,2,1,0:T(4,128)(2,1)S(1)} async-done(((bf16[128,3,4,128]{3,2,1,0:T(4,128)(2,1)}), bf16[128,3,4,128]{3,2,1,0:T(4,128)(2,1)S(1)}, u32[]{:S(2)}, u32[]{:S(2)}) %all-to-all-start) | async-done | bytes 393248 | tf_op jit(solution)/shard_map/all_to_all | solution.py:37
  61.4 0.7 copy.257
  62.2 7.9 %all-to-all-start.1 = ((bf16[32,4,512]{2,1,0:T(4,128)(2,1)}), bf16[32,4,512]{2,1,0:T(4,128)(2,1)S(1)}, u32[]{:S(2)}, u32[]{:S(2)}) async-start(bf16[32,4,512]{2,1,0:T(4,128)(2,1)} %copy.257), calls=%async_computation.1 | async-start | bytes 262144 | tf_op jit(solution)/shard_map/all_to_all | solution.py:51
  70.6 7.1 %all-to-all-done.1 = bf16[32,4,512]{2,1,0:T(4,128)(2,1)S(1)} async-done(((bf16[32,4,512]{2,1,0:T(4,128)(2,1)}), bf16[32,4,512]{2,1,0:T(4,128)(2,1)S(1)}, u32[]{:S(2)}, u32[]{:S(2)}) %all-to-all-start.1) | async-done | bytes 131104 | tf_op jit(solution)/shard_map/all_to_all | solution.py:51
  80.4 1.0 concatenate.13
  81.4 3.9 %all-to-all-start.2 = ((bf16[32,4,1152]{2,1,0:T(4,128)(2,1)}), bf16[32,4,1152]{2,1,0:T(4,128)(2,1)S(1)}, u32[]{:S(2)}, u32[]{:S(2)}) async-start(bf16[32,4,1152]{2,1,0:T(4,128)(2,1)} %concatenate.13), calls=%async_computation.2 | async-start | bytes 589824 | tf_op jit(solution)/shard_map/all_to_all | solution.py:80
  85.5 9.3 %all-to-all-done.2 = bf16[32,4,1152]{2,1,0:T(4,128)(2,1)S(1)} async-done(((bf16[32,4,1152]{2,1,0:T(4,128)(2,1)}), bf16[32,4,1152]{2,1,0:T(4,128)(2,1)S(1)}, u32[]{:S(2)}, u32[]{:S(2)}) %all-to-all-start.2) | async-done | bytes 294944 | tf_op jit(solution)/shard_map/all_to_all | solution.py:80
  95.3 0.6 broadcast_in_dim.16
  95.9 3.6 %all-to-all-start.3 = ((bf16[32,4,128]{2,1,0:T(4,128)(2,1)}), bf16[32,4,128]{2,1,0:T(4,128)(2,1)S(1)}, u32[]{:S(2)}, u32[]{:S(2)}) async-start(bf16[32,4,128]{2,1,0:T(4,128)(2,1)} %bitcast.62), calls=%async_computation.3 | async-start | bytes 65536 | tf_op jit(solution)/shard_map/all_to_all | solution.py:85
  100.1 6.8 %all-to-all-done.3 = bf16[32,4,128]{2,1,0:T(4,128)(2,1)S(1)} async-done(((bf16[32,4,128]{2,1,0:T(4,128)(2,1)}), bf16[32,4,128]{2,1,0:T(4,128)(2,1)S(1)}, u32[]{:S(2)}, u32[]{:S(2)}) %all-to-all-start.3) | async-done | bytes 32800 | tf_op jit(solution)/shard_map/all_to_all | solution.py:85
  107.0 0.9 fusion.14
  (111 shorter events, 8.1 us)
Async XLA Ops:
  0.0 0.7 copy-start.4
  12.6 2.1 %copy-start.1 = (bf16[2,128,4,32]{1,3,2,0:T(8,128)(2,1)S(1)}, bf16[2,128,4,32]{1,3,2,0:T(8,128)(2,1)}, u32[]{:S(2)}) copy-start(bf16[2,128,4,32]{1,3,2,0:T(8,128)(2,1)} %param.16) | copy-start | bytes 196612
  12.7 0.7 copy-start.10
  14.7 0.7 copy-start.8
  14.7 0.7 copy-start.9
  16.7 16.9 %copy-start.6 = (f32[2,32]{1,0:T(2,128)S(1)}, f32[2,32]{1,0:T(2,128)}, u32[]{:S(2)}) copy-start(f32[2,32]{1,0:T(2,128)} %param.19) | copy-start | bytes 772
  16.7 16.9 %copy-start.7 = (f32[2,32]{1,0:T(2,128)S(1)}, f32[2,32]{1,0:T(2,128)}, u32[]{:S(2)}) copy-start(f32[2,32]{1,0:T(2,128)} %param.18) | copy-start | bytes 772
  16.7 44.0 %all-to-all-start = ((bf16[128,3,4,128]{3,2,1,0:T(4,128)(2,1)}), bf16[128,3,4,128]{3,2,1,0:T(4,128)(2,1)S(1)}, u32[]{:S(2)}, u32[]{:S(2)}) async-start(bf16[128,3,4,128]{3,2,1,0:T(4,128)(2,1)} %bitcast.25), calls=%async_computation | async-start | bytes 786432 | tf_op jit(solution)/shard_map/all_to_all | solution.py:37
  33.6 0.7 copy-start.5
  39.9 0.7 copy-start
  40.6 0.7 copy-start.2
  41.4 0.7 copy-start.3
  62.2 15.6 %all-to-all-start.1 = ((bf16[32,4,512]{2,1,0:T(4,128)(2,1)}), bf16[32,4,512]{2,1,0:T(4,128)(2,1)S(1)}, u32[]{:S(2)}, u32[]{:S(2)}) async-start(bf16[32,4,512]{2,1,0:T(4,128)(2,1)} %copy.257), calls=%async_computation.1 | async-start | bytes 262144 | tf_op jit(solution)/shard_map/all_to_all | solution.py:51
  81.4 13.4 %all-to-all-start.2 = ((bf16[32,4,1152]{2,1,0:T(4,128)(2,1)}), bf16[32,4,1152]{2,1,0:T(4,128)(2,1)S(1)}, u32[]{:S(2)}, u32[]{:S(2)}) async-start(bf16[32,4,1152]{2,1,0:T(4,128)(2,1)} %concatenate.13), calls=%async_computation.2 | async-start | bytes 589824 | tf_op jit(solution)/shard_map/all_to_all | solution.py:80
  95.9 11.0 %all-to-all-start.3 = ((bf16[32,4,128]{2,1,0:T(4,128)(2,1)}), bf16[32,4,128]{2,1,0:T(4,128)(2,1)S(1)}, u32[]{:S(2)}, u32[]{:S(2)}) async-start(bf16[32,4,128]{2,1,0:T(4,128)(2,1)} %bitcast.62), calls=%async_computation.3 | async-start | bytes 65536 | tf_op jit(solution)/shard_map/all_to_all | solution.py:85

commit v3 on v1

v3 whole, which is shorter than its diff:
```python
import jax
import jax.numpy as jnp
from jax import lax
from jax.sharding import Mesh, PartitionSpec as P

epsilon = 1e-05
bf16 = jnp.bfloat16
f32 = jnp.float32
ROW = ("x", "z", "yh")
PLANE = ("x", "yh", "ch")


def norm(v, gain, bias):
    mean = jnp.mean(v, axis=0)
    var = jnp.mean(v * v, axis=0) - mean * mean
    return ((v - mean) * lax.rsqrt(var + epsilon) * gain[:, None] + bias[:, None]).astype(bf16)


def three(v):
    hi = lax.reduce_precision(v, 8, 7)
    mid = lax.reduce_precision(v - hi, 8, 7)
    return jnp.stack([hi, mid, v - hi - mid]).astype(bf16)


def by_plane(v):
    return v.reshape(4, 16, 2).swapaxes(1, 2).reshape(128)


def body(pair_rep, residue_mask, chain_ids, in_gain, in_bias, w_proj, w_gate, pair_bias, out_gain, out_bias, w_out):
    ix, iz, iyh, q = (lax.axis_index(a) for a in ("x", "z", "yh", "ch"))
    send = pair_rep.reshape(4, 8, 4, 16, 2).transpose(2, 1, 0, 4, 3).reshape(1, 4, 8, 128)
    send = jnp.broadcast_to(send, (16, 4, 8, 128)).reshape(64, 8, 128)
    got = lax.all_to_all(send, ("z", "ch"), 0, 0, tiled=True)

    packed = jnp.concatenate(
        [
            w_proj.reshape(256, 128),
            w_gate.transpose(1, 0, 2).reshape(64, 128),
            w_out.reshape(64, 128),
            jnp.pad(three(jnp.stack([pair_bias, out_gain, out_bias])).reshape(576), (0, 448)).reshape(8, 128),
        ],
        axis=0,
    )
    packed = lax.all_gather(packed, "ch", axis=0)
    wp = packed[:, :256].reshape(4, 2, 128, 4, 32).transpose(1, 2, 3, 0, 4).reshape(2, 128, 4, 128)
    wg = packed[:, 256:320].reshape(4, 128, 2, 32).transpose(2, 1, 0, 3).reshape(2, 128, 128)
    wo = packed[:, 320:384].reshape(4, 2, 32, 128).swapaxes(0, 1).reshape(2, 128, 128)
    small = packed[:, 384:].reshape(4, 1024)[:, :576].reshape(4, 3, 3, 2, 32).astype(f32)
    small = (small[:, 0] + small[:, 1] + small[:, 2]).transpose(1, 2, 0, 3).reshape(3, 2, 128)
    pbias, og, ob = small[0], small[1], small[2]

    mask = by_plane(residue_mask.astype(f32)).reshape(8, 16)
    chain = by_plane(chain_ids).reshape(8, 16)
    mine = ix * 2 + iyh
    mask_r = lax.dynamic_index_in_dim(mask, mine, 0, keepdims=False)
    chain_r = lax.dynamic_index_in_dim(chain, mine, 0, keepdims=False)
    mask_c = lax.dynamic_index_in_dim(mask.reshape(4, 32), q, 0, keepdims=False)
    chain_c = lax.dynamic_index_in_dim(chain.reshape(4, 32), q, 0, keepdims=False)
    pm = (mask_r[:, None] * mask_c[None, :]).reshape(512)
    same = (chain_r[:, None] == chain_c[None, :]).astype(f32).reshape(512)

    z0 = got.reshape(16, 4, 8, 4, 32).transpose(1, 3, 2, 0, 4).reshape(128, 512).astype(f32)
    n0 = norm(z0, in_gain[0], in_bias[0])
    p0 = jnp.einsum("cp,cxd->xdp", n0, wp[0], preferred_element_type=f32)
    left = (jax.nn.sigmoid(p0[0]) * p0[1] * pm).astype(bf16)
    right = (jax.nn.sigmoid(p0[2]) * p0[3] * pm).astype(bf16)
    send = jnp.stack([left, right]).reshape(2, 4, 32, 16, 32).transpose(2, 0, 3, 1, 4).reshape(32, 32, 128)
    got = lax.all_to_all(send, PLANE, 0, 0, tiled=True).reshape(8, 4, 2, 16, 4, 32)
    x0 = jnp.einsum("aqzdk,bqydk->dazby", got[:, :, 0], got[:, :, 1], preferred_element_type=f32).astype(bf16)
    x0 = x0.reshape(4, 8, 16, 4, 32).transpose(1, 3, 2, 0, 4).reshape(32, 16, 128)
    x0 = lax.all_to_all(x0, PLANE, 0, 0, tiled=True)
    gate = jax.nn.sigmoid(
        jnp.einsum("cp,cd->dp", n0, wg[0], preferred_element_type=f32) + pbias[0][:, None] * same
    )
    x0 = x0.reshape(32, 16, 4, 32).transpose(2, 0, 1, 3).reshape(128, 512).astype(f32)
    xn = norm(x0, og[0], ob[0])
    y = jnp.einsum("dp,dc->cp", xn, wo[0], preferred_element_type=f32)
    z1 = (z0 + gate * y).astype(bf16)
    n1 = norm(z1.astype(f32), in_gain[1], in_bias[1])
    p1 = jnp.einsum("cp,cxd->xdp", n1, wp[1], preferred_element_type=f32)
    left = (jax.nn.sigmoid(p1[0]) * p1[1] * pm).astype(bf16)
    right = (jax.nn.sigmoid(p1[2]) * p1[3] * pm).astype(bf16)
    left = lax.dynamic_index_in_dim(left.reshape(4, 32, 16, 2, 16), iz, 4, keepdims=False)
    left = jnp.pad(left.transpose(1, 2, 0, 3).reshape(32, 16, 8), ((0, 0), (0, 0), (0, 120)))
    right = right.reshape(4, 32, 16, 32).transpose(1, 2, 0, 3).reshape(32, 16, 128)
    got = lax.all_to_all(jnp.concatenate([right, left], axis=1), PLANE, 0, 0, tiled=True)

    z1_row = lax.dynamic_slice_in_dim(z1, iz * 32, 32, 1)
    n1_row = lax.dynamic_slice_in_dim(n1, iz * 32, 32, 1)
    same_row = lax.dynamic_slice_in_dim(same, iz * 32, 32, 0)
    gate1 = jax.nn.sigmoid(
        jnp.einsum("cp,cd->dp", n1_row, wg[1], preferred_element_type=f32) + pbias[1][:, None] * same_row
    ).astype(bf16)
    zg = jnp.stack([z1_row, gate1]).reshape(2, 4, 4, 8, 32).transpose(1, 0, 3, 2, 4).reshape(4, 16, 128)
    zg = lax.all_to_all(zg, "ch", 0, 0, tiled=True)
    zg = zg.reshape(4, 2, 8, 4, 32).transpose(1, 3, 2, 0, 4).reshape(2, 32, 128).astype(f32)

    r1 = got[:, :16].reshape(8, 4, 16, 4, 32)
    l1 = got[:, 16:, :8].reshape(8, 4, 16, 4, 2)
    x1 = jnp.einsum("aqzdy,apzdk->qydpk", l1, r1, preferred_element_type=f32).astype(bf16)
    x1 = jnp.broadcast_to(x1.reshape(8, 1, 4, 128), (8, 4, 4, 128)).reshape(32, 4, 128)
    x1 = lax.all_to_all(x1, PLANE, 0, 0, tiled=True)
    x1 = x1.swapaxes(0, 1).reshape(128, 128).astype(f32)
    xn = norm(x1, og[1], ob[1])
    wo1 = lax.dynamic_slice_in_dim(wo[1], q * 32, 32, 1)
    y = jnp.einsum("dp,dc->cp", xn, wo1, preferred_element_type=f32)
    out = (zg[0] + zg[1] * y).astype(bf16)
    return out.reshape(32, 4, 2, 16).swapaxes(2, 3).reshape(32, 1, 128)


def solution(mesh):
    fine = Mesh(mesh.devices.reshape(4, 16, 2, 4), ("x", "z", "yh", "ch"))
    return jax.shard_map(
        body,
        mesh=fine,
        in_specs=(
            P("ch", ROW, None),
            P(),
            P(),
            P(),
            P(),
            P(None, None, None, "ch"),
            P(None, None, "ch"),
            P(None, "ch"),
            P(None, "ch"),
            P(None, "ch"),
            P(None, "ch", None),
        ),
        out_specs=P("ch", ROW, None),
        check_vma=False,
    )
```

time: 115 us -> 113 us (0.983)
  blocking collectives: 43.4 us -> 7.2 us
  local copies, waits for them, and re-layouts: 11.3 us -> 23.5 us
  starting transfers between devices: 31.2 us -> 40.6 us
  waiting for transfers between devices: 23.1 us -> 31.8 us
  other arithmetic: 2.11 us -> 5.59 us
    all_gather x7 -> x1, blocking collectives: 43.4 us -> 7.2 us  [body(): packed = lax.all_gather(packed, 'ch', axis=0)]
    all_to_all x4 -> x6, starting transfers between devices: 31.2 us -> 40.6 us  [the longest x1 18.2 us: body(): got = lax.all_to_all(send, ('z', 'ch'), 0, 0, tiled=True)]
    all_to_all x4 -> x6, waiting for transfers between devices: 23.1 us -> 31.8 us  [the longest x1 8.73 us: body(): lax.all_to_all(jnp.concatenate([right, left], axis=1), PLANE, 0, 0, tiled...]
    reshape x6 -> x19, local copies, waits for them, and re-layouts: 1.04 us -> 6.87 us  [the longest x2 1.4 us: body(): x0.reshape(4, 8, 16, 4, 32).transpose(1, 3, 2, 0, 4).reshape(32, 16, 128)]
    slice x8 -> x18, local copies, waits for them, and re-layouts: 0.48 us -> 3.52 us  [the longest x2 1.26 us: body(): wg[0]]
    unnamed x24 -> x27, local copies, waits for them, and re-layouts: 3.52 us -> 0.97 us
    convert_element_type x4 -> x11, local copies, waits for them, and re-layouts: 0.49 us -> 2.85 us  [the longest x3 1.5 us: body(): got.reshape(16, 4, 8, 4, 32).transpose(1, 3, 2, 0, 4).reshape(128, 512)]
    convert_element_type x1 -> x4, local copies, waits for them, and re-layouts: 0.04 us -> 1.69 us  [norm(): ((v - mean) * lax.rsqrt(var + epsilon) * gain[:, None] + bias[:, None]).a...]
  transfers between devices with their start and end apart: 4 -> 6, of which waited for: 3 -> 5; matrix products, arithmetic and copies ran while one was open for 3% -> 13% of each run, Pallas kernels for 0% -> 0%
where the time goes in v3:
time: 113 us; the launch traced here: 112 us
  starting transfers between devices  40.6 us (36%)
  waiting for transfers between devices  31.8 us (28%)
  local copies, waits for them, and re-layouts  23.5 us (21%)
  blocking collectives  7.2 us (6%)
  other arithmetic  5.59 us (5%)
  matrix products  2.55 us (2%)
    all_to_all x1, starting transfers between devices, body(): got = lax.all_to_all(send, ('z', 'ch'), 0, 0, tiled=True)  18.2 us
    all_to_all x1, waiting for transfers between devices, body(): lax.all_to_all(jnp.concatenate([right, left], axis=1), PLANE, 0, 0, tiled...  8.73 us
    all_to_all x1, waiting for transfers between devices, body(): x0 = lax.all_to_all(x0, PLANE, 0, 0, tiled=True)  7.59 us
    all_to_all x1, starting transfers between devices, body(): lax.all_to_all(send, PLANE, 0, 0, tiled=True).reshape(8, 4, 2, 16, 4, 32)  7.32 us
    all_gather x1, blocking collectives, body(): packed = lax.all_gather(packed, 'ch', axis=0)  7.2 us
    all_to_all x1, waiting for transfers between devices, body(): x1 = lax.all_to_all(x1, PLANE, 0, 0, tiled=True)  7.07 us
    all_to_all x1, waiting for transfers between devices, body(): lax.all_to_all(send, PLANE, 0, 0, tiled=True).reshape(8, 4, 2, 16, 4, 32)  6.79 us
    all_to_all x1, starting transfers between devices, body(): lax.all_to_all(jnp.concatenate([right, left], axis=1), PLANE, 0, 0, tiled...  4.15 us
  transfers between devices with their start and end apart: 6, of which 5 were waited for; matrix products, arithmetic and copies ran while one was open for 13% of the time, Pallas kernels for 0%

profile of v3, /device:TPU:1, one launch (start us, length us, event | category | flops | bytes accessed | tf_op | source)
XLA Modules:
  0.0 112.1 jit_solution(4766533581411632312)
XLA Ops:
  0.0 0.8 copy.102
  1.9 18.2 %all-to-all-start = ((bf16[64,8,128]{2,1,0:T(8,128)(2,1)}), bf16[64,8,128]{2,1,0:T(8,128)(2,1)S(1)}, u32[]{:S(2)}, u32[]{:S(2)}) async-start(bf16[64,8,128]{2,1,0:T(8,128)(2,1)} %bitcast.1), calls=%async_computation | async-start | bytes 262144 | tf_op jit(solution)/shard_map/all_to_all | solution.py:33
  20.1 0.7 reduce-precision_convert_fusion.1
  21.0 0.8 copy.108
  21.9 0.8 copy.106
  23.3 7.2 %all-gather = bf16[1568,128]{1,0:T(8,128)(2,1)S(1)} all-gather(bf16[392,128]{1,0:T(8,128)(2,1)S(1)} %copy.110), channel_id=2, replica_groups=mesh['x'=4,'z'=16,'yh'=2,'ch'=4] {'ch'}, dimensions={0}, use_global_device_ids=true | all-gather | bytes 501760 | tf_op jit(solution)/shard_map/all_gather | solution.py:44
  34.4 1.2 %fusion.68 = (bf16[1,128,4,32]{3,0,1,2:T(2,128)(2,1)}, bf16[1,128,4,32]{3,0,1,2:T(2,128)(2,1)}) fusion(bf16[2,128,4,32]{3,0,1,2:T(2,128)(2,1)S(1)} %bitcast.165), kind=kLoop, calls=%fused_computation.140 | loop fusion | bytes 131072 | tf_op jit(solution)/shard_map/slice | solution.py:73
  35.5 1.7 %all-to-all-done = bf16[64,8,128]{2,1,0:T(8,128)(2,1)S(1)} async-done(((bf16[64,8,128]{2,1,0:T(8,128)(2,1)}), bf16[64,8,128]{2,1,0:T(8,128)(2,1)S(1)}, u32[]{:S(2)}, u32[]{:S(2)}) %all-to-all-start) | async-done | bytes 131104 | tf_op jit(solution)/shard_map/all_to_all | solution.py:33
  41.3 0.8 maximum_bitcast_fusion
  42.2 1.2 %reshape.544 = bf16[32,32,128]{2,1,0:T(8,128)(2,1)} reshape(bf16[32,2,16,4,32]{4,3,2,1,0:T(4,128)(2,1)S(1)} %maximum_bitcast_fusion) | data formatting | bytes 524288 | tf_op jit(solution)/shard_map/reshape | solution.py:67
  43.4 7.3 %all-to-all-start.1 = ((bf16[32,32,128]{2,1,0:T(8,128)(2,1)}), bf16[32,32,128]{2,1,0:T(8,128)(2,1)S(1)}, u32[]{:S(2)}, u32[]{:S(2)}) async-start(bf16[32,32,128]{2,1,0:T(8,128)(2,1)} %reshape.544), calls=%async_computation.1 | async-start | bytes 524288 | tf_op jit(solution)/shard_map/all_to_all | solution.py:68
  52.9 6.8 %all-to-all-done.1 = bf16[32,32,128]{2,1,0:T(8,128)(2,1)S(1)} async-done(((bf16[32,32,128]{2,1,0:T(8,128)(2,1)}), bf16[32,32,128]{2,1,0:T(8,128)(2,1)S(1)}, u32[]{:S(2)}, u32[]{:S(2)}) %all-to-all-start.1) | async-done | bytes 262176 | tf_op jit(solution)/shard_map/all_to_all | solution.py:68
  60.6 0.8 bitcast_convert_fusion
  62.6 0.9 reshape.547
  63.5 3.7 %all-to-all-start.2 = ((bf16[32,16,128]{2,1,0:T(8,128)(2,1)}), bf16[32,16,128]{2,1,0:T(8,128)(2,1)S(1)}, u32[]{:S(2)}, u32[]{:S(2)}) async-start(bf16[32,16,128]{2,1,0:T(8,128)(2,1)} %reshape.547), calls=%async_computation.2 | async-start | bytes 262144 | tf_op jit(solution)/shard_map/all_to_all | solution.py:71
  67.4 7.6 %all-to-all-done.2 = bf16[32,16,128]{2,1,0:T(8,128)(2,1)S(1)} async-done(((bf16[32,16,128]{2,1,0:T(8,128)(2,1)}), bf16[32,16,128]{2,1,0:T(8,128)(2,1)S(1)}, u32[]{:S(2)}, u32[]{:S(2)}) %all-to-all-start.2) | async-done | bytes 131104 | tf_op jit(solution)/shard_map/all_to_all | solution.py:71
  77.5 0.7 reshape.548
  78.2 3.6 %all-to-all-start.3 = ((bf16[4,16,128]{2,1,0:T(8,128)(2,1)}), bf16[4,16,128]{2,1,0:T(8,128)(2,1)S(1)}, u32[]{:S(2)}, u32[]{:S(2)}) async-start(bf16[4,16,128]{2,1,0:T(8,128)(2,1)} %reshape.548), calls=%async_computation.3 | async-start | bytes 32768 | tf_op jit(solution)/shard_map/all_to_all | solution.py:95
  83.4 0.7 fusion.21
  84.4 0.7 fusion.29
  85.1 4.2 %all-to-all-start.4 = ((bf16[32,32,128]{2,1,0:T(8,128)(2,1)}), bf16[32,32,128]{2,1,0:T(8,128)(2,1)S(1)}, u32[]{:S(2)}, u32[]{:S(2)}) async-start(bf16[32,32,128]{2,1,0:T(8,128)(2,1)} %fusion.29), calls=%async_computation.4 | async-start | bytes 524288 | tf_op jit(solution)/shard_map/all_to_all | solution.py:86
  89.5 8.7 %all-to-all-done.4 = bf16[32,32,128]{2,1,0:T(8,128)(2,1)S(1)} async-done(((bf16[32,32,128]{2,1,0:T(8,128)(2,1)}), bf16[32,32,128]{2,1,0:T(8,128)(2,1)S(1)}, u32[]{:S(2)}, u32[]{:S(2)}) %all-to-all-start.4) | async-done | bytes 262176 | tf_op jit(solution)/shard_map/all_to_all | solution.py:86
  99.7 3.7 %all-to-all-start.5 = ((bf16[32,4,128]{2,1,0:T(4,128)(2,1)}), bf16[32,4,128]{2,1,0:T(4,128)(2,1)S(1)}, u32[]{:S(2)}, u32[]{:S(2)}) async-start(bf16[32,4,128]{2,1,0:T(4,128)(2,1)} %bitcast.63), calls=%async_computation.5 | async-start | bytes 65536 | tf_op jit(solution)/shard_map/all_to_all | solution.py:102
  103.7 7.1 %all-to-all-done.5 = bf16[32,4,128]{2,1,0:T(4,128)(2,1)S(1)} async-done(((bf16[32,4,128]{2,1,0:T(4,128)(2,1)}), bf16[32,4,128]{2,1,0:T(4,128)(2,1)S(1)}, u32[]{:S(2)}, u32[]{:S(2)}) %all-to-all-start.5) | async-done | bytes 32800 | tf_op jit(solution)/shard_map/all_to_all | solution.py:102
  (148 shorter events, 21.4 us)
Async XLA Ops:
  0.0 23.0 %copy-start.2 = (bf16[2,128,4,32]{1,3,2,0:T(8,128)(2,1)S(1)}, bf16[2,128,4,32]{1,3,2,0:T(8,128)(2,1)}, u32[]{:S(2)}) copy-start(bf16[2,128,4,32]{1,3,2,0:T(8,128)(2,1)} %param.16) | copy-start | bytes 196612
  1.9 35.3 %all-to-all-start = ((bf16[64,8,128]{2,1,0:T(8,128)(2,1)}), bf16[64,8,128]{2,1,0:T(8,128)(2,1)S(1)}, u32[]{:S(2)}, u32[]{:S(2)}) async-start(bf16[64,8,128]{2,1,0:T(8,128)(2,1)} %bitcast.1), calls=%async_computation | async-start | bytes 262144 | tf_op jit(solution)/shard_map/all_to_all | solution.py:33
  23.0 7.6 %copy-start.9 = (s32[128]{0:T(128)S(1)}, s32[128]{0:T(128)}, u32[]{:S(2)}) copy-start(s32[128]{0:T(128)} %param.13) | copy-start | bytes 1540
  31.6 0.8 copy-start.10
  31.6 1.3 %copy-start.7 = (f32[2,128]{1,0:T(2,128)S(1)}, f32[2,128]{1,0:T(2,128)}, u32[]{:S(2)}) copy-start(f32[2,128]{1,0:T(2,128)} %param.15) | copy-start | bytes 3076
  31.6 1.3 %copy-start.8 = (f32[2,128]{1,0:T(2,128)S(1)}, f32[2,128]{1,0:T(2,128)}, u32[]{:S(2)}) copy-start(f32[2,128]{1,0:T(2,128)} %param.14) | copy-start | bytes 3076
  42.2 8.7 %copy-start.1 = (bf16[1,128,4,32]{3,0,1,2:T(2,128)(2,1)S(1)}, bf16[1,128,4,32]{3,0,1,2:T(2,128)(2,1)}, u32[]{:S(2)}) copy-start(bf16[1,128,4,32]{3,0,1,2:T(2,128)(2,1)} %get-tuple-element.30) | copy-start | bytes 98308
  42.2 8.8 %copy-start = (bf16[1,128,4,32]{3,0,1,2:T(2,128)(2,1)S(1)}, bf16[1,128,4,32]{3,0,1,2:T(2,128)(2,1)}, u32[]{:S(2)}) copy-start(bf16[1,128,4,32]{3,0,1,2:T(2,128)(2,1)} %get-tuple-element.29) | copy-start | bytes 98308
  43.4 7.7 %copy-start.4 = (f32[4,32]{1,0:T(4,128)S(1)}, f32[4,32]{1,0:T(4,128)}, u32[]{:S(2)}) copy-start(f32[4,32]{1,0:T(4,128)} %get-tuple-element.37) | copy-start | bytes 1540
  43.4 7.8 %copy-start.3 = (f32[4,32]{1,0:T(4,128)S(1)}, f32[4,32]{1,0:T(4,128)}, u32[]{:S(2)}) copy-start(f32[4,32]{1,0:T(4,128)} %get-tuple-element.38) | copy-start | bytes 1540
  43.4 16.3 %all-to-all-start.1 = ((bf16[32,32,128]{2,1,0:T(8,128)(2,1)}), bf16[32,32,128]{2,1,0:T(8,128)(2,1)S(1)}, u32[]{:S(2)}, u32[]{:S(2)}) async-start(bf16[32,32,128]{2,1,0:T(8,128)(2,1)} %reshape.544), calls=%async_computation.1 | async-start | bytes 524288 | tf_op jit(solution)/shard_map/all_to_all | solution.py:68
  63.5 11.5 %all-to-all-start.2 = ((bf16[32,16,128]{2,1,0:T(8,128)(2,1)}), bf16[32,16,128]{2,1,0:T(8,128)(2,1)S(1)}, u32[]{:S(2)}, u32[]{:S(2)}) async-start(bf16[32,16,128]{2,1,0:T(8,128)(2,1)} %reshape.547), calls=%async_computation.2 | async-start | bytes 262144 | tf_op jit(solution)/shard_map/all_to_all | solution.py:71
  76.1 0.8 copy-start.5
  76.1 0.8 copy-start.6
  78.2 6.9 %all-to-all-start.3 = ((bf16[4,16,128]{2,1,0:T(8,128)(2,1)}), bf16[4,16,128]{2,1,0:T(8,128)(2,1)S(1)}, u32[]{:S(2)}, u32[]{:S(2)}) async-start(bf16[4,16,128]{2,1,0:T(8,128)(2,1)} %reshape.548), calls=%async_computation.3 | async-start | bytes 32768 | tf_op jit(solution)/shard_map/all_to_all | solution.py:95
  85.1 13.2 %all-to-all-start.4 = ((bf16[32,32,128]{2,1,0:T(8,128)(2,1)}), bf16[32,32,128]{2,1,0:T(8,128)(2,1)S(1)}, u32[]{:S(2)}, u32[]{:S(2)}) async-start(bf16[32,32,128]{2,1,0:T(8,128)(2,1)} %fusion.29), calls=%async_computation.4 | async-start | bytes 524288 | tf_op jit(solution)/shard_map/all_to_all | solution.py:86
  99.7 11.1 %all-to-all-start.5 = ((bf16[32,4,128]{2,1,0:T(4,128)(2,1)}), bf16[32,4,128]{2,1,0:T(4,128)(2,1)S(1)}, u32[]{:S(2)}, u32[]{:S(2)}) async-start(bf16[32,4,128]{2,1,0:T(4,128)(2,1)} %bitcast.63), calls=%async_computation.5 | async-start | bytes 65536 | tf_op jit(solution)/shard_map/all_to_all | solution.py:102

commit v4 on v3

v4 whole, which is shorter than its diff:
```python
import jax
import jax.numpy as jnp
from jax import lax
from jax.experimental import pallas as pl
from jax.experimental.pallas import tpu as pltpu
from jax.sharding import Mesh, PartitionSpec as P

epsilon = 1e-05
bf16 = jnp.bfloat16
f32 = jnp.float32
ROW = ("x", "z", "yh")
PLANE = ("x", "yh", "ch")
VMEM = pl.BlockSpec(memory_space=pltpu.VMEM)
SMEM = pl.BlockSpec(memory_space=pltpu.SMEM)


def call(kernel, outs, ins, scratch=(), flops=100_000_000):
    specs = [SMEM if a.dtype == jnp.int32 else VMEM for a in ins]
    moved = sum(a.size * a.dtype.itemsize for a in ins)
    return pl.pallas_call(
        kernel,
        out_shape=[jax.ShapeDtypeStruct(s, d) for s, d in outs],
        in_specs=specs,
        out_specs=[VMEM] * len(outs),
        scratch_shapes=[pltpu.VMEM(s, f32) for s in scratch],
        compiler_params=pltpu.CompilerParams(vmem_limit_bytes=32 * 1024 * 1024),
        cost_estimate=pl.CostEstimate(flops=flops, bytes_accessed=moved, transcendentals=0),
    )(*ins)


def tn(a, b):
    return lax.dot_general(a, b, (((0,), (0,)), ((), ())), preferred_element_type=f32)


def nt(a, b):
    return lax.dot_general(a, b, (((1,), (1,)), ((), ())), preferred_element_type=f32)


def sigmoid(v):
    return 1.0 / (1.0 + jnp.exp(-v))


def norm(v, gain, bias):
    mean = jnp.mean(v, axis=0, keepdims=True)
    var = jnp.mean(v * v, axis=0, keepdims=True) - mean * mean
    return ((v - mean) * lax.rsqrt(var + epsilon) * gain + bias).astype(bf16)


def lanes(pieces):
    return jnp.concatenate(pieces, axis=1)


def permutation():
    k = lax.broadcasted_iota(jnp.int32, (128, 128), 0)
    p = lax.broadcasted_iota(jnp.int32, (128, 128), 1)
    place = (k & 96) | ((k & 1) << 4) | ((k & 31) >> 1)
    return (place == p).astype(f32).astype(bf16)


def spread_kernel(x_ref, out_ref):
    t = jnp.dot(x_ref[...], permutation(), preferred_element_type=f32)
    for q in range(4):
        piece = lanes([t[c * 8 : c * 8 + 8, q * 32 : q * 32 + 32] for c in range(4)]).astype(bf16)
        for z in range(16):
            out_ref[z * 4 + q] = piece


def project(n, u, packed_ref, pm, out_ref, scr):
    sides = ([], [])
    for q in range(4):
        p = tn(packed_ref[q, u * 128 : u * 128 + 128, :], n)
        sides[0].append(sigmoid(p[0:32]) * p[32:64] * pm)
        sides[1].append(sigmoid(p[64:96]) * p[96:128] * pm)
    for s in range(2):
        for z in range(16):
            scr[pl.ds(s * 16 + z, 32, stride=32), :] = lanes([v[:, z * 32 : z * 32 + 32] for v in sides[s]])
    out_ref[...] = scr[...].astype(bf16).reshape(32, 32, 128)


def first_kernel(got_ref, cols_ref, packed_ref, pm_ref, out_ref, z_ref, n_ref, scr):
    rows = []
    for q in range(4):
        for c in range(4):
            pieces = [got_ref[z * 4 + q].astype(f32)[:, c * 32 : c * 32 + 32] for z in range(16)]
            rows.append(lanes(pieces))
    z0 = jnp.concatenate(rows, axis=0)
    z_ref[...] = z0
    n = norm(z0, cols_ref[:, 0:1], cols_ref[:, 2:3])
    n_ref[...] = n
    project(n, 0, packed_ref, pm_ref[...], out_ref, scr)


def gate_kernel(n_ref, packed_ref, cols_ref, same_ref, out_ref):
    for q in range(4):
        w = packed_ref[q, 256:384, 0:32]
        logits = tn(w, n_ref[...])
        out_ref[q * 32 : q * 32 + 32, :] = sigmoid(
            logits + cols_ref[q * 32 : q * 32 + 32, 8:9] * same_ref[...]
        )


def outgoing_kernel(got_ref, out_ref):
    row = lax.broadcasted_iota(jnp.int32, (128, 512), 0) >> 5
    lane = (lax.broadcasted_iota(jnp.int32, (128, 512), 1) >> 5) & 3
    same = row == lane
    left, right = [], []
    for q in range(4):
        left.append(jnp.concatenate([got_ref[a * 4 + q, 0:16, :] for a in range(8)], axis=0))
        right.append(jnp.concatenate([got_ref[a * 4 + q, 16:32, :] for a in range(8)], axis=0))
    left, right = lanes(left), lanes(right)
    for q in range(4):
        part = right[q * 32 : q * 32 + 32].astype(f32)
        block = jnp.where(same, jnp.concatenate([part] * 4, axis=0), 0.0).astype(bf16)
        x = nt(left, block).astype(bf16)
        for b in range(8):
            out_ref[b * 4 + q] = x[b * 16 : b * 16 + 16]


def middle_kernel(got_ref, z_ref, gate_ref, cols_ref, packed_ref, pm_ref, out_ref, z1_ref, n1_ref, scr, xs):
    xs[...] = got_ref[...].astype(f32).reshape(512, 128)
    slabs = [xs[pl.ds(z, 32, stride=16), :] for z in range(16)]
    x0 = jnp.concatenate(
        [lanes([s[:, d * 32 : d * 32 + 32] for s in slabs]) for d in range(4)], axis=0
    )
    xn = norm(x0, cols_ref[:, 4:5], cols_ref[:, 6:7])
    w = jnp.concatenate([packed_ref[q, 384:416, :] for q in range(4)], axis=0)
    z1 = (z_ref[...] + gate_ref[...] * tn(w, xn)).astype(bf16)
    z1_ref[...] = z1
    n1 = norm(z1.astype(f32), cols_ref[:, 1:2], cols_ref[:, 3:4])
    n1_ref[...] = n1
    project(n1, 1, packed_ref, pm_ref[...], out_ref, scr)


def own_kernel(at_ref, z1_ref, n1_ref, packed_ref, cols_ref, same_ref, out_ref):
    lane = lax.broadcasted_iota(jnp.int32, (512, 128), 0)
    col = lax.broadcasted_iota(jnp.int32, (512, 128), 1)
    pick = ((lane == at_ref[0] * 32 + col) & (col < 32)).astype(f32).astype(bf16)
    z1 = jnp.dot(z1_ref[...], pick, preferred_element_type=f32)
    n1 = jnp.dot(n1_ref[...], pick, preferred_element_type=f32).astype(bf16)
    same = jnp.dot(
        jnp.broadcast_to(same_ref[...], (8, 512)).astype(bf16), pick, preferred_element_type=f32
    )[0:1]
    for q in range(4):
        w = packed_ref[q, 256:384, 32:64]
        gate = sigmoid(tn(w, n1) + cols_ref[q * 32 : q * 32 + 32, 9:10] * same)
        part = z1[q * 32 : q * 32 + 32]
        out_ref[q * 32 : q * 32 + 32, :] = lanes(
            [part[:, 0:32], gate[:, 0:32], jnp.zeros((32, 64), f32)]
        ).astype(bf16)


def incoming_kernel(at_ref, got_ref, out_ref, scr):
    left, right = [], []
    for q in range(4):
        left.append(jnp.concatenate([got_ref[a * 4 + q, 0:16, :] for a in range(8)], axis=0))
        right.append(jnp.concatenate([got_ref[a * 4 + q, 16:32, :] for a in range(8)], axis=0))
    row = lax.broadcasted_iota(jnp.int32, (32, 512), 0)
    lane = lax.broadcasted_iota(jnp.int32, (32, 512), 1)
    want = (((row >> 1) & 3) << 7) | ((row >> 3) << 5) | ((row & 1) << 4) | at_ref[0]
    pick = (lane == want).astype(f32).astype(bf16)
    mine = nt(pick, lanes(left)).astype(bf16)
    prods = [jnp.dot(mine, r, preferred_element_type=f32) for r in right]
    for d in range(4):
        x = lanes([p[d * 8 : d * 8 + 8, d * 32 : d * 32 + 32] for p in prods])
        for q in range(4):
            scr[pl.ds(q * 8 + d, 8, stride=32), :] = x
            scr[pl.ds(q * 8 + d + 4, 8, stride=32), :] = x
    out_ref[...] = scr[...].astype(bf16).reshape(32, 8, 128)


def last_kernel(at_ref, got_ref, zg_ref, packed_ref, cols_ref, out_ref, xs, ys):
    xs[...] = got_ref[...].astype(f32).reshape(256, 128)
    x1 = jnp.concatenate([xs[pl.ds(d, 32, stride=8), :] for d in range(4)], axis=0)
    xn = norm(x1, cols_ref[:, 5:6], cols_ref[:, 7:8])
    w = jnp.concatenate([packed_ref[q, 416:448, :] for q in range(4)], axis=0)
    ys[...] = tn(w, xn)
    start = pl.multiple_of(at_ref[1] * 32, 32)
    y = ys[pl.ds(start, 32), :]
    parts = [zg_ref[s, pl.ds(start, 32), :].astype(f32) for s in range(4)]
    z1 = lanes([p[:, 0:32] for p in parts])
    gate = lanes([p[:, 32:64] for p in parts])
    out = (z1 + gate * y).astype(bf16)
    out_ref[...] = nt(out, permutation()).astype(bf16)


def three(v):
    hi = lax.reduce_precision(v, 8, 7)
    mid = lax.reduce_precision(v - hi, 8, 7)
    return jnp.stack([hi, mid, v - hi - mid]).astype(bf16)


def by_plane(v):
    return v.reshape(4, 16, 2).swapaxes(1, 2).reshape(128)


def body(pair_rep, residue_mask, chain_ids, in_gain, in_bias, w_proj, w_gate, pair_bias, out_gain, out_bias, w_out):
    ix, iz, iyh, q = (lax.axis_index(a) for a in ("x", "z", "yh", "ch"))
    at = jnp.stack([iz, q]).astype(jnp.int32)
    (send,) = call(spread_kernel, [((64, 8, 128), bf16)], [pair_rep.reshape(32, 128)])
    got = lax.all_to_all(send, ("z", "ch"), 0, 0, tiled=True)

    gates = jnp.concatenate([w_gate[0], w_gate[1], jnp.zeros((128, 64), bf16)], axis=1)
    small = three(jnp.stack([out_gain, out_bias, pair_bias])).reshape(18, 32)
    packed = jnp.concatenate(
        [w_proj.reshape(256, 128), gates, w_out.reshape(64, 128), jnp.pad(small, ((0, 14), (0, 96)))], axis=0
    )
    packed = lax.all_gather(packed, "ch", axis=0)
    small = packed[:, 448:466, :32].reshape(4, 3, 6, 32).astype(f32).sum(axis=1)
    small = small.transpose(0, 2, 1).reshape(128, 6)
    cols = jnp.concatenate([in_gain.T, in_bias.T, small], axis=1)

    mask = by_plane(residue_mask.astype(f32)).reshape(8, 16)
    chain = by_plane(chain_ids).reshape(8, 16)
    mine = ix * 2 + iyh
    mask_r = lax.dynamic_index_in_dim(mask, mine, 0, keepdims=False)
    chain_r = lax.dynamic_index_in_dim(chain, mine, 0, keepdims=False)
    mask_c = lax.dynamic_index_in_dim(mask.reshape(4, 32), q, 0, keepdims=False)
    chain_c = lax.dynamic_index_in_dim(chain.reshape(4, 32), q, 0, keepdims=False)
    pm = (mask_r[:, None] * mask_c[None, :]).reshape(1, 512)
    same = (chain_r[:, None] == chain_c[None, :]).astype(f32).reshape(1, 512)

    send, z0, n0 = call(
        first_kernel,
        [((32, 32, 128), bf16), ((128, 512), f32), ((128, 512), bf16)],
        [got, cols, packed, pm],
        [(1024, 128)],
    )
    got = lax.all_to_all(send, PLANE, 0, 0, tiled=True)
    (gate,) = call(gate_kernel, [((128, 512), f32)], [n0, packed, cols, same])
    (send,) = call(outgoing_kernel, [((32, 16, 128), bf16)], [got])
    got = lax.all_to_all(send, PLANE, 0, 0, tiled=True)
    send, z1, n1 = call(
        middle_kernel,
        [((32, 32, 128), bf16), ((128, 512), bf16), ((128, 512), bf16)],
        [got, z0, gate, cols, packed, pm],
        [(1024, 128), (512, 128)],
    )
    got = lax.all_to_all(send, PLANE, 0, 0, tiled=True)
    (zg,) = call(own_kernel, [((128, 128), bf16)], [at, z1, n1, packed, cols, same])
    (send,) = call(incoming_kernel, [((32, 8, 128), bf16)], [at, got], [(256, 128)])
    send, zg = lax.optimization_barrier((send, zg))
    got = lax.all_to_all(send, PLANE, 0, 0, tiled=True)
    zg = lax.all_gather(zg, "ch", axis=0)
    (out,) = call(
        last_kernel, [((32, 128), bf16)], [at, got, zg, packed, cols], [(256, 128), (128, 128)]
    )
    return out.reshape(32, 1, 128)


def solution(mesh):
    fine = Mesh(mesh.devices.reshape(4, 16, 2, 4), ("x", "z", "yh", "ch"))
    return jax.shard_map(
        body,
        mesh=fine,
        in_specs=(
            P("ch", ROW, None),
            P(),
            P(),
            P(),
            P(),
            P(None, None, None, "ch"),
            P(None, None, "ch"),
            P(None, "ch"),
            P(None, "ch"),
            P(None, "ch"),
            P(None, "ch", None),
        ),
        out_specs=P("ch", ROW, None),
        check_vma=False,
    )
```

time: 113 us -> 97.9 us (0.87)
  local copies, waits for them, and re-layouts: 23.5 us -> 5.12 us
  Pallas kernels: 0 us -> 10.4 us
  blocking collectives: 7.2 us -> 13.4 us
  other arithmetic: 5.59 us -> 0.37 us
  starting transfers between devices: 40.6 us -> 36.8 us
  matrix products: 2.55 us -> 0 us
    pallas_call x0 -> x8, Pallas kernels: none -> 10.4 us  [call(): pl.pallas_call(kernel, out_shape=[jax.ShapeDtypeStruct(s, d) for s, d in...]
    reshape x16 -> x1, local copies, waits for them, and re-layouts: 5.79 us -> 0.08 us  [body(): small = small.transpose(0, 2, 1).reshape(128, 6)]
    all_gather x0 -> x1, blocking collectives: none -> 5.7 us  [body(): zg = lax.all_gather(zg, 'ch', axis=0)]
    convert_element_type x14 -> x2, local copies, waits for them, and re-layouts: 4.45 us -> 0.09 us  [the longest x1 0.08 us: body(): same = (chain_r[:, None] == chain_c[None, :]).astype(f32).reshape(1, 512)]
    all_to_all x5 -> x4, waiting for transfers between devices: 30.2 us -> 25.8 us  [body(): got = lax.all_to_all(send, PLANE, 0, 0, tiled=True)]
    all_to_all x5 -> x4, starting transfers between devices: 22.5 us -> 18.6 us  [body(): got = lax.all_to_all(send, PLANE, 0, 0, tiled=True)]
    slice x18 -> x0, local copies, waits for them, and re-layouts: 3.52 us -> none  [the longest x2 1.26 us: body(): wg[0]]
    all_to_all x1, waiting for transfers between devices: 1.66 us -> 5.03 us  [body(): got = lax.all_to_all(send, ('z', 'ch'), 0, 0, tiled=True)]
  transfers between devices with their start and end apart: 6 -> 5, of which waited for: 5 -> 5; matrix products, arithmetic and copies ran while one was open for 13% -> 2% of each run, Pallas kernels for 0% -> 1%
where the time goes in v4:
time: 97.9 us; the launch traced here: 97.1 us
  starting transfers between devices  36.8 us (38%)
  waiting for transfers between devices  30.9 us (32%)
  blocking collectives  13.4 us (14%)
  Pallas kernels  10.4 us (11%)
  local copies, waits for them, and re-layouts  5.12 us (5%)
    all_to_all x4, waiting for transfers between devices, body(): got = lax.all_to_all(send, PLANE, 0, 0, tiled=True)  25.8 us
    all_to_all x4, starting transfers between devices, body(): got = lax.all_to_all(send, PLANE, 0, 0, tiled=True)  18.6 us
    all_to_all x1, starting transfers between devices, body(): got = lax.all_to_all(send, ('z', 'ch'), 0, 0, tiled=True)  18.2 us
    pallas_call x8, Pallas kernels, call(): pl.pallas_call(kernel, out_shape=[jax.ShapeDtypeStruct(s, d) for s, d in...  10.4 us
    all_gather x1, blocking collectives, body(): packed = lax.all_gather(packed, 'ch', axis=0)  7.71 us
    all_gather x1, blocking collectives, body(): zg = lax.all_gather(zg, 'ch', axis=0)  5.7 us
    all_to_all x1, waiting for transfers between devices, body(): got = lax.all_to_all(send, ('z', 'ch'), 0, 0, tiled=True)  5.03 us
    unnamed x24, local copies, waits for them, and re-layouts  3.72 us
  transfers between devices with their start and end apart: 5, of which 5 were waited for; matrix products, arithmetic and copies ran while one was open for 2% of the time, Pallas kernels for 1%

profile of v4, /device:TPU:1, one launch (start us, length us, event | category | flops | bytes accessed | tf_op | source)
XLA Modules:
  0.0 97.1 jit_solution(12802073222768388476)
XLA Ops:
  0.0 0.7 copy-done
  0.7 0.9 shard_map.109
  1.6 18.2 %all-to-all-start = ((bf16[64,8,128]{2,1,0:T(8,128)(2,1)}), bf16[64,8,128]{2,1,0:T(8,128)(2,1)S(1)}, u32[]{:S(2)}, u32[]{:S(2)}) async-start(bf16[64,8,128]{2,1,0:T(8,128)(2,1)} %shard_map.109), calls=%async_computation | async-start | bytes 262144 | tf_op jit(solution)/shard_map/all_to_all | solution.py:200
  19.8 0.6 copy-done.10
  20.5 0.6 copy-done.6
  21.3 0.6 copy-done.3
  23.2 7.7 %all-gather = bf16[1920,128]{1,0:T(8,128)(2,1)S(1)} all-gather(bf16[480,128]{1,0:T(8,128)(2,1)S(1)} %copy.45), channel_id=2, replica_groups=mesh['x'=4,'z'=16,'yh'=2,'ch'=4] {'ch'}, dimensions={0}, use_global_device_ids=true | all-gather | bytes 614400 | tf_op jit(solution)/shard_map/all_gather | solution.py:207
  31.0 0.6 copy-done.5
  31.8 5.0 %all-to-all-done.got_ref = bf16[64,8,128]{2,1,0:T(8,128)(2,1)S(1)} async-done(((bf16[64,8,128]{2,1,0:T(8,128)(2,1)}), bf16[64,8,128]{2,1,0:T(8,128)(2,1)S(1)}, u32[]{:S(2)}, u32[]{:S(2)}) %all-to-all-start) | async-done | bytes 131104 | tf_op jit(solution)/shard_map/all_to_all | solution.py:200
  36.9 1.9 %shard_map.110 = (bf16[32,32,128]{2,1,0:T(8,128)(2,1)}, f32[128,512]{1,0:T(8,128)S(1)}, bf16[128,512]{1,0:T(8,128)(2,1)S(1)}) custom-call(bf16[64,8,128]{2,1,0:T(8,128)(2,1)S(1)} %all-to-all-done.got_ref, f32[128,10]{1,0:T(8,128)S(1)} %copy.49.cols_ref, bf16[4,480,128]{2,1,0:T(8,128)(2,1)S(1)} %bitcast.40, f32[1,512]{1,0:T(1,128)S(1)} %mul.36.pm_ref), custom_call_target="tpu_custom_call" | custom-call | flops 100000000 | bytes 629760 | tf_op jit(solution)/shard_map/pallas_call | solution.py:20
  38.7 7.3 %all-to-all-start.1 = ((bf16[32,32,128]{2,1,0:T(8,128)(2,1)}), bf16[32,32,128]{2,1,0:T(8,128)(2,1)S(1)}, u32[]{:S(2)}, u32[]{:S(2)}) async-start(bf16[32,32,128]{2,1,0:T(8,128)(2,1)} %get-tuple-element.13), calls=%async_computation.1 | async-start | bytes 524288 | tf_op jit(solution)/shard_map/all_to_all | solution.py:228
  46.4 8.6 %all-to-all-done.1.got_ref = bf16[32,32,128]{2,1,0:T(8,128)(2,1)S(1)} async-done(((bf16[32,32,128]{2,1,0:T(8,128)(2,1)}), bf16[32,32,128]{2,1,0:T(8,128)(2,1)S(1)}, u32[]{:S(2)}, u32[]{:S(2)}) %all-to-all-start.1) | async-done | bytes 262176 | tf_op jit(solution)/shard_map/all_to_all | solution.py:228
  55.1 1.0 shard_map.111
  56.0 3.7 %all-to-all-start.2 = ((bf16[32,16,128]{2,1,0:T(8,128)(2,1)}), bf16[32,16,128]{2,1,0:T(8,128)(2,1)S(1)}, u32[]{:S(2)}, u32[]{:S(2)}) async-start(bf16[32,16,128]{2,1,0:T(8,128)(2,1)} %shard_map.111), calls=%async_computation.2 | async-start | bytes 262144 | tf_op jit(solution)/shard_map/all_to_all | solution.py:231
  60.1 7.4 %all-to-all-done.2.got_ref = bf16[32,16,128]{2,1,0:T(8,128)(2,1)S(1)} async-done(((bf16[32,16,128]{2,1,0:T(8,128)(2,1)}), bf16[32,16,128]{2,1,0:T(8,128)(2,1)S(1)}, u32[]{:S(2)}, u32[]{:S(2)}) %all-to-all-start.2) | async-done | bytes 131104 | tf_op jit(solution)/shard_map/all_to_all | solution.py:231
  67.5 2.2 %shard_map.113 = (bf16[32,32,128]{2,1,0:T(8,128)(2,1)}, bf16[128,512]{1,0:T(8,128)(2,1)S(1)}, bf16[128,512]{1,0:T(8,128)(2,1)S(1)}) custom-call(bf16[32,16,128]{2,1,0:T(8,128)(2,1)S(1)} %all-to-all-done.2.got_ref, f32[128,512]{1,0:T(8,128)S(1)} %get-tuple-element.14.z_ref, f32[128,512]{1,0:T(8,128)S(1)} %shard_map.112.gate_ref, ...), custom_call_target="tpu_custom_call" | custom-call | flops 100000000 | bytes 1154048 | tf_op jit(solution)/shard_map/pallas_call | solution.py:20
  69.7 3.9 %all-to-all-start.3 = ((bf16[32,32,128]{2,1,0:T(8,128)(2,1)}), bf16[32,32,128]{2,1,0:T(8,128)(2,1)S(1)}, u32[]{:S(2)}, u32[]{:S(2)}) async-start(bf16[32,32,128]{2,1,0:T(8,128)(2,1)} %get-tuple-element.16), calls=%async_computation.3 | async-start | bytes 524288 | tf_op jit(solution)/shard_map/all_to_all | solution.py:238
  73.7 1.0 %shard_map.115 = bf16[128,128]{1,0:T(8,128)(2,1)S(1)} custom-call(s32[2]{0:T(128)S(1)} %pad_add_fusion.at_ref, bf16[128,512]{1,0:T(8,128)(2,1)S(1)} %get-tuple-element.17.z1_ref, bf16[128,512]{1,0:T(8,128)(2,1)S(1)} %get-tuple-element.18.n1_ref, bf16[4,480,128]{2,1,0:T(8,128)(2,1)S(1)} %bitcast.43, f32[128,10]{1,0:T(8,128)S(1)} %copy.49.cols_ref, ...), custom_call_target="tpu_custom_call" | custom-call | flops 100000000 | bytes 760840 | tf_op jit(solution)/shard_map/pallas_call | solution.py:20
  74.7 8.0 %all-to-all-done.3.got_ref = bf16[32,32,128]{2,1,0:T(8,128)(2,1)S(1)} async-done(((bf16[32,32,128]{2,1,0:T(8,128)(2,1)}), bf16[32,32,128]{2,1,0:T(8,128)(2,1)S(1)}, u32[]{:S(2)}, u32[]{:S(2)}) %all-to-all-start.3) | async-done | bytes 262176 | tf_op jit(solution)/shard_map/all_to_all | solution.py:238
  82.8 1.6 %shard_map.114 = bf16[32,8,128]{2,1,0:T(8,128)(2,1)} custom-call(s32[2]{0:T(128)S(1)} %pad_add_fusion.at_ref, bf16[32,32,128]{2,1,0:T(8,128)(2,1)S(1)} %all-to-all-done.3.got_ref), custom_call_target="tpu_custom_call" | custom-call | flops 100000000 | bytes 262152 | tf_op jit(solution)/shard_map/pallas_call | solution.py:20
  84.4 3.7 %all-to-all-start.4 = ((bf16[32,8,128]{2,1,0:T(8,128)(2,1)}), bf16[32,8,128]{2,1,0:T(8,128)(2,1)S(1)}, u32[]{:S(2)}, u32[]{:S(2)}) async-start(bf16[32,8,128]{2,1,0:T(8,128)(2,1)} %shard_map.114), calls=%async_computation.4 | async-start | bytes 131072 | tf_op jit(solution)/shard_map/all_to_all | solution.py:242
  88.1 5.7 %all-gather.1 = bf16[512,128]{1,0:T(8,128)(2,1)S(1)} all-gather(bf16[128,128]{1,0:T(8,128)(2,1)S(1)} %shard_map.115), channel_id=3, replica_groups=mesh['x'=4,'z'=16,'yh'=2,'ch'=4] {'ch'}, dimensions={0}, use_global_device_ids=true | all-gather | bytes 163840 | tf_op jit(solution)/shard_map/all_gather | solution.py:243
  93.8 1.8 %all-to-all-done.4.got_ref = bf16[32,8,128]{2,1,0:T(8,128)(2,1)S(1)} async-done(((bf16[32,8,128]{2,1,0:T(8,128)(2,1)}), bf16[32,8,128]{2,1,0:T(8,128)(2,1)S(1)}, u32[]{:S(2)}, u32[]{:S(2)}) %all-to-all-start.4) | async-done | bytes 65568 | tf_op jit(solution)/shard_map/all_to_all | solution.py:242
  95.6 1.5 %shard_map.116 = bf16[32,128]{1,0:T(8,128)(2,1)} custom-call(s32[2]{0:T(128)S(1)} %pad_add_fusion.at_ref, bf16[32,8,128]{2,1,0:T(8,128)(2,1)S(1)} %all-to-all-done.4.got_ref, bf16[4,128,128]{2,1,0:T(8,128)(2,1)S(1)} %bitcast.45, bf16[4,480,128]{2,1,0:T(8,128)(2,1)S(1)} %bitcast.44, f32[128,10]{1,0:T(8,128)S(1)} %copy.49.cols_ref), custom_call_target="tpu_custom_call" | custom-call | flops 100000000 | bytes 693256 | tf_op jit(solution)/shard_map/pallas_call | solution.py:20
  (52 shorter events, 2.7 us)
Async XLA Ops:
  0.0 0.7 copy-start
  1.6 35.3 %all-to-all-start = ((bf16[64,8,128]{2,1,0:T(8,128)(2,1)}), bf16[64,8,128]{2,1,0:T(8,128)(2,1)S(1)}, u32[]{:S(2)}, u32[]{:S(2)}) async-start(bf16[64,8,128]{2,1,0:T(8,128)(2,1)} %shard_map.109), calls=%async_computation | async-start | bytes 262144 | tf_op jit(solution)/shard_map/all_to_all | solution.py:200
  19.8 0.7 copy-start.10
  19.8 0.7 copy-start.7
  19.8 0.7 copy-start.8
  20.4 0.7 copy-start.6
  21.1 0.7 copy-start.3
  21.8 0.7 copy-start.2
  22.0 0.8 copy-start.1
  30.9 0.7 copy-start.5
  31.0 0.7 copy-start.4
  38.7 7.3 %copy-start.9 = (s32[128]{0:T(128)S(1)}, s32[128]{0:T(128)}, u32[]{:S(2)}) copy-start(s32[128]{0:T(128)} %param.13) | copy-start | bytes 1540
  38.7 16.3 %all-to-all-start.1 = ((bf16[32,32,128]{2,1,0:T(8,128)(2,1)}), bf16[32,32,128]{2,1,0:T(8,128)(2,1)S(1)}, u32[]{:S(2)}, u32[]{:S(2)}) async-start(bf16[32,32,128]{2,1,0:T(8,128)(2,1)} %get-tuple-element.13), calls=%async_computation.1 | async-start | bytes 524288 | tf_op jit(solution)/shard_map/all_to_all | solution.py:228
  56.0 11.5 %all-to-all-start.2 = ((bf16[32,16,128]{2,1,0:T(8,128)(2,1)}), bf16[32,16,128]{2,1,0:T(8,128)(2,1)S(1)}, u32[]{:S(2)}, u32[]{:S(2)}) async-start(bf16[32,16,128]{2,1,0:T(8,128)(2,1)} %shard_map.111), calls=%async_computation.2 | async-start | bytes 262144 | tf_op jit(solution)/shard_map/all_to_all | solution.py:231
  69.7 13.0 %all-to-all-start.3 = ((bf16[32,32,128]{2,1,0:T(8,128)(2,1)}), bf16[32,32,128]{2,1,0:T(8,128)(2,1)S(1)}, u32[]{:S(2)}, u32[]{:S(2)}) async-start(bf16[32,32,128]{2,1,0:T(8,128)(2,1)} %get-tuple-element.16), calls=%async_computation.3 | async-start | bytes 524288 | tf_op jit(solution)/shard_map/all_to_all | solution.py:238
  84.4 11.2 %all-to-all-start.4 = ((bf16[32,8,128]{2,1,0:T(8,128)(2,1)}), bf16[32,8,128]{2,1,0:T(8,128)(2,1)S(1)}, u32[]{:S(2)}, u32[]{:S(2)}) async-start(bf16[32,8,128]{2,1,0:T(8,128)(2,1)} %shard_map.114), calls=%async_computation.4 | async-start | bytes 131072 | tf_op jit(solution)/shard_map/all_to_all | solution.py:242

commit v5 on v4

--- a/solution.py
+++ b/solution.py
@@ -11,16 +11,15 @@
 ROW = ("x", "z", "yh")
 PLANE = ("x", "yh", "ch")
 VMEM = pl.BlockSpec(memory_space=pltpu.VMEM)
-SMEM = pl.BlockSpec(memory_space=pltpu.SMEM)
+HBM = pl.BlockSpec(memory_space=pltpu.HBM)
 
 
 def call(kernel, outs, ins, scratch=(), flops=100_000_000):
-    specs = [SMEM if a.dtype == jnp.int32 else VMEM for a in ins]
     moved = sum(a.size * a.dtype.itemsize for a in ins)
     return pl.pallas_call(
         kernel,
         out_shape=[jax.ShapeDtypeStruct(s, d) for s, d in outs],
-        in_specs=specs,
+        in_specs=[VMEM] * len(ins),
         out_specs=[VMEM] * len(outs),
         scratch_shapes=[pltpu.VMEM(s, f32) for s in scratch],
         compiler_params=pltpu.CompilerParams(vmem_limit_bytes=32 * 1024 * 1024),
@@ -37,7 +36,7 @@
 
 
 def sigmoid(v):
-    return 1.0 / (1.0 + jnp.exp(-v))
+    return 0.5 * jnp.tanh(0.5 * v) + 0.5
 
 
 def norm(v, gain, bias):
@@ -57,18 +56,41 @@
     return (place == p).astype(f32).astype(bf16)
 
 
-def spread_kernel(x_ref, out_ref):
-    t = jnp.dot(x_ref[...], permutation(), preferred_element_type=f32)
-    for q in range(4):
-        piece = lanes([t[c * 8 : c * 8 + 8, q * 32 : q * 32 + 32] for c in range(4)]).astype(bf16)
-        for z in range(16):
-            out_ref[z * 4 + q] = piece
-
-
-def project(n, u, packed_ref, pm, out_ref, scr):
+def spread_kernel(x_ref, out_ref, x_vmem, tile, sem_in, sems):
+    load = pltpu.make_async_copy(x_ref, x_vmem, sem_in)
+    load.start()
+    perm = permutation()
+    load.wait()
+    t = jnp.dot(x_vmem[...], perm, preferred_element_type=f32)
+    for q in range(4):
+        piece = lanes([t[c * 8 : c * 8 + 8, q * 32 : q * 32 + 32] for c in range(4)])
+        tile[q] = piece.astype(bf16)
+    copies = [pltpu.make_async_copy(tile, out_ref.at[z * 4 : z * 4 + 4], sems.at[z]) for z in range(16)]
+    for c in copies:
+        c.start()
+    for c in copies:
+        c.wait()
+
+
+def spread(x):
+    return pl.pallas_call(
+        spread_kernel,
+        out_shape=jax.ShapeDtypeStruct((64, 8, 128), bf16),
+        in_specs=[HBM],
+        out_specs=HBM,
+        scratch_shapes=[
+            pltpu.VMEM((32, 128), bf16),
+            pltpu.VMEM((4, 8, 128), bf16),
+            pltpu.SemaphoreType.DMA,
+            pltpu.SemaphoreType.DMA((16,)),
+        ],
+    )(x)
+
+
+def project(n, w_ref, pm, out_ref, scr):
     sides = ([], [])
     for q in range(4):
-        p = tn(packed_ref[q, u * 128 : u * 128 + 128, :], n)
+        p = jnp.dot(w_ref[q, 0:128, :], n, preferred_element_type=f32)
         sides[0].append(sigmoid(p[0:32]) * p[32:64] * pm)
         sides[1].append(sigmoid(p[64:96]) * p[96:128] * pm)
     for s in range(2):
@@ -77,7 +99,7 @@
     out_ref[...] = scr[...].astype(bf16).reshape(32, 32, 128)
 
 
-def first_kernel(got_ref, cols_ref, packed_ref, pm_ref, out_ref, z_ref, n_ref, scr):
+def first_kernel(got_ref, gain_ref, w_ref, pm_ref, out_ref, z_ref, n_ref, scr):
     rows = []
     for q in range(4):
         for c in range(4):
@@ -85,17 +107,16 @@
             rows.append(lanes(pieces))
     z0 = jnp.concatenate(rows, axis=0)
     z_ref[...] = z0
-    n = norm(z0, cols_ref[:, 0:1], cols_ref[:, 2:3])
+    n = norm(z0, gain_ref[:, 0:1], gain_ref[:, 2:3])
     n_ref[...] = n
-    project(n, 0, packed_ref, pm_ref[...], out_ref, scr)
+    project(n, w_ref, pm_ref[...], out_ref, scr)
 
 
 def gate_kernel(n_ref, packed_ref, cols_ref, same_ref, out_ref):
     for q in range(4):
-        w = packed_ref[q, 256:384, 0:32]
-        logits = tn(w, n_ref[...])
+        logits = jnp.dot(packed_ref[q, 128:160, :], n_ref[...], preferred_element_type=f32)
         out_ref[q * 32 : q * 32 + 32, :] = sigmoid(
-            logits + cols_ref[q * 32 : q * 32 + 32, 8:9] * same_ref[...]
+            logits + cols_ref[q * 32 : q * 32 + 32, 4:5] * same_ref[...]
         )
 
 
@@ -116,47 +137,47 @@
             out_ref[b * 4 + q] = x[b * 16 : b * 16 + 16]
 
 
-def middle_kernel(got_ref, z_ref, gate_ref, cols_ref, packed_ref, pm_ref, out_ref, z1_ref, n1_ref, scr, xs):
+def middle_kernel(got_ref, z_ref, gate_ref, gain_ref, cols_ref, packed_ref, pm_ref, out_ref, z1_ref, n1_ref, scr, xs):
     xs[...] = got_ref[...].astype(f32).reshape(512, 128)
     slabs = [xs[pl.ds(z, 32, stride=16), :] for z in range(16)]
     x0 = jnp.concatenate(
         [lanes([s[:, d * 32 : d * 32 + 32] for s in slabs]) for d in range(4)], axis=0
     )
-    xn = norm(x0, cols_ref[:, 4:5], cols_ref[:, 6:7])
-    w = jnp.concatenate([packed_ref[q, 384:416, :] for q in range(4)], axis=0)
+    xn = norm(x0, cols_ref[:, 0:1], cols_ref[:, 2:3])
+    w = jnp.concatenate([packed_ref[q, 192:224, :] for q in range(4)], axis=0)
     z1 = (z_ref[...] + gate_ref[...] * tn(w, xn)).astype(bf16)
     z1_ref[...] = z1
-    n1 = norm(z1.astype(f32), cols_ref[:, 1:2], cols_ref[:, 3:4])
+    n1 = norm(z1.astype(f32), gain_ref[:, 1:2], gain_ref[:, 3:4])
     n1_ref[...] = n1
-    project(n1, 1, packed_ref, pm_ref[...], out_ref, scr)
-
-
-def own_kernel(at_ref, z1_ref, n1_ref, packed_ref, cols_ref, same_ref, out_ref):
+    project(n1, packed_ref, pm_ref[...], out_ref, scr)
+
+
+def own_kernel(z1_ref, n1_ref, packed_ref, cols_ref, same_ref, out_ref):
     lane = lax.broadcasted_iota(jnp.int32, (512, 128), 0)
     col = lax.broadcasted_iota(jnp.int32, (512, 128), 1)
-    pick = ((lane == at_ref[0] * 32 + col) & (col < 32)).astype(f32).astype(bf16)
+    pick = ((lane == lax.axis_index("z") * 32 + col) & (col < 32)).astype(f32).astype(bf16)
     z1 = jnp.dot(z1_ref[...], pick, preferred_element_type=f32)
     n1 = jnp.dot(n1_ref[...], pick, preferred_element_type=f32).astype(bf16)
     same = jnp.dot(
         jnp.broadcast_to(same_ref[...], (8, 512)).astype(bf16), pick, preferred_element_type=f32
     )[0:1]
     for q in range(4):
-        w = packed_ref[q, 256:384, 32:64]
-        gate = sigmoid(tn(w, n1) + cols_ref[q * 32 : q * 32 + 32, 9:10] * same)
+        logits = jnp.dot(packed_ref[q, 160:192, :], n1, preferred_element_type=f32)
+        gate = sigmoid(logits + cols_ref[q * 32 : q * 32 + 32, 5:6] * same)
         part = z1[q * 32 : q * 32 + 32]
         out_ref[q * 32 : q * 32 + 32, :] = lanes(
             [part[:, 0:32], gate[:, 0:32], jnp.zeros((32, 64), f32)]
         ).astype(bf16)
 
 
-def incoming_kernel(at_ref, got_ref, out_ref, scr):
+def incoming_kernel(got_ref, out_ref, scr):
     left, right = [], []
     for q in range(4):
         left.append(jnp.concatenate([got_ref[a * 4 + q, 0:16, :] for a in range(8)], axis=0))
         right.append(jnp.concatenate([got_ref[a * 4 + q, 16:32, :] for a in range(8)], axis=0))
     row = lax.broadcasted_iota(jnp.int32, (32, 512), 0)
     lane = lax.broadcasted_iota(jnp.int32, (32, 512), 1)
-    want = (((row >> 1) & 3) << 7) | ((row >> 3) << 5) | ((row & 1) << 4) | at_ref[0]
+    want = (((row >> 1) & 3) << 7) | ((row >> 3) << 5) | ((row & 1) << 4) | lax.axis_index("z")
     pick = (lane == want).astype(f32).astype(bf16)
     mine = nt(pick, lanes(left)).astype(bf16)
     prods = [jnp.dot(mine, r, preferred_element_type=f32) for r in right]
@@ -168,13 +189,13 @@
     out_ref[...] = scr[...].astype(bf16).reshape(32, 8, 128)
 
 
-def last_kernel(at_ref, got_ref, zg_ref, packed_ref, cols_ref, out_ref, xs, ys):
+def last_kernel(got_ref, zg_ref, packed_ref, cols_ref, out_ref, xs, ys):
     xs[...] = got_ref[...].astype(f32).reshape(256, 128)
     x1 = jnp.concatenate([xs[pl.ds(d, 32, stride=8), :] for d in range(4)], axis=0)
-    xn = norm(x1, cols_ref[:, 5:6], cols_ref[:, 7:8])
-    w = jnp.concatenate([packed_ref[q, 416:448, :] for q in range(4)], axis=0)
+    xn = norm(x1, cols_ref[:, 1:2], cols_ref[:, 3:4])
+    w = jnp.concatenate([packed_ref[q, 224:256, :] for q in range(4)], axis=0)
     ys[...] = tn(w, xn)
-    start = pl.multiple_of(at_ref[1] * 32, 32)
+    start = pl.multiple_of(lax.axis_index("ch") * 32, 32)
     y = ys[pl.ds(start, 32), :]
     parts = [zg_ref[s, pl.ds(start, 32), :].astype(f32) for s in range(4)]
     z1 = lanes([p[:, 0:32] for p in parts])
@@ -194,20 +215,23 @@
 
 
 def body(pair_rep, residue_mask, chain_ids, in_gain, in_bias, w_proj, w_gate, pair_bias, out_gain, out_bias, w_out):
-    ix, iz, iyh, q = (lax.axis_index(a) for a in ("x", "z", "yh", "ch"))
-    at = jnp.stack([iz, q]).astype(jnp.int32)
-    (send,) = call(spread_kernel, [((64, 8, 128), bf16)], [pair_rep.reshape(32, 128)])
+    ix, iyh, q = (lax.axis_index(a) for a in ("x", "yh", "ch"))
+    send = spread(pair_rep.reshape(32, 128))
     got = lax.all_to_all(send, ("z", "ch"), 0, 0, tiled=True)
 
-    gates = jnp.concatenate([w_gate[0], w_gate[1], jnp.zeros((128, 64), bf16)], axis=1)
+    w_proj = w_proj.transpose(0, 2, 3, 1).reshape(2, 128, 128)
+    w0 = lax.all_gather(w_proj[0], "ch", axis=0)
     small = three(jnp.stack([out_gain, out_bias, pair_bias])).reshape(18, 32)
     packed = jnp.concatenate(
-        [w_proj.reshape(256, 128), gates, w_out.reshape(64, 128), jnp.pad(small, ((0, 14), (0, 96)))], axis=0
-    )
-    packed = lax.all_gather(packed, "ch", axis=0)
-    small = packed[:, 448:466, :32].reshape(4, 3, 6, 32).astype(f32).sum(axis=1)
-    small = small.transpose(0, 2, 1).reshape(128, 6)
-    cols = jnp.concatenate([in_gain.T, in_bias.T, small], axis=1)
+        [
+            w_proj[1],
+            w_gate.transpose(0, 2, 1).reshape(64, 128),
+            w_out.reshape(64, 128),
+            jnp.pad(small, ((0, 14), (0, 96))),
+        ],
+        axis=0,
+    )
+    gains = jnp.concatenate([in_gain.T, in_bias.T], axis=1)
 
     mask = by_plane(residue_mask.astype(f32)).reshape(8, 16)
     chain = by_plane(chain_ids).reshape(8, 16)
@@ -222,27 +246,31 @@
     send, z0, n0 = call(
         first_kernel,
         [((32, 32, 128), bf16), ((128, 512), f32), ((128, 512), bf16)],
-        [got, cols, packed, pm],
+        [got, gains, w0, pm],
         [(1024, 128)],
     )
-    got = lax.all_to_all(send, PLANE, 0, 0, tiled=True)
+    send, packed = lax.optimization_barrier((send, packed))
+    got = lax.all_to_all(send, PLANE, 0, 0, tiled=True)
+    packed = lax.all_gather(packed, "ch", axis=0)
+    cols = packed[:, 256:274, :32].reshape(4, 3, 6, 32).astype(f32).sum(axis=1)
+    cols = cols.transpose(0, 2, 1).reshape(128, 6)
     (gate,) = call(gate_kernel, [((128, 512), f32)], [n0, packed, cols, same])
     (send,) = call(outgoing_kernel, [((32, 16, 128), bf16)], [got])
     got = lax.all_to_all(send, PLANE, 0, 0, tiled=True)
     send, z1, n1 = call(
         middle_kernel,
         [((32, 32, 128), bf16), ((128, 512), bf16), ((128, 512), bf16)],
-        [got, z0, gate, cols, packed, pm],
+        [got, z0, gate, gains, cols, packed, pm],
         [(1024, 128), (512, 128)],
     )
     got = lax.all_to_all(send, PLANE, 0, 0, tiled=True)
-    (zg,) = call(own_kernel, [((128, 128), bf16)], [at, z1, n1, packed, cols, same])
-    (send,) = call(incoming_kernel, [((32, 8, 128), bf16)], [at, got], [(256, 128)])
+    (zg,) = call(own_kernel, [((128, 128), bf16)], [z1, n1, packed, cols, same])
+    (send,) = call(incoming_kernel, [((32, 8, 128), bf16)], [got], [(256, 128)])
     send, zg = lax.optimization_barrier((send, zg))
     got = lax.all_to_all(send, PLANE, 0, 0, tiled=True)
     zg = lax.all_gather(zg, "ch", axis=0)
     (out,) = call(
-        last_kernel, [((32, 128), bf16)], [at, got, zg, packed, cols], [(256, 128), (128, 128)]
+        last_kernel, [((32, 128), bf16)], [got, zg, packed, cols], [(256, 128), (128, 128)]
     )
     return out.reshape(32, 1, 128)
 

time: 97.9 us -> 98.7 us (level)
  blocking collectives: 13.4 us -> 19.9 us
  waiting for transfers between devices: 30.9 us -> 26 us
  starting transfers between devices: 36.8 us -> 38.8 us
  local copies, waits for them, and re-layouts: 5.12 us -> 3.53 us
    all_to_all x4, waiting for transfers between devices: 25.8 us -> 18.3 us  [body(): got = lax.all_to_all(send, PLANE, 0, 0, tiled=True)]
    all_gather x0 -> x1, blocking collectives: none -> 5.87 us  [body(): w0 = lax.all_gather(w_proj[0], 'ch', axis=0)]
    all_to_all x1, waiting for transfers between devices: 5.03 us -> 7.68 us  [body(): got = lax.all_to_all(send, ('z', 'ch'), 0, 0, tiled=True)]
    pallas_call x8 -> x7, Pallas kernels: 10.4 us -> 7.79 us  [call(): pl.pallas_call(kernel, out_shape=[jax.ShapeDtypeStruct(s, d) for s, d in...]
    all_to_all x4, starting transfers between devices: 18.6 us -> 20.6 us  [body(): got = lax.all_to_all(send, PLANE, 0, 0, tiled=True)]
    pallas_call x0 -> x1, Pallas kernels: none -> 1.71 us  [spread(): pl.pallas_call(spread_kernel, out_shape=jax.ShapeDtypeStruct((64, 8, 128)...]
    unnamed x24 -> x20, local copies, waits for them, and re-layouts: 3.72 us -> 2.47 us
  transfers between devices with their start and end apart: 5 -> 5, of which waited for: 5 -> 5; matrix products, arithmetic and copies ran while one was open for 2% -> 1% of each run, Pallas kernels for 1% -> 1%
where the time goes in v5:
time: 98.7 us; the launch traced here: 98.1 us
  starting transfers between devices  38.8 us (39%)
  waiting for transfers between devices  26 us (26%)
  blocking collectives  19.9 us (20%)
  Pallas kernels  9.5 us (10%)
  local copies, waits for them, and re-layouts  3.53 us (4%)
    all_to_all x4, starting transfers between devices, body(): got = lax.all_to_all(send, PLANE, 0, 0, tiled=True)  20.6 us
    all_to_all x4, waiting for transfers between devices, body(): got = lax.all_to_all(send, PLANE, 0, 0, tiled=True)  18.3 us
    all_to_all x1, starting transfers between devices, body(): got = lax.all_to_all(send, ('z', 'ch'), 0, 0, tiled=True)  18.2 us
    all_gather x1, blocking collectives, body(): packed = lax.all_gather(packed, 'ch', axis=0)  8.3 us
    pallas_call x7, Pallas kernels, call(): pl.pallas_call(kernel, out_shape=[jax.ShapeDtypeStruct(s, d) for s, d in...  7.79 us
    all_to_all x1, waiting for transfers between devices, body(): got = lax.all_to_all(send, ('z', 'ch'), 0, 0, tiled=True)  7.68 us
    all_gather x1, blocking collectives, body(): w0 = lax.all_gather(w_proj[0], 'ch', axis=0)  5.87 us
    all_gather x1, blocking collectives, body(): zg = lax.all_gather(zg, 'ch', axis=0)  5.7 us
  transfers between devices with their start and end apart: 5, of which 5 were waited for; matrix products, arithmetic and copies ran while one was open for 1% of the time, Pallas kernels for 1%

profile of v5, /device:TPU:1, one launch (start us, length us, event | category | flops | bytes accessed | tf_op | source)
XLA Modules:
  0.0 98.1 jit_solution(5122160456564425409)
XLA Ops:
  0.0 1.7 %shard_map.109 = bf16[64,8,128]{2,1,0:T(8,128)(2,1)} custom-call(bf16[32,128]{1,0:T(8,128)(2,1)} %bitcast.52), custom_call_target="tpu_custom_call" | custom-call | tf_op jit(solution)/shard_map/pallas_call | solution.py:76
  1.7 18.2 %all-to-all-start = ((bf16[64,8,128]{2,1,0:T(8,128)(2,1)}), bf16[64,8,128]{2,1,0:T(8,128)(2,1)S(1)}, u32[]{:S(2)}, u32[]{:S(2)}) async-start(bf16[64,8,128]{2,1,0:T(8,128)(2,1)} %shard_map.109), calls=%async_computation | async-start | bytes 262144 | tf_op jit(solution)/shard_map/all_to_all | solution.py:220
  19.9 0.6 copy-done.9
  20.6 0.7 copy-done.4
  21.8 0.6 copy-done.8
  22.7 0.3 copy-done.6
  23.4 5.9 %all_gather.15.w_ref = bf16[4,128,128]{2,1,0:T(8,128)(2,1)S(1)} all-gather(bf16[1,128,128]{2,1,0:T(8,128)(2,1)S(1)} %bitcast.42), channel_id=1, replica_groups=mesh['x'=4,'z'=16,'yh'=2,'ch'=4] {'ch'}, dimensions={0}, use_global_device_ids=true | all-gather | bytes 163840 | tf_op jit(solution)/shard_map/all_gather | solution.py:223
  29.3 7.7 %all-to-all-done.got_ref = bf16[64,8,128]{2,1,0:T(8,128)(2,1)S(1)} async-done(((bf16[64,8,128]{2,1,0:T(8,128)(2,1)}), bf16[64,8,128]{2,1,0:T(8,128)(2,1)S(1)}, u32[]{:S(2)}, u32[]{:S(2)}) %all-to-all-start) | async-done | bytes 131104 | tf_op jit(solution)/shard_map/all_to_all | solution.py:220
  37.0 1.9 %shard_map.110 = (bf16[32,32,128]{2,1,0:T(8,128)(2,1)}, f32[128,512]{1,0:T(8,128)S(1)}, bf16[128,512]{1,0:T(8,128)(2,1)S(1)}) custom-call(bf16[64,8,128]{2,1,0:T(8,128)(2,1)S(1)} %all-to-all-done.got_ref, f32[128,4]{1,0:T(8,128)S(1)} %copy.27.gain_ref, bf16[4,128,128]{2,1,0:T(8,128)(2,1)S(1)} %all_gather.15.w_ref, f32[1,512]{1,0:T(1,128)S(1)} %mul.36.pm_ref), custom_call_target="tpu_custom_call" | custom-call | flops 100000000 | bytes 266240 | tf_op jit(solution)/shard_map/pallas_call | solution.py:19
  38.9 7.2 %all-to-all-start.1 = ((bf16[32,32,128]{2,1,0:T(8,128)(2,1)}), bf16[32,32,128]{2,1,0:T(8,128)(2,1)S(1)}, u32[]{:S(2)}, u32[]{:S(2)}) async-start(bf16[32,32,128]{2,1,0:T(8,128)(2,1)} %get-tuple-element.16), calls=%async_computation.1 | async-start | bytes 524288 | tf_op jit(solution)/shard_map/all_to_all | solution.py:253
  46.2 8.3 %all-gather = bf16[1152,128]{1,0:T(8,128)(2,1)S(1)} all-gather(bf16[288,128]{1,0:T(8,128)(2,1)S(1)} %fusion.1), channel_id=2, replica_groups=mesh['x'=4,'z'=16,'yh'=2,'ch'=4] {'ch'}, dimensions={0}, use_global_device_ids=true | all-gather | bytes 368640 | tf_op jit(solution)/shard_map/all_gather | solution.py:254
  54.5 0.6 all-to-all-done.1.got_ref
  55.1 1.0 shard_map.111
  56.0 5.9 %all-to-all-start.2 = ((bf16[32,16,128]{2,1,0:T(8,128)(2,1)}), bf16[32,16,128]{2,1,0:T(8,128)(2,1)S(1)}, u32[]{:S(2)}, u32[]{:S(2)}) async-start(bf16[32,16,128]{2,1,0:T(8,128)(2,1)} %shard_map.111), calls=%async_computation.2 | async-start | bytes 262144 | tf_op jit(solution)/shard_map/all_to_all | solution.py:259
  62.3 7.3 %all-to-all-done.2.got_ref = bf16[32,16,128]{2,1,0:T(8,128)(2,1)S(1)} async-done(((bf16[32,16,128]{2,1,0:T(8,128)(2,1)}), bf16[32,16,128]{2,1,0:T(8,128)(2,1)S(1)}, u32[]{:S(2)}, u32[]{:S(2)}) %all-to-all-start.2) | async-done | bytes 131104 | tf_op jit(solution)/shard_map/all_to_all | solution.py:259
  69.6 2.2 %shard_map.113 = (bf16[32,32,128]{2,1,0:T(8,128)(2,1)}, bf16[128,512]{1,0:T(8,128)(2,1)S(1)}, bf16[128,512]{1,0:T(8,128)(2,1)S(1)}) custom-call(bf16[32,16,128]{2,1,0:T(8,128)(2,1)S(1)} %all-to-all-done.2.got_ref, f32[128,512]{1,0:T(8,128)S(1)} %get-tuple-element.17.z_ref, f32[128,512]{1,0:T(8,128)S(1)} %shard_map.112.gate_ref, f32[128,4]{1,0:T(8,128)S(1)} %copy.27.gain_ref, ...), custom_call_target="tpu_custom_call" | custom-call | flops 100000000 | bytes 957440 | tf_op jit(solution)/shard_map/pallas_call | solution.py:19
  71.8 3.9 %all-to-all-start.3 = ((bf16[32,32,128]{2,1,0:T(8,128)(2,1)}), bf16[32,32,128]{2,1,0:T(8,128)(2,1)S(1)}, u32[]{:S(2)}, u32[]{:S(2)}) async-start(bf16[32,32,128]{2,1,0:T(8,128)(2,1)} %get-tuple-element.20), calls=%async_computation.3 | async-start | bytes 524288 | tf_op jit(solution)/shard_map/all_to_all | solution.py:266
  75.8 0.4 shard_map.115
  76.2 8.7 %all-to-all-done.3.got_ref = bf16[32,32,128]{2,1,0:T(8,128)(2,1)S(1)} async-done(((bf16[32,32,128]{2,1,0:T(8,128)(2,1)}), bf16[32,32,128]{2,1,0:T(8,128)(2,1)S(1)}, u32[]{:S(2)}, u32[]{:S(2)}) %all-to-all-start.3) | async-done | bytes 262176 | tf_op jit(solution)/shard_map/all_to_all | solution.py:266
  84.9 1.1 %shard_map.114 = bf16[32,8,128]{2,1,0:T(8,128)(2,1)} custom-call(bf16[32,32,128]{2,1,0:T(8,128)(2,1)S(1)} %all-to-all-done.3.got_ref), custom_call_target="tpu_custom_call" | custom-call | flops 100000000 | bytes 262144 | tf_op jit(solution)/shard_map/pallas_call | solution.py:19
  86.0 3.7 %all-to-all-start.4 = ((bf16[32,8,128]{2,1,0:T(8,128)(2,1)}), bf16[32,8,128]{2,1,0:T(8,128)(2,1)S(1)}, u32[]{:S(2)}, u32[]{:S(2)}) async-start(bf16[32,8,128]{2,1,0:T(8,128)(2,1)} %shard_map.114), calls=%async_computation.4 | async-start | bytes 131072 | tf_op jit(solution)/shard_map/all_to_all | solution.py:270
  89.6 5.7 %all-gather.1 = bf16[512,128]{1,0:T(8,128)(2,1)S(1)} all-gather(bf16[128,128]{1,0:T(8,128)(2,1)S(1)} %shard_map.115), channel_id=3, replica_groups=mesh['x'=4,'z'=16,'yh'=2,'ch'=4] {'ch'}, dimensions={0}, use_global_device_ids=true | all-gather | bytes 163840 | tf_op jit(solution)/shard_map/all_gather | solution.py:271
  95.3 1.8 %all-to-all-done.4.got_ref = bf16[32,8,128]{2,1,0:T(8,128)(2,1)S(1)} async-done(((bf16[32,8,128]{2,1,0:T(8,128)(2,1)}), bf16[32,8,128]{2,1,0:T(8,128)(2,1)S(1)}, u32[]{:S(2)}, u32[]{:S(2)}) %all-to-all-start.4) | async-done | bytes 65568 | tf_op jit(solution)/shard_map/all_to_all | solution.py:270
  97.1 1.0 shard_map.116
  (44 shorter events, 1.7 us)
Async XLA Ops:
  1.7 35.3 %all-to-all-start = ((bf16[64,8,128]{2,1,0:T(8,128)(2,1)}), bf16[64,8,128]{2,1,0:T(8,128)(2,1)S(1)}, u32[]{:S(2)}, u32[]{:S(2)}) async-start(bf16[64,8,128]{2,1,0:T(8,128)(2,1)} %shard_map.109), calls=%async_computation | async-start | bytes 262144 | tf_op jit(solution)/shard_map/all_to_all | solution.py:220
  19.9 0.7 copy-start.9
  20.6 0.7 copy-start.4
  20.6 0.7 copy-start.5
  20.6 0.7 copy-start.3
  21.7 0.7 copy-start.8
  22.4 0.7 copy-start.6
  22.4 0.7 copy-start.7
  22.5 0.8 copy-start
  23.4 5.9 %copy-start.1 = (bf16[2,32,128]{2,1,0:T(8,128)(2,1)S(1)}, bf16[2,32,128]{2,1,0:T(8,128)(2,1)}, u32[]{:S(2)}) copy-start(bf16[2,32,128]{2,1,0:T(8,128)(2,1)} %param.21) | copy-start | bytes 49156
  23.4 5.9 %copy-start.2 = (bf16[2,128,32]{1,2,0:T(8,128)(2,1)S(1)}, bf16[2,128,32]{1,2,0:T(8,128)(2,1)}, u32[]{:S(2)}) copy-start(bf16[2,128,32]{1,2,0:T(8,128)(2,1)} %param.17) | copy-start | bytes 49156
  38.9 16.2 %all-to-all-start.1 = ((bf16[32,32,128]{2,1,0:T(8,128)(2,1)}), bf16[32,32,128]{2,1,0:T(8,128)(2,1)S(1)}, u32[]{:S(2)}, u32[]{:S(2)}) async-start(bf16[32,32,128]{2,1,0:T(8,128)(2,1)} %get-tuple-element.16), calls=%async_computation.1 | async-start | bytes 524288 | tf_op jit(solution)/shard_map/all_to_all | solution.py:253
  56.0 13.6 %all-to-all-start.2 = ((bf16[32,16,128]{2,1,0:T(8,128)(2,1)}), bf16[32,16,128]{2,1,0:T(8,128)(2,1)S(1)}, u32[]{:S(2)}, u32[]{:S(2)}) async-start(bf16[32,16,128]{2,1,0:T(8,128)(2,1)} %shard_map.111), calls=%async_computation.2 | async-start | bytes 262144 | tf_op jit(solution)/shard_map/all_to_all | solution.py:259
  71.8 13.0 %all-to-all-start.3 = ((bf16[32,32,128]{2,1,0:T(8,128)(2,1)}), bf16[32,32,128]{2,1,0:T(8,128)(2,1)S(1)}, u32[]{:S(2)}, u32[]{:S(2)}) async-start(bf16[32,32,128]{2,1,0:T(8,128)(2,1)} %get-tuple-element.20), calls=%async_computation.3 | async-start | bytes 524288 | tf_op jit(solution)/shard_map/all_to_all | solution.py:266
  86.0 11.2 %all-to-all-start.4 = ((bf16[32,8,128]{2,1,0:T(8,128)(2,1)}), bf16[32,8,128]{2,1,0:T(8,128)(2,1)S(1)}, u32[]{:S(2)}, u32[]{:S(2)}) async-start(bf16[32,8,128]{2,1,0:T(8,128)(2,1)} %shard_map.114), calls=%async_computation.4 | async-start | bytes 131072 | tf_op jit(solution)/shard_map/all_to_all | solution.py:270

commit v6 on v5

v6 whole, which is shorter than its diff:
```python
import jax
import jax.numpy as jnp
from jax import lax
from jax.experimental import pallas as pl
from jax.experimental.pallas import tpu as pltpu
from jax.sharding import Mesh, PartitionSpec as P

epsilon = 1e-05
bf16 = jnp.bfloat16
f32 = jnp.float32
ROW = ("x", "z", "yh")
PLANE = ("x", "yh", "ch")
VMEM = pl.BlockSpec(memory_space=pltpu.VMEM)
HBM = pl.BlockSpec(memory_space=pltpu.HBM)


def call(kernel, outs, ins, scratch=(), flops=100_000_000):
    moved = sum(a.size * a.dtype.itemsize for a in ins)
    return pl.pallas_call(
        kernel,
        out_shape=[jax.ShapeDtypeStruct(s, d) for s, d in outs],
        in_specs=[VMEM] * len(ins),
        out_specs=[VMEM] * len(outs),
        scratch_shapes=[pltpu.VMEM(s, f32) for s in scratch],
        compiler_params=pltpu.CompilerParams(vmem_limit_bytes=32 * 1024 * 1024),
        cost_estimate=pl.CostEstimate(flops=flops, bytes_accessed=moved, transcendentals=0),
    )(*ins)


def tn(a, b):
    return lax.dot_general(a, b, (((0,), (0,)), ((), ())), preferred_element_type=f32)


def nt(a, b):
    return lax.dot_general(a, b, (((1,), (1,)), ((), ())), preferred_element_type=f32)


def sigmoid(v):
    return 0.5 * jnp.tanh(0.5 * v) + 0.5


def norm(v, gain, bias):
    mean = jnp.mean(v, axis=0, keepdims=True)
    var = jnp.mean(v * v, axis=0, keepdims=True) - mean * mean
    return ((v - mean) * lax.rsqrt(var + epsilon) * gain + bias).astype(bf16)


def lanes(pieces):
    return jnp.concatenate(pieces, axis=1)


def permutation():
    k = lax.broadcasted_iota(jnp.int32, (128, 128), 0)
    p = lax.broadcasted_iota(jnp.int32, (128, 128), 1)
    place = (k & 96) | ((k & 1) << 4) | ((k & 31) >> 1)
    return (place == p).astype(f32).astype(bf16)


def spread_kernel(x_ref, out_ref, tile, sems):
    t = jnp.dot(x_ref[...], permutation(), preferred_element_type=f32)
    for q in range(4):
        piece = lanes([t[c * 8 : c * 8 + 8, q * 32 : q * 32 + 32] for c in range(4)])
        tile[q] = piece.astype(bf16)
    copies = [pltpu.make_async_copy(tile, out_ref.at[z * 4 : z * 4 + 4], sems.at[z]) for z in range(16)]
    for c in copies:
        c.start()
    for c in copies:
        c.wait()


def spread(x):
    return pl.pallas_call(
        spread_kernel,
        out_shape=jax.ShapeDtypeStruct((64, 8, 128), bf16),
        in_specs=[VMEM],
        out_specs=HBM,
        scratch_shapes=[pltpu.VMEM((4, 8, 128), bf16), pltpu.SemaphoreType.DMA((16,))],
    )(x)


def project(n, w_ref, u, pm, out_ref):
    sides = ([], [])
    for q in range(4):
        w = w_ref[q, u * 128 : u * 128 + 128, :]
        p = jnp.dot(w, n, preferred_element_type=f32)
        sides[0].append(sigmoid(p[0:32]) * p[32:64] * pm)
        sides[1].append(sigmoid(p[64:96]) * p[96:128] * pm)
    for s in range(2):
        v = jnp.stack([lanes([v[:, z * 32 : z * 32 + 32] for v in sides[s]]) for z in range(16)], axis=0)
        out_ref[:, s * 16 : s * 16 + 16, :] = jnp.swapaxes(v, 0, 1).astype(bf16)


def gates(n, w_ref, u, cols, same):
    w = jnp.concatenate([w_ref[q, 256 + u * 32 : 288 + u * 32, :] for q in range(4)], axis=0)
    return sigmoid(jnp.dot(w, n, preferred_element_type=f32) + cols * same)


def first_kernel(got_ref, gain_ref, cols_ref, w_ref, pm_ref, same_ref, out_ref, z_ref, gate_ref):
    rows = []
    for q in range(4):
        for c in range(4):
            pieces = [got_ref[z * 4 + q].astype(f32)[:, c * 32 : c * 32 + 32] for z in range(16)]
            rows.append(lanes(pieces))
    z0 = jnp.concatenate(rows, axis=0)
    z_ref[...] = z0
    n = norm(z0, gain_ref[:, 0:1], gain_ref[:, 2:3])
    gate_ref[...] = gates(n, w_ref, 0, cols_ref[:, 4:5], same_ref[...])
    project(n, w_ref, 0, pm_ref[...], out_ref)


def outgoing_kernel(got_ref, out_ref):
    row = lax.broadcasted_iota(jnp.int32, (128, 512), 0) >> 5
    lane = (lax.broadcasted_iota(jnp.int32, (128, 512), 1) >> 5) & 3
    same = row == lane
    left, right = [], []
    for q in range(4):
        left.append(jnp.concatenate([got_ref[a * 4 + q, 0:16, :] for a in range(8)], axis=0))
        right.append(jnp.concatenate([got_ref[a * 4 + q, 16:32, :] for a in range(8)], axis=0))
    left, right = lanes(left), lanes(right)
    for q in range(4):
        part = right[q * 32 : q * 32 + 32].astype(f32)
        block = jnp.where(same, jnp.concatenate([part] * 4, axis=0), 0.0).astype(bf16)
        x = nt(left, block).astype(bf16)
        for b in range(8):
            out_ref[b * 4 + q] = x[b * 16 : b * 16 + 16]


def middle_kernel(got_ref, z_ref, gate_ref, gain_ref, cols_ref, w_ref, pm_ref, out_ref, z1_ref, n1_ref):
    x = jnp.swapaxes(got_ref[...].astype(f32), 0, 1)
    x0 = jnp.concatenate(
        [lanes([x[z][:, d * 32 : d * 32 + 32] for z in range(16)]) for d in range(4)], axis=0
    )
    xn = norm(x0, cols_ref[:, 0:1], cols_ref[:, 2:3])
    w = jnp.concatenate([w_ref[q, 320:352, :] for q in range(4)], axis=0)
    z1 = (z_ref[...] + gate_ref[...] * tn(w, xn)).astype(bf16)
    z1_ref[...] = z1
    n1 = norm(z1.astype(f32), gain_ref[:, 1:2], gain_ref[:, 3:4])
    n1_ref[...] = n1
    project(n1, w_ref, 1, pm_ref[...], out_ref)


def incoming_kernel(got_ref, z1_ref, n1_ref, cols_ref, w_ref, same_ref, out_ref):
    here = lax.axis_index("z")
    left, right = [], []
    for q in range(4):
        left.append(jnp.concatenate([got_ref[a * 4 + q, 0:16, :] for a in range(8)], axis=0))
        right.append(jnp.concatenate([got_ref[a * 4 + q, 16:32, :] for a in range(8)], axis=0))
    row = lax.broadcasted_iota(jnp.int32, (32, 512), 0)
    lane = lax.broadcasted_iota(jnp.int32, (32, 512), 1)
    want = (((row >> 1) & 3) << 7) | ((row >> 3) << 5) | ((row & 1) << 4) | here
    pick = (lane == want).astype(f32).astype(bf16)
    mine = nt(pick, lanes(left)).astype(bf16)
    prods = [jnp.dot(mine, r, preferred_element_type=f32) for r in right]
    xs = [lanes([p[d * 8 : d * 8 + 8, d * 32 : d * 32 + 32] for p in prods]) for d in range(4)]
    x = jnp.swapaxes(jnp.stack(xs + xs, axis=0), 0, 1).astype(bf16)
    lane = lax.broadcasted_iota(jnp.int32, (512, 128), 0)
    col = lax.broadcasted_iota(jnp.int32, (512, 128), 1)
    pick = ((lane == here * 32 + col) & (col < 32)).astype(f32).astype(bf16)
    z1 = jnp.dot(z1_ref[...], pick, preferred_element_type=f32)
    n1 = jnp.dot(n1_ref[...], pick, preferred_element_type=f32).astype(bf16)
    same = jnp.dot(
        jnp.broadcast_to(same_ref[...], (8, 512)).astype(bf16), pick, preferred_element_type=f32
    )[0:1]
    gate = gates(n1, w_ref, 1, cols_ref[:, 5:6], same)
    for q in range(4):
        zq, gq = (
            lanes([v[q * 32 + c * 8 : q * 32 + c * 8 + 8, 0:32] for c in range(4)]).astype(bf16)
            for v in (z1, gate)
        )
        for a in range(8):
            out_ref[a * 4 + q, 0:8, :] = x[a]
            out_ref[a * 4 + q, 8:16, :] = zq
            out_ref[a * 4 + q, 16:24, :] = gq


def last_kernel(got_ref, cols_ref, w_ref, out_ref, ys):
    x = jnp.swapaxes(got_ref[:, 0:8, :].astype(f32), 0, 1)
    x1 = jnp.concatenate([x[d] for d in range(4)], axis=0)
    xn = norm(x1, cols_ref[:, 1:2], cols_ref[:, 3:4])
    w = jnp.concatenate([w_ref[q, 352:384, :] for q in range(4)], axis=0)
    ys[...] = tn(w, xn)
    y = ys[pl.ds(pl.multiple_of(lax.axis_index("ch") * 32, 32), 32), :]
    home = (lax.axis_index("x") * 2 + lax.axis_index("yh")) * 4
    own = [got_ref[home + s].astype(f32) for s in range(4)]
    z1, gate = (
        jnp.concatenate(
            [lanes([o[r : r + 8, c * 32 : c * 32 + 32] for o in own]) for c in range(4)], axis=0
        )
        for r in (8, 16)
    )
    out = (z1 + gate * y).astype(bf16)
    out_ref[...] = nt(out, permutation()).astype(bf16)


def three(v):
    hi = lax.reduce_precision(v, 8, 7)
    mid = lax.reduce_precision(v - hi, 8, 7)
    return jnp.stack([hi, mid, v - hi - mid]).astype(bf16)


def by_plane(v):
    return v.reshape(4, 16, 2).swapaxes(1, 2).reshape(128)


def body(pair_rep, residue_mask, chain_ids, in_gain, in_bias, w_proj, w_gate, pair_bias, out_gain, out_bias, w_out):
    ix, iyh, q = (lax.axis_index(a) for a in ("x", "yh", "ch"))
    send = spread(pair_rep.reshape(32, 128))
    got = lax.all_to_all(send, ("z", "ch"), 0, 0, tiled=True)

    w_proj = w_proj.transpose(0, 2, 3, 1).reshape(2, 128, 128)
    small = three(jnp.stack([out_gain, out_bias, pair_bias])).reshape(18, 32)
    packed = jnp.concatenate(
        [
            w_proj.reshape(256, 128),
            w_gate.transpose(0, 2, 1).reshape(64, 128),
            w_out.reshape(64, 128),
            jnp.pad(small, ((0, 14), (0, 96))),
        ],
        axis=0,
    )
    packed = lax.all_gather(packed, "ch", axis=0)
    cols = packed[:, 384:402, :32].reshape(4, 3, 6, 32).astype(f32).sum(axis=1)
    cols = cols.transpose(0, 2, 1).reshape(128, 6)
    gains = jnp.concatenate([in_gain.T, in_bias.T], axis=1)

    mask = by_plane(residue_mask.astype(f32)).reshape(8, 16)
    chain = by_plane(chain_ids).reshape(8, 16)
    mine = ix * 2 + iyh
    mask_r = lax.dynamic_index_in_dim(mask, mine, 0, keepdims=False)
    chain_r = lax.dynamic_index_in_dim(chain, mine, 0, keepdims=False)
    mask_c = lax.dynamic_index_in_dim(mask.reshape(4, 32), q, 0, keepdims=False)
    chain_c = lax.dynamic_index_in_dim(chain.reshape(4, 32), q, 0, keepdims=False)
    pm = (mask_r[:, None] * mask_c[None, :]).reshape(1, 512)
    same = (chain_r[:, None] == chain_c[None, :]).astype(f32).reshape(1, 512)

    got, packed, cols, gains, pm, same = lax.optimization_barrier((got, packed, cols, gains, pm, same))
    send, z0, gate = call(
        first_kernel,
        [((32, 32, 128), bf16), ((128, 512), f32), ((128, 512), f32)],
        [got, gains, cols, packed, pm, same],
    )
    got = lax.all_to_all(send, PLANE, 0, 0, tiled=True)
    (send,) = call(outgoing_kernel, [((32, 16, 128), bf16)], [got])
    got = lax.all_to_all(send, PLANE, 0, 0, tiled=True)
    send, z1, n1 = call(
        middle_kernel,
        [((32, 32, 128), bf16), ((128, 512), bf16), ((128, 512), bf16)],
        [got, z0, gate, gains, cols, packed, pm],
    )
    got = lax.all_to_all(send, PLANE, 0, 0, tiled=True)
    (send,) = call(incoming_kernel, [((32, 24, 128), bf16)], [got, z1, n1, cols, packed, same])
    got = lax.all_to_all(send, PLANE, 0, 0, tiled=True)
    (out,) = call(last_kernel, [((32, 128), bf16)], [got, cols, packed], [(128, 128)])
    return out.reshape(32, 1, 128)


def solution(mesh):
    fine = Mesh(mesh.devices.reshape(4, 16, 2, 4), ("x", "z", "yh", "ch"))
    return jax.shard_map(
        body,
        mesh=fine,
        in_specs=(
            P("ch", ROW, None),
            P(),
            P(),
            P(),
            P(),
            P(None, None, None, "ch"),
            P(None, None, "ch"),
            P(None, "ch"),
            P(None, "ch"),
            P(None, "ch"),
            P(None, "ch", None),
        ),
        out_specs=P("ch", ROW, None),
        check_vma=False,
    )
```

time: 98.7 us -> 93.4 us (0.946)
  blocking collectives: 19.9 us -> 58.9 us
  starting transfers between devices: 38.8 us -> 18.2 us
  waiting for transfers between devices: 26 us -> 5.43 us
  Pallas kernels: 9.5 us -> 5.87 us
    all_to_all x0 -> x4, blocking collectives: none -> 51.5 us  [body(): got = lax.all_to_all(send, PLANE, 0, 0, tiled=True)]
    all_to_all x4 -> x0, starting transfers between devices: 20.6 us -> none  [body(): got = lax.all_to_all(send, PLANE, 0, 0, tiled=True)]
    all_to_all x4 -> x0, waiting for transfers between devices: 18.3 us -> none  [body(): got = lax.all_to_all(send, PLANE, 0, 0, tiled=True)]
    all_gather x2 -> x0, blocking collectives: 11.6 us -> none  [the longest x1 5.87 us: body(): w0 = lax.all_gather(w_proj[0], 'ch', axis=0)]
    pallas_call x7 -> x5, Pallas kernels: 7.79 us -> 4.15 us  [call(): pl.pallas_call(kernel, out_shape=[jax.ShapeDtypeStruct(s, d) for s, d in...]
    all_to_all x1, waiting for transfers between devices: 7.68 us -> 5.43 us  [body(): got = lax.all_to_all(send, ('z', 'ch'), 0, 0, tiled=True)]
  transfers between devices with their start and end apart: 5 -> 1, of which waited for: 5 -> 1; matrix products, arithmetic and copies ran while one was open for 1% -> 1% of each run, Pallas kernels for 1% -> 0%
where the time goes in v6:
time: 93.4 us; the launch traced here: 92.8 us
  blocking collectives  58.9 us (63%)
  starting transfers between devices  18.2 us (19%)
  Pallas kernels  5.87 us (6%)
  waiting for transfers between devices  5.43 us (6%)
  local copies, waits for them, and re-layouts  4.1 us (4%)
    all_to_all x4, blocking collectives, body(): got = lax.all_to_all(send, PLANE, 0, 0, tiled=True)  51.5 us
    all_to_all x1, starting transfers between devices, body(): got = lax.all_to_all(send, ('z', 'ch'), 0, 0, tiled=True)  18.2 us
    all_gather x1, blocking collectives, body(): packed = lax.all_gather(packed, 'ch', axis=0)  7.35 us
    all_to_all x1, waiting for transfers between devices, body(): got = lax.all_to_all(send, ('z', 'ch'), 0, 0, tiled=True)  5.43 us
    pallas_call x5, Pallas kernels, call(): pl.pallas_call(kernel, out_shape=[jax.ShapeDtypeStruct(s, d) for s, d in...  4.15 us
    unnamed x20, local copies, waits for them, and re-layouts  3.05 us
  transfers between devices with their start and end apart: 1, of which 1 were waited for; matrix products, arithmetic and copies ran while one was open for 1% of the time, Pallas kernels for 0%

profile of v6, /device:TPU:1, one launch (start us, length us, event | category | flops | bytes accessed | tf_op | source)
XLA Modules:
  0.0 92.8 jit_solution(16676279849302409610)
XLA Ops:
  0.0 1.7 %shard_map.109 = bf16[64,8,128]{2,1,0:T(8,128)(2,1)} custom-call(bf16[32,128]{1,0:T(8,128)(2,1)} %bitcast.48), custom_call_target="tpu_custom_call" | custom-call | tf_op jit(solution)/shard_map/pallas_call | solution.py:72
  1.7 18.2 %all-to-all-start = ((bf16[64,8,128]{2,1,0:T(8,128)(2,1)}), bf16[64,8,128]{2,1,0:T(8,128)(2,1)S(1)}, u32[]{:S(2)}, u32[]{:S(2)}) async-start(bf16[64,8,128]{2,1,0:T(8,128)(2,1)} %shard_map.109), calls=%async_computation | async-start | bytes 262144 | tf_op jit(solution)/shard_map/all_to_all | solution.py:208
  19.9 0.6 copy-done.9
  20.6 0.7 copy-done.4
  21.3 0.1 reshape.242
  21.5 0.1 copy.27
  21.7 0.5 copy-done.8
  22.1 0.1 reshape.243
  22.7 0.5 copy-done.2
  23.4 7.3 %all-gather = bf16[1664,128]{1,0:T(8,128)(2,1)S(1)} all-gather(bf16[416,128]{1,0:T(8,128)(2,1)S(1)} %fusion.1), channel_id=2, replica_groups=mesh['x'=4,'z'=16,'yh'=2,'ch'=4] {'ch'}, dimensions={0}, use_global_device_ids=true | all-gather | bytes 532480 | tf_op jit(solution)/shard_map/all_gather | solution.py:221
  30.8 0.1 copy.26
  30.9 0.6 copy-done.7
  31.5 0.1 copy-done.6
  31.6 5.4 %all-to-all-done.got_ref = bf16[64,8,128]{2,1,0:T(8,128)(2,1)S(1)} async-done(((bf16[64,8,128]{2,1,0:T(8,128)(2,1)}), bf16[64,8,128]{2,1,0:T(8,128)(2,1)S(1)}, u32[]{:S(2)}, u32[]{:S(2)}) %all-to-all-start) | async-done | bytes 131104 | tf_op jit(solution)/shard_map/all_to_all | solution.py:208
  37.0 0.1 copy.31.gain_ref
  37.1 1.0 %shard_map.110 = (bf16[32,32,128]{2,1,0:T(8,128)(2,1)S(1)}, f32[128,512]{1,0:T(8,128)S(1)}, f32[128,512]{1,0:T(8,128)S(1)}) custom-call(bf16[64,8,128]{2,1,0:T(8,128)(2,1)S(1)} %all-to-all-done.got_ref, f32[128,4]{1,0:T(8,128)S(1)} %copy.31.gain_ref, f32[128,6]{1,0:T(8,128)S(1)} %bitcast.35, bf16[4,416,128]{2,1,0:T(8,128)(2,1)S(1)} %bitcast.31, ...), custom_call_target="tpu_custom_call" | custom-call | flops 100000000 | bytes 566272 | tf_op jit(solution)/shard_map/pallas_call | solution.py:19
  38.1 16.0 %all_to_all.25.got_ref = bf16[32,32,128]{2,1,0:T(8,128)(2,1)S(1)} all-to-all(bf16[32,32,128]{2,1,0:T(8,128)(2,1)S(1)} %get-tuple-element.23), channel_id=1, replica_groups=mesh['x'=4,'z'=16,'yh'=2,'ch'=4] {'x','yh','ch'}, dimensions={0} | all-to-all | bytes 524288 | tf_op jit(solution)/shard_map/all_to_all | solution.py:242
  54.1 0.3 shard_map.111
  54.4 11.2 %all_to_all.26.got_ref = bf16[32,16,128]{2,1,0:T(8,128)(2,1)S(1)} all-to-all(bf16[32,16,128]{2,1,0:T(8,128)(2,1)S(1)} %shard_map.111), channel_id=1, replica_groups=mesh['x'=4,'z'=16,'yh'=2,'ch'=4] {'x','yh','ch'}, dimensions={0} | all-to-all | bytes 262144 | tf_op jit(solution)/shard_map/all_to_all | solution.py:244
  65.5 1.3 %shard_map.112 = (bf16[32,32,128]{2,1,0:T(8,128)(2,1)S(1)}, bf16[128,512]{1,0:T(8,128)(2,1)S(1)}, bf16[128,512]{1,0:T(8,128)(2,1)S(1)}) custom-call(bf16[32,16,128]{2,1,0:T(8,128)(2,1)S(1)} %all_to_all.26.got_ref, f32[128,512]{1,0:T(8,128)S(1)} %get-tuple-element.24.z_ref, f32[128,512]{1,0:T(8,128)S(1)} %get-tuple-element.25.gate_ref, ...), custom_call_target="tpu_custom_call" | custom-call | flops 100000000 | bytes 1088512 | tf_op jit(solution)/shard_map/pallas_call | solution.py:19
  66.8 12.6 %all_to_all.27.got_ref = bf16[32,32,128]{2,1,0:T(8,128)(2,1)S(1)} all-to-all(bf16[32,32,128]{2,1,0:T(8,128)(2,1)S(1)} %get-tuple-element.26), channel_id=1, replica_groups=mesh['x'=4,'z'=16,'yh'=2,'ch'=4] {'x','yh','ch'}, dimensions={0} | all-to-all | bytes 524288 | tf_op jit(solution)/shard_map/all_to_all | solution.py:250
  79.4 0.7 shard_map.113
  80.0 11.8 %all_to_all.28.got_ref = bf16[32,24,128]{2,1,0:T(8,128)(2,1)S(1)} all-to-all(bf16[32,24,128]{2,1,0:T(8,128)(2,1)S(1)} %shard_map.113), channel_id=1, replica_groups=mesh['x'=4,'z'=16,'yh'=2,'ch'=4] {'x','yh','ch'}, dimensions={0} | all-to-all | bytes 393216 | tf_op jit(solution)/shard_map/all_to_all | solution.py:252
  91.9 1.0 %shard_map.114 = bf16[32,128]{1,0:T(8,128)(2,1)} custom-call(bf16[32,24,128]{2,1,0:T(8,128)(2,1)S(1)} %all_to_all.28.got_ref, f32[128,6]{1,0:T(8,128)S(1)} %bitcast.38, bf16[4,416,128]{2,1,0:T(8,128)(2,1)S(1)} %bitcast.34), custom_call_target="tpu_custom_call" | custom-call | flops 100000000 | bytes 625664 | tf_op jit(solution)/shard_map/pallas_call | solution.py:19
  (35 shorter events, 0.8 us)
Async XLA Ops:
  1.7 35.3 %all-to-all-start = ((bf16[64,8,128]{2,1,0:T(8,128)(2,1)}), bf16[64,8,128]{2,1,0:T(8,128)(2,1)S(1)}, u32[]{:S(2)}, u32[]{:S(2)}) async-start(bf16[64,8,128]{2,1,0:T(8,128)(2,1)} %shard_map.109), calls=%async_computation | async-start | bytes 262144 | tf_op jit(solution)/shard_map/all_to_all | solution.py:208
  19.9 0.7 copy-start.9
  20.6 0.7 copy-start.4
  20.6 0.7 copy-start.5
  20.6 0.7 copy-start.3
  21.5 0.7 copy-start.8
  21.6 1.1 %copy-start = (bf16[2,128,4,32]{1,3,2,0:T(8,128)(2,1)S(1)}, bf16[2,128,4,32]{1,3,2,0:T(8,128)(2,1)}, u32[]{:S(2)}) copy-start(bf16[2,128,4,32]{1,3,2,0:T(8,128)(2,1)} %param.16) | copy-start | bytes 196612
  22.5 0.7 copy-start.2
  22.5 0.7 copy-start.1
  30.8 0.7 copy-start.7
  30.9 0.7 copy-start.6

commit v7 on v6

--- a/solution.py
+++ b/solution.py
@@ -75,7 +75,80 @@
         in_specs=[VMEM],
         out_specs=HBM,
         scratch_shapes=[pltpu.VMEM((4, 8, 128), bf16), pltpu.SemaphoreType.DMA((16,))],
+        compiler_params=pltpu.CompilerParams(vmem_limit_bytes=32 * 1024 * 1024),
     )(x)
+
+
+def prepare_kernel(
+    mask_ref, chain_ref, gain_ref, bias_ref, pb_ref, og_ref, ob_ref, wp_ref, wg_ref, wo_ref,
+    packed_ref, gains_ref, pm_ref, same_ref, marks, inner, outer, sems,
+):
+    places = [
+        (wp_ref, packed_ref.at[0:256]),
+        (wg_ref, packed_ref.at[256:320]),
+        (wo_ref, packed_ref.at[320:384]),
+        (mask_ref, marks.at[0:1]),
+        (chain_ref, marks.at[1:2]),
+        (gain_ref, inner.at[0:2]),
+        (bias_ref, inner.at[2:4]),
+        (og_ref, outer.at[0]),
+        (ob_ref, outer.at[1]),
+        (pb_ref, outer.at[2]),
+    ]
+    copies = [pltpu.make_async_copy(a, b, sems.at[i]) for i, (a, b) in enumerate(places)]
+    for c in copies[3:] + copies[:3]:
+        c.start()
+    ix, iyh, q = (lax.axis_index(a) for a in ("x", "yh", "ch"))
+    place = lax.broadcasted_iota(jnp.int32, (128, 512), 0)
+    pair = lax.broadcasted_iota(jnp.int32, (128, 512), 1)
+    rows = place == (ix * 32 + iyh) + ((pair >> 5) << 1)
+    columns = place == q * 32 + (((pair & 15) << 1) | ((pair >> 4) & 1))
+    rows, columns = (v.astype(f32).astype(bf16) for v in (rows, columns))
+    for c in copies[3:]:
+        c.wait()
+    m = marks[0:2, :].astype(f32)
+    m = jnp.concatenate([m, jnp.zeros((6, 128), f32)], axis=0).astype(bf16)
+    r = jnp.dot(m, rows, preferred_element_type=f32)
+    c = jnp.dot(m, columns, preferred_element_type=f32)
+    pm_ref[...] = r[0:1] * c[0:1]
+    same_ref[...] = (r[1:2] == c[1:2]).astype(f32)
+    g = jnp.concatenate([inner[0:4, :], jnp.zeros((124, 128), f32)], axis=0)
+    gains_ref[...] = g.T[:, 0:8]
+    v = jnp.concatenate([outer[i] for i in range(3)], axis=0)
+    hi = v.astype(bf16).astype(f32)
+    mid = (v - hi).astype(bf16).astype(f32)
+    low = v - hi - mid
+    v = jnp.concatenate([hi, mid, low, jnp.zeros((110, 32), f32)], axis=0)
+    v = lanes([v, jnp.zeros((128, 96), f32)])
+    packed_ref[384:416, :] = v.T[0:32].astype(bf16)
+    for c in copies[:3]:
+        c.wait()
+
+
+def prepare(*args):
+    return pl.pallas_call(
+        prepare_kernel,
+        out_shape=[
+            jax.ShapeDtypeStruct((416, 128), bf16),
+            jax.ShapeDtypeStruct((128, 8), f32),
+            jax.ShapeDtypeStruct((1, 512), f32),
+            jax.ShapeDtypeStruct((1, 512), f32),
+        ],
+        in_specs=[HBM] * 10,
+        out_specs=[VMEM] * 4,
+        scratch_shapes=[
+            pltpu.VMEM((2, 128), jnp.int32),
+            pltpu.VMEM((4, 128), f32),
+            pltpu.VMEM((3, 2, 32), f32),
+            pltpu.SemaphoreType.DMA((10,)),
+        ],
+        compiler_params=pltpu.CompilerParams(vmem_limit_bytes=32 * 1024 * 1024),
+    )(*args)
+
+
+def columns_of(w_ref):
+    v = jnp.concatenate([w_ref[q, 384:416, :].astype(f32) for q in range(4)], axis=0)
+    return v[:, 0:6] + v[:, 6:12] + v[:, 12:18]
 
 
 def project(n, w_ref, u, pm, out_ref):
@@ -95,7 +168,7 @@
     return sigmoid(jnp.dot(w, n, preferred_element_type=f32) + cols * same)
 
 
-def first_kernel(got_ref, gain_ref, cols_ref, w_ref, pm_ref, same_ref, out_ref, z_ref, gate_ref):
+def first_kernel(got_ref, gain_ref, w_ref, pm_ref, same_ref, out_ref, z_ref, gate_ref):
     rows = []
     for q in range(4):
         for c in range(4):
@@ -104,7 +177,7 @@
     z0 = jnp.concatenate(rows, axis=0)
     z_ref[...] = z0
     n = norm(z0, gain_ref[:, 0:1], gain_ref[:, 2:3])
-    gate_ref[...] = gates(n, w_ref, 0, cols_ref[:, 4:5], same_ref[...])
+    gate_ref[...] = gates(n, w_ref, 0, columns_of(w_ref)[:, 4:5], same_ref[...])
     project(n, w_ref, 0, pm_ref[...], out_ref)
 
 
@@ -125,12 +198,13 @@
             out_ref[b * 4 + q] = x[b * 16 : b * 16 + 16]
 
 
-def middle_kernel(got_ref, z_ref, gate_ref, gain_ref, cols_ref, w_ref, pm_ref, out_ref, z1_ref, n1_ref):
+def middle_kernel(got_ref, z_ref, gate_ref, gain_ref, w_ref, pm_ref, out_ref, z1_ref, n1_ref):
     x = jnp.swapaxes(got_ref[...].astype(f32), 0, 1)
     x0 = jnp.concatenate(
         [lanes([x[z][:, d * 32 : d * 32 + 32] for z in range(16)]) for d in range(4)], axis=0
     )
-    xn = norm(x0, cols_ref[:, 0:1], cols_ref[:, 2:3])
+    cols = columns_of(w_ref)
+    xn = norm(x0, cols[:, 0:1], cols[:, 2:3])
     w = jnp.concatenate([w_ref[q, 320:352, :] for q in range(4)], axis=0)
     z1 = (z_ref[...] + gate_ref[...] * tn(w, xn)).astype(bf16)
     z1_ref[...] = z1
@@ -139,7 +213,7 @@
     project(n1, w_ref, 1, pm_ref[...], out_ref)
 
 
-def incoming_kernel(got_ref, z1_ref, n1_ref, cols_ref, w_ref, same_ref, out_ref):
+def incoming_kernel(got_ref, z1_ref, n1_ref, w_ref, same_ref, out_ref):
     here = lax.axis_index("z")
     left, right = [], []
     for q in range(4):
@@ -161,7 +235,7 @@
     same = jnp.dot(
         jnp.broadcast_to(same_ref[...], (8, 512)).astype(bf16), pick, preferred_element_type=f32
     )[0:1]
-    gate = gates(n1, w_ref, 1, cols_ref[:, 5:6], same)
+    gate = gates(n1, w_ref, 1, columns_of(w_ref)[:, 5:6], same)
     for q in range(4):
         zq, gq = (
             lanes([v[q * 32 + c * 8 : q * 32 + c * 8 + 8, 0:32] for c in range(4)]).astype(bf16)
@@ -173,10 +247,11 @@
             out_ref[a * 4 + q, 16:24, :] = gq
 
 
-def last_kernel(got_ref, cols_ref, w_ref, out_ref, ys):
+def last_kernel(got_ref, w_ref, out_ref, ys):
     x = jnp.swapaxes(got_ref[:, 0:8, :].astype(f32), 0, 1)
     x1 = jnp.concatenate([x[d] for d in range(4)], axis=0)
-    xn = norm(x1, cols_ref[:, 1:2], cols_ref[:, 3:4])
+    cols = columns_of(w_ref)
+    xn = norm(x1, cols[:, 1:2], cols[:, 3:4])
     w = jnp.concatenate([w_ref[q, 352:384, :] for q in range(4)], axis=0)
     ys[...] = tn(w, xn)
     y = ys[pl.ds(pl.multiple_of(lax.axis_index("ch") * 32, 32), 32), :]
@@ -192,52 +267,29 @@
     out_ref[...] = nt(out, permutation()).astype(bf16)
 
 
-def three(v):
-    hi = lax.reduce_precision(v, 8, 7)
-    mid = lax.reduce_precision(v - hi, 8, 7)
-    return jnp.stack([hi, mid, v - hi - mid]).astype(bf16)
-
-
-def by_plane(v):
-    return v.reshape(4, 16, 2).swapaxes(1, 2).reshape(128)
-
-
 def body(pair_rep, residue_mask, chain_ids, in_gain, in_bias, w_proj, w_gate, pair_bias, out_gain, out_bias, w_out):
-    ix, iyh, q = (lax.axis_index(a) for a in ("x", "yh", "ch"))
     send = spread(pair_rep.reshape(32, 128))
+    args = (
+        residue_mask.reshape(1, 128),
+        chain_ids.reshape(1, 128),
+        in_gain,
+        in_bias,
+        pair_bias,
+        out_gain,
+        out_bias,
+        w_proj.transpose(0, 2, 3, 1).reshape(256, 128),
+        w_gate.transpose(0, 2, 1).reshape(64, 128),
+        w_out.reshape(64, 128),
+    )
+    send, *args = lax.optimization_barrier((send, *args))
     got = lax.all_to_all(send, ("z", "ch"), 0, 0, tiled=True)
-
-    w_proj = w_proj.transpose(0, 2, 3, 1).reshape(2, 128, 128)
-    small = three(jnp.stack([out_gain, out_bias, pair_bias])).reshape(18, 32)
-    packed = jnp.concatenate(
-        [
-            w_proj.reshape(256, 128),
-            w_gate.transpose(0, 2, 1).reshape(64, 128),
-            w_out.reshape(64, 128),
-            jnp.pad(small, ((0, 14), (0, 96))),
-        ],
-        axis=0,
-    )
+    packed, gains, pm, same = prepare(*args)
     packed = lax.all_gather(packed, "ch", axis=0)
-    cols = packed[:, 384:402, :32].reshape(4, 3, 6, 32).astype(f32).sum(axis=1)
-    cols = cols.transpose(0, 2, 1).reshape(128, 6)
-    gains = jnp.concatenate([in_gain.T, in_bias.T], axis=1)
-
-    mask = by_plane(residue_mask.astype(f32)).reshape(8, 16)
-    chain = by_plane(chain_ids).reshape(8, 16)
-    mine = ix * 2 + iyh
-    mask_r = lax.dynamic_index_in_dim(mask, mine, 0, keepdims=False)
-    chain_r = lax.dynamic_index_in_dim(chain, mine, 0, keepdims=False)
-    mask_c = lax.dynamic_index_in_dim(mask.reshape(4, 32), q, 0, keepdims=False)
-    chain_c = lax.dynamic_index_in_dim(chain.reshape(4, 32), q, 0, keepdims=False)
-    pm = (mask_r[:, None] * mask_c[None, :]).reshape(1, 512)
-    same = (chain_r[:, None] == chain_c[None, :]).astype(f32).reshape(1, 512)
-
-    got, packed, cols, gains, pm, same = lax.optimization_barrier((got, packed, cols, gains, pm, same))
+    got, packed, gains, pm, same = lax.optimization_barrier((got, packed, gains, pm, same))
     send, z0, gate = call(
         first_kernel,
         [((32, 32, 128), bf16), ((128, 512), f32), ((128, 512), f32)],
-        [got, gains, cols, packed, pm, same],
+        [got, gains, packed, pm, same],
     )
     got = lax.all_to_all(send, PLANE, 0, 0, tiled=True)
     (send,) = call(outgoing_kernel, [((32, 16, 128), bf16)], [got])
@@ -245,12 +297,12 @@
     send, z1, n1 = call(
         middle_kernel,
         [((32, 32, 128), bf16), ((128, 512), bf16), ((128, 512), bf16)],
-        [got, z0, gate, gains, cols, packed, pm],
+        [got, z0, gate, gains, packed, pm],
     )
     got = lax.all_to_all(send, PLANE, 0, 0, tiled=True)
-    (send,) = call(incoming_kernel, [((32, 24, 128), bf16)], [got, z1, n1, cols, packed, same])
+    (send,) = call(incoming_kernel, [((32, 24, 128), bf16)], [got, z1, n1, packed, same])
     got = lax.all_to_all(send, PLANE, 0, 0, tiled=True)
-    (out,) = call(last_kernel, [((32, 128), bf16)], [got, cols, packed], [(128, 128)])
+    (out,) = call(last_kernel, [((32, 128), bf16)], [got, packed], [(128, 128)])
     return out.reshape(32, 1, 128)
 
 

time: 93.4 us -> 93.5 us (level)
  waiting for transfers between devices: 5.43 us -> 9.17 us
  local copies, waits for them, and re-layouts: 4.1 us -> 0.76 us
    all_to_all x1, waiting for transfers between devices: 5.43 us -> 9.17 us  [body(): got = lax.all_to_all(send, ('z', 'ch'), 0, 0, tiled=True)]
    unnamed x20 -> x22, local copies, waits for them, and re-layouts: 3.05 us -> 0.76 us
  transfers between devices with their start and end apart: 1 -> 1, of which waited for: 1 -> 1; matrix products, arithmetic and copies ran while one was open for 1% -> 0% of each run, Pallas kernels for 0% -> 0%
where the time goes in v7:
time: 93.5 us; the launch traced here: 93.1 us
  blocking collectives  58.9 us (63%)
  starting transfers between devices  18.3 us (20%)
  waiting for transfers between devices  9.17 us (10%)
  Pallas kernels  5.77 us (6%)
    all_to_all x4, blocking collectives, body(): got = lax.all_to_all(send, PLANE, 0, 0, tiled=True)  51.5 us
    all_to_all x1, starting transfers between devices, body(): got = lax.all_to_all(send, ('z', 'ch'), 0, 0, tiled=True)  18.3 us
    all_to_all x1, waiting for transfers between devices, body(): got = lax.all_to_all(send, ('z', 'ch'), 0, 0, tiled=True)  9.17 us
    all_gather x1, blocking collectives, body(): packed = lax.all_gather(packed, 'ch', axis=0)  7.36 us
    pallas_call x5, Pallas kernels, call(): pl.pallas_call(kernel, out_shape=[jax.ShapeDtypeStruct(s, d) for s, d in...  4.28 us
  transfers between devices with their start and end apart: 1, of which 1 were waited for; matrix products, arithmetic and copies ran while one was open for 0% of the time, Pallas kernels for 0%

profile of v7, /device:TPU:1, one launch (start us, length us, event | category | flops | bytes accessed | tf_op | source)
XLA Modules:
  0.0 93.1 jit_solution(8680065396619931836)
XLA Ops:
  0.0 0.7 copy-done.3
  0.7 1.0 %shard_map.109 = bf16[64,8,128]{2,1,0:T(8,128)(2,1)} custom-call(bf16[32,128]{1,0:T(8,128)(2,1)S(1)} %bitcast.19), custom_call_target="tpu_custom_call" | custom-call | tf_op jit(solution)/shard_map/pallas_call | solution.py:72
  1.7 0.0 copy-start
  1.7 0.0 copy-start.1
  1.8 0.0 copy-start.2
  1.8 0.0 copy-start.4
  1.8 0.0 copy-start.5
  1.8 0.0 copy-start.6
  1.8 0.0 copy-start.7
  1.8 0.0 copy-start.8
  1.8 0.0 copy-start.9
  1.9 18.3 %all-to-all-start = ((bf16[64,8,128]{2,1,0:T(8,128)(2,1)}), bf16[64,8,128]{2,1,0:T(8,128)(2,1)S(1)}, u32[]{:S(2)}, u32[]{:S(2)}) async-start(bf16[64,8,128]{2,1,0:T(8,128)(2,1)} %shard_map.109), calls=%async_computation | async-start | bytes 262144 | tf_op jit(solution)/shard_map/all_to_all | solution.py:285
  20.3 0.5 shard_map.110
  20.7 7.4 %all-gather = bf16[1664,128]{1,0:T(8,128)(2,1)S(1)} all-gather(bf16[416,128]{1,0:T(8,128)(2,1)S(1)} %get-tuple-element.42), channel_id=2, replica_groups=mesh['x'=4,'z'=16,'yh'=2,'ch'=4] {'ch'}, dimensions={0}, use_global_device_ids=true | all-gather | bytes 532480 | tf_op jit(solution)/shard_map/all_gather | solution.py:287
  28.1 9.2 %all-to-all-done.got_ref = bf16[64,8,128]{2,1,0:T(8,128)(2,1)S(1)} async-done(((bf16[64,8,128]{2,1,0:T(8,128)(2,1)}), bf16[64,8,128]{2,1,0:T(8,128)(2,1)S(1)}, u32[]{:S(2)}, u32[]{:S(2)}) %all-to-all-start) | async-done | bytes 131104 | tf_op jit(solution)/shard_map/all_to_all | solution.py:285
  37.3 0.9 %shard_map.111 = (bf16[32,32,128]{2,1,0:T(8,128)(2,1)S(1)}, f32[128,512]{1,0:T(8,128)S(1)}, f32[128,512]{1,0:T(8,128)S(1)}) custom-call(bf16[64,8,128]{2,1,0:T(8,128)(2,1)S(1)} %all-to-all-done.got_ref, f32[128,8]{1,0:T(8,128)S(1)} %get-tuple-element.47.gain_ref, bf16[4,416,128]{2,1,0:T(8,128)(2,1)S(1)} %bitcast.12, f32[1,512]{1,0:T(1,128)S(1)} %get-tuple-element.49.pm_ref, ...), custom_call_target="tpu_custom_call" | custom-call | flops 100000000 | bytes 565248 | tf_op jit(solution)/shard_map/pallas_call | solution.py:19
  38.2 16.0 %all_to_all.25.got_ref = bf16[32,32,128]{2,1,0:T(8,128)(2,1)S(1)} all-to-all(bf16[32,32,128]{2,1,0:T(8,128)(2,1)S(1)} %get-tuple-element.51), channel_id=1, replica_groups=mesh['x'=4,'z'=16,'yh'=2,'ch'=4] {'x','yh','ch'}, dimensions={0} | all-to-all | bytes 524288 | tf_op jit(solution)/shard_map/all_to_all | solution.py:294
  54.2 0.3 shard_map.112
  54.5 11.2 %all_to_all.26.got_ref = bf16[32,16,128]{2,1,0:T(8,128)(2,1)S(1)} all-to-all(bf16[32,16,128]{2,1,0:T(8,128)(2,1)S(1)} %shard_map.112), channel_id=1, replica_groups=mesh['x'=4,'z'=16,'yh'=2,'ch'=4] {'x','yh','ch'}, dimensions={0} | all-to-all | bytes 262144 | tf_op jit(solution)/shard_map/all_to_all | solution.py:296
  65.7 1.3 %shard_map.113 = (bf16[32,32,128]{2,1,0:T(8,128)(2,1)S(1)}, bf16[128,512]{1,0:T(8,128)(2,1)S(1)}, bf16[128,512]{1,0:T(8,128)(2,1)S(1)}) custom-call(bf16[32,16,128]{2,1,0:T(8,128)(2,1)S(1)} %all_to_all.26.got_ref, f32[128,512]{1,0:T(8,128)S(1)} %get-tuple-element.52.z_ref, f32[128,512]{1,0:T(8,128)S(1)} %get-tuple-element.53.gate_ref, ...), custom_call_target="tpu_custom_call" | custom-call | flops 100000000 | bytes 1087488 | tf_op jit(solution)/shard_map/pallas_call | solution.py:19
  67.0 12.6 %all_to_all.27.got_ref = bf16[32,32,128]{2,1,0:T(8,128)(2,1)S(1)} all-to-all(bf16[32,32,128]{2,1,0:T(8,128)(2,1)S(1)} %get-tuple-element.54), channel_id=1, replica_groups=mesh['x'=4,'z'=16,'yh'=2,'ch'=4] {'x','yh','ch'}, dimensions={0} | all-to-all | bytes 524288 | tf_op jit(solution)/shard_map/all_to_all | solution.py:302
  79.6 0.7 shard_map.114
  80.3 11.8 %all_to_all.28.got_ref = bf16[32,24,128]{2,1,0:T(8,128)(2,1)S(1)} all-to-all(bf16[32,24,128]{2,1,0:T(8,128)(2,1)S(1)} %shard_map.114), channel_id=1, replica_groups=mesh['x'=4,'z'=16,'yh'=2,'ch'=4] {'x','yh','ch'}, dimensions={0} | all-to-all | bytes 393216 | tf_op jit(solution)/shard_map/all_to_all | solution.py:304
  92.1 1.0 %shard_map.115 = bf16[32,128]{1,0:T(8,128)(2,1)} custom-call(bf16[32,24,128]{2,1,0:T(8,128)(2,1)S(1)} %all_to_all.28.got_ref, bf16[4,416,128]{2,1,0:T(8,128)(2,1)S(1)} %bitcast.15), custom_call_target="tpu_custom_call" | custom-call | flops 100000000 | bytes 622592 | tf_op jit(solution)/shard_map/pallas_call | solution.py:19
  (12 shorter events, 0.0 us)
Async XLA Ops:
  0.0 0.7 copy-start.3
  1.7 18.4 %copy-start = (bf16[2,128,4,32]{1,3,2,0:T(8,128)(2,1)S(1)}, bf16[2,128,4,32]{1,3,2,0:T(8,128)(2,1)}, u32[]{:S(2)}) copy-start(bf16[2,128,4,32]{1,3,2,0:T(8,128)(2,1)} %param.16) | copy-start | bytes 196612
  1.7 18.4 %copy-start.1 = (bf16[2,128,32]{1,2,0:T(8,128)(2,1)S(1)}, bf16[2,128,32]{1,2,0:T(8,128)(2,1)}, u32[]{:S(2)}) copy-start(bf16[2,128,32]{1,2,0:T(8,128)(2,1)} %param.17) | copy-start | bytes 49156
  1.8 18.4 %copy-start.2 = (bf16[2,32,128]{2,1,0:T(8,128)(2,1)S(1)}, bf16[2,32,128]{2,1,0:T(8,128)(2,1)}, u32[]{:S(2)}) copy-start(bf16[2,32,128]{2,1,0:T(8,128)(2,1)} %param.21) | copy-start | bytes 49156
  1.8 18.4 %copy-start.4 = (f32[2,128]{1,0:T(2,128)S(1)}, f32[2,128]{1,0:T(2,128)}, u32[]{:S(2)}) copy-start(f32[2,128]{1,0:T(2,128)} %gain_ref) | copy-start | bytes 3076
  1.8 18.4 %copy-start.5 = (f32[2,128]{1,0:T(2,128)S(1)}, f32[2,128]{1,0:T(2,128)}, u32[]{:S(2)}) copy-start(f32[2,128]{1,0:T(2,128)} %bias_ref) | copy-start | bytes 3076
  1.8 18.4 %copy-start.6 = (f32[2,32]{1,0:T(2,128)S(1)}, f32[2,32]{1,0:T(2,128)}, u32[]{:S(2)}) copy-start(f32[2,32]{1,0:T(2,128)} %pb_ref) | copy-start | bytes 772
  1.8 18.4 %copy-start.7 = (f32[2,32]{1,0:T(2,128)S(1)}, f32[2,32]{1,0:T(2,128)}, u32[]{:S(2)}) copy-start(f32[2,32]{1,0:T(2,128)} %og_ref) | copy-start | bytes 772
  1.8 18.4 %copy-start.8 = (f32[2,32]{1,0:T(2,128)S(1)}, f32[2,32]{1,0:T(2,128)}, u32[]{:S(2)}) copy-start(f32[2,32]{1,0:T(2,128)} %ob_ref) | copy-start | bytes 772
  1.8 18.4 %copy-start.9 = (s32[128]{0:T(128)S(1)}, s32[128]{0:T(128)}, u32[]{:S(2)}) copy-start(s32[128]{0:T(128)} %param.12) | copy-start | bytes 1540
  1.8 18.4 %copy-start.10 = (s32[128]{0:T(128)S(1)}, s32[128]{0:T(128)}, u32[]{:S(2)}) copy-start(s32[128]{0:T(128)} %param.13) | copy-start | bytes 1540
  1.9 35.4 %all-to-all-start = ((bf16[64,8,128]{2,1,0:T(8,128)(2,1)}), bf16[64,8,128]{2,1,0:T(8,128)(2,1)S(1)}, u32[]{:S(2)}, u32[]{:S(2)}) async-start(bf16[64,8,128]{2,1,0:T(8,128)(2,1)} %shard_map.109), calls=%async_computation | async-start | bytes 262144 | tf_op jit(solution)/shard_map/all_to_all | solution.py:285

commit v8 on v7

--- a/solution.py
+++ b/solution.py
@@ -151,16 +151,18 @@
     return v[:, 0:6] + v[:, 6:12] + v[:, 12:18]
 
 
-def project(n, w_ref, u, pm, out_ref):
+def project(n, w_ref, u, pm):
     sides = ([], [])
     for q in range(4):
         w = w_ref[q, u * 128 : u * 128 + 128, :]
         p = jnp.dot(w, n, preferred_element_type=f32)
         sides[0].append(sigmoid(p[0:32]) * p[32:64] * pm)
         sides[1].append(sigmoid(p[64:96]) * p[96:128] * pm)
-    for s in range(2):
-        v = jnp.stack([lanes([v[:, z * 32 : z * 32 + 32] for v in sides[s]]) for z in range(16)], axis=0)
-        out_ref[:, s * 16 : s * 16 + 16, :] = jnp.swapaxes(v, 0, 1).astype(bf16)
+    return sides
+
+
+def slabs(v):
+    return [lanes([a[:, z * 32 : z * 32 + 32] for a in v]) for z in range(16)]
 
 
 def gates(n, w_ref, u, cols, same):
@@ -178,7 +180,9 @@
     z_ref[...] = z0
     n = norm(z0, gain_ref[:, 0:1], gain_ref[:, 2:3])
     gate_ref[...] = gates(n, w_ref, 0, columns_of(w_ref)[:, 4:5], same_ref[...])
-    project(n, w_ref, 0, pm_ref[...], out_ref)
+    for s, v in enumerate(project(n, w_ref, 0, pm_ref[...])):
+        v = jnp.swapaxes(jnp.stack(slabs(v), axis=0), 0, 1)
+        out_ref[:, s * 16 : s * 16 + 16, :] = v.astype(bf16)
 
 
 def outgoing_kernel(got_ref, out_ref):
@@ -210,23 +214,58 @@
     z1_ref[...] = z1
     n1 = norm(z1.astype(f32), gain_ref[:, 1:2], gain_ref[:, 3:4])
     n1_ref[...] = n1
-    project(n1, w_ref, 1, pm_ref[...], out_ref)
+    left, right = project(n1, w_ref, 1, pm_ref[...])
+    lane = lax.broadcasted_iota(jnp.int32, (512, 128), 0)
+    col = lax.broadcasted_iota(jnp.int32, (512, 128), 1)
+    want = ((col & 15) << 5) | (((col >> 4) & 1) << 4) | lax.axis_index("z")
+    pick = ((lane == want) & (col < 32)).astype(f32).astype(bf16)
+    left = lanes([jnp.dot(v.astype(bf16), pick, preferred_element_type=f32)[:, 0:32] for v in left])
+    v = jnp.swapaxes(jnp.stack(slabs(right) + [left] * 8, axis=0), 0, 1)
+    first = lax.broadcasted_iota(jnp.int32, (8, 128), 0) == 0
+    for g in range(16):
+        marks = jnp.where(first, v[g, 16:24], v[16 + g, 16:24]).astype(bf16)
+        for yh in range(2):
+            at = (g // 4) * 8 + yh * 4 + g % 4
+            out_ref[at, 0:16, :] = v[g, 0:16].astype(bf16)
+            out_ref[at, 16:32, :] = v[16 + g, 0:16].astype(bf16)
+            out_ref[at, 32:40, :] = marks
 
 
 def incoming_kernel(got_ref, z1_ref, n1_ref, w_ref, same_ref, out_ref):
     here = lax.axis_index("z")
-    left, right = [], []
-    for q in range(4):
-        left.append(jnp.concatenate([got_ref[a * 4 + q, 0:16, :] for a in range(8)], axis=0))
-        right.append(jnp.concatenate([got_ref[a * 4 + q, 16:32, :] for a in range(8)], axis=0))
-    row = lax.broadcasted_iota(jnp.int32, (32, 512), 0)
-    lane = lax.broadcasted_iota(jnp.int32, (32, 512), 1)
-    want = (((row >> 1) & 3) << 7) | ((row >> 3) << 5) | ((row & 1) << 4) | here
-    pick = (lane == want).astype(f32).astype(bf16)
-    mine = nt(pick, lanes(left)).astype(bf16)
+    right = [
+        lanes(
+            [
+                jnp.concatenate([got_ref[a * 4 + q, h * 16 : h * 16 + 16, :] for a in range(8)], axis=0)
+                for h in range(2)
+            ]
+        )
+        for q in range(4)
+    ]
+    row = lax.broadcasted_iota(jnp.int32, (32, 128), 0)
+    lane = lax.broadcasted_iota(jnp.int32, (32, 128), 1)
+    wanted = ((row >> 3) == (lane >> 5)) & (((lane >> 4) & 1) == lax.axis_index("yh"))
+    parts = []
+    for a in range(8):
+        tiles = [got_ref[a * 4 + x, 32:40, :].astype(f32) for x in range(4)]
+        rows = jnp.concatenate([t[h : h + 1] for h in range(2) for t in tiles], axis=0)
+        parts.append(jnp.where(wanted, jnp.concatenate([rows] * 4, axis=0), 0.0).astype(bf16))
+    source = lax.broadcasted_iota(jnp.int32, (1024, 128), 0)
+    target = lax.broadcasted_iota(jnp.int32, (1024, 128), 1)
+    place = ((source >> 7) << 4) | (source & 15)
+    place = (place == target).astype(f32).astype(bf16)
+    mine = jnp.dot(lanes(parts), place, preferred_element_type=f32).astype(bf16)
     prods = [jnp.dot(mine, r, preferred_element_type=f32) for r in right]
-    xs = [lanes([p[d * 8 : d * 8 + 8, d * 32 : d * 32 + 32] for p in prods]) for d in range(4)]
-    x = jnp.swapaxes(jnp.stack(xs + xs, axis=0), 0, 1).astype(bf16)
+    upper = lax.broadcasted_iota(jnp.int32, (8, 128), 0) < 4
+    xs = []
+    for d in range(4):
+        h0, h1 = (
+            lanes([p[d * 8 : d * 8 + 8, h * 128 + d * 32 : h * 128 + d * 32 + 32] for p in prods])
+            for h in range(2)
+        )
+        xs.append(jnp.where(upper, h0, h1))
+    x = jnp.swapaxes(jnp.stack(xs + xs, axis=0), 0, 1)
+    x = [jnp.where(upper, x[i], x[4 + i]).astype(bf16) for i in range(4)]
     lane = lax.broadcasted_iota(jnp.int32, (512, 128), 0)
     col = lax.broadcasted_iota(jnp.int32, (512, 128), 1)
     pick = ((lane == here * 32 + col) & (col < 32)).astype(f32).astype(bf16)
@@ -241,7 +280,7 @@
             lanes([v[q * 32 + c * 8 : q * 32 + c * 8 + 8, 0:32] for c in range(4)]).astype(bf16)
             for v in (z1, gate)
         )
-        for a in range(8):
+        for a in range(4):
             out_ref[a * 4 + q, 0:8, :] = x[a]
             out_ref[a * 4 + q, 8:16, :] = zq
             out_ref[a * 4 + q, 16:24, :] = gq
@@ -249,13 +288,13 @@
 
 def last_kernel(got_ref, w_ref, out_ref, ys):
     x = jnp.swapaxes(got_ref[:, 0:8, :].astype(f32), 0, 1)
-    x1 = jnp.concatenate([x[d] for d in range(4)], axis=0)
+    x1 = jnp.concatenate([x[h * 4 + d] for d in range(4) for h in range(2)], axis=0)
     cols = columns_of(w_ref)
     xn = norm(x1, cols[:, 1:2], cols[:, 3:4])
     w = jnp.concatenate([w_ref[q, 352:384, :] for q in range(4)], axis=0)
     ys[...] = tn(w, xn)
     y = ys[pl.ds(pl.multiple_of(lax.axis_index("ch") * 32, 32), 32), :]
-    home = (lax.axis_index("x") * 2 + lax.axis_index("yh")) * 4
+    home = lax.axis_index("x") * 4
     own = [got_ref[home + s].astype(f32) for s in range(4)]
     z1, gate = (
         jnp.concatenate(
@@ -296,12 +335,12 @@
     got = lax.all_to_all(send, PLANE, 0, 0, tiled=True)
     send, z1, n1 = call(
         middle_kernel,
-        [((32, 32, 128), bf16), ((128, 512), bf16), ((128, 512), bf16)],
+        [((32, 40, 128), bf16), ((128, 512), bf16), ((128, 512), bf16)],
         [got, z0, gate, gains, packed, pm],
     )
     got = lax.all_to_all(send, PLANE, 0, 0, tiled=True)
-    (send,) = call(incoming_kernel, [((32, 24, 128), bf16)], [got, z1, n1, packed, same])
-    got = lax.all_to_all(send, PLANE, 0, 0, tiled=True)
+    (send,) = call(incoming_kernel, [((16, 24, 128), bf16)], [got, z1, n1, packed, same])
+    got = lax.all_to_all(send, ("x", "ch"), 0, 0, tiled=True)
     (out,) = call(last_kernel, [((32, 128), bf16)], [got, packed], [(128, 128)])
     return out.reshape(32, 1, 128)
 

time: 93.5 us -> 90.7 us (0.970)
  blocking collectives: 58.9 us -> 56.2 us
    all_to_all x4 -> x3, blocking collectives: 51.5 us -> 40.4 us  [body(): got = lax.all_to_all(send, PLANE, 0, 0, tiled=True)]
    all_to_all x0 -> x1, blocking collectives: none -> 8.52 us  [body(): got = lax.all_to_all(send, ('x', 'ch'), 0, 0, tiled=True)]
  transfers between devices with their start and end apart: 1 -> 1, of which waited for: 1 -> 1; matrix products, arithmetic and copies ran while one was open for 0% -> 0% of each run, Pallas kernels for 0% -> 1%
where the time goes in v8:
time: 90.7 us; the launch traced here: 90.3 us
  blocking collectives  56.2 us (62%)
  starting transfers between devices  18.3 us (20%)
  waiting for transfers between devices  9.17 us (10%)
  Pallas kernels  5.62 us (6%)
    all_to_all x3, blocking collectives, body(): got = lax.all_to_all(send, PLANE, 0, 0, tiled=True)  40.4 us
    all_to_all x1, starting transfers between devices, body(): got = lax.all_to_all(send, ('z', 'ch'), 0, 0, tiled=True)  18.3 us
    all_to_all x1, waiting for transfers between devices, body(): got = lax.all_to_all(send, ('z', 'ch'), 0, 0, tiled=True)  9.17 us
    all_to_all x1, blocking collectives, body(): got = lax.all_to_all(send, ('x', 'ch'), 0, 0, tiled=True)  8.52 us
    all_gather x1, blocking collectives, body(): packed = lax.all_gather(packed, 'ch', axis=0)  7.36 us
    pallas_call x5, Pallas kernels, call(): pl.pallas_call(kernel, out_shape=[jax.ShapeDtypeStruct(s, d) for s, d in...  4.12 us
  transfers between devices with their start and end apart: 1, of which 1 were waited for; matrix products, arithmetic and copies ran while one was open for 0% of the time, Pallas kernels for 1%

profile of v8, /device:TPU:1, one launch (start us, length us, event | category | flops | bytes accessed | tf_op | source)
XLA Modules:
  0.0 90.3 jit_solution(6881698917020641812)
XLA Ops:
  0.0 0.7 copy-done.3
  0.7 1.0 %shard_map.109 = bf16[64,8,128]{2,1,0:T(8,128)(2,1)} custom-call(bf16[32,128]{1,0:T(8,128)(2,1)S(1)} %bitcast.19), custom_call_target="tpu_custom_call" | custom-call | tf_op jit(solution)/shard_map/pallas_call | solution.py:72
  1.7 0.0 copy-start
  1.7 0.0 copy-start.1
  1.8 0.0 copy-start.2
  1.8 0.0 copy-start.4
  1.8 0.0 copy-start.5
  1.8 0.0 copy-start.6
  1.8 0.0 copy-start.7
  1.8 0.0 copy-start.8
  1.8 0.0 copy-start.9
  1.9 18.3 %all-to-all-start = ((bf16[64,8,128]{2,1,0:T(8,128)(2,1)}), bf16[64,8,128]{2,1,0:T(8,128)(2,1)S(1)}, u32[]{:S(2)}, u32[]{:S(2)}) async-start(bf16[64,8,128]{2,1,0:T(8,128)(2,1)} %shard_map.109), calls=%async_computation | async-start | bytes 262144 | tf_op jit(solution)/shard_map/all_to_all | solution.py:324
  20.3 0.5 shard_map.110
  20.7 7.4 %all-gather = bf16[1664,128]{1,0:T(8,128)(2,1)S(1)} all-gather(bf16[416,128]{1,0:T(8,128)(2,1)S(1)} %get-tuple-element.42), channel_id=2, replica_groups=mesh['x'=4,'z'=16,'yh'=2,'ch'=4] {'ch'}, dimensions={0}, use_global_device_ids=true | all-gather | bytes 532480 | tf_op jit(solution)/shard_map/all_gather | solution.py:326
  28.1 9.2 %all-to-all-done.got_ref = bf16[64,8,128]{2,1,0:T(8,128)(2,1)S(1)} async-done(((bf16[64,8,128]{2,1,0:T(8,128)(2,1)}), bf16[64,8,128]{2,1,0:T(8,128)(2,1)S(1)}, u32[]{:S(2)}, u32[]{:S(2)}) %all-to-all-start) | async-done | bytes 131104 | tf_op jit(solution)/shard_map/all_to_all | solution.py:324
  37.3 0.9 %shard_map.111 = (bf16[32,32,128]{2,1,0:T(8,128)(2,1)S(1)}, f32[128,512]{1,0:T(8,128)S(1)}, f32[128,512]{1,0:T(8,128)S(1)}) custom-call(bf16[64,8,128]{2,1,0:T(8,128)(2,1)S(1)} %all-to-all-done.got_ref, f32[128,8]{1,0:T(8,128)S(1)} %get-tuple-element.47.gain_ref, bf16[4,416,128]{2,1,0:T(8,128)(2,1)S(1)} %bitcast.12, f32[1,512]{1,0:T(1,128)S(1)} %get-tuple-element.49.pm_ref, ...), custom_call_target="tpu_custom_call" | custom-call | flops 100000000 | bytes 565248 | tf_op jit(solution)/shard_map/pallas_call | solution.py:19
  38.2 16.0 %all_to_all.25.got_ref = bf16[32,32,128]{2,1,0:T(8,128)(2,1)S(1)} all-to-all(bf16[32,32,128]{2,1,0:T(8,128)(2,1)S(1)} %get-tuple-element.51), channel_id=1, replica_groups=mesh['x'=4,'z'=16,'yh'=2,'ch'=4] {'x','yh','ch'}, dimensions={0} | all-to-all | bytes 524288 | tf_op jit(solution)/shard_map/all_to_all | solution.py:333
  54.2 0.3 shard_map.112
  54.5 11.2 %all_to_all.26.got_ref = bf16[32,16,128]{2,1,0:T(8,128)(2,1)S(1)} all-to-all(bf16[32,16,128]{2,1,0:T(8,128)(2,1)S(1)} %shard_map.112), channel_id=1, replica_groups=mesh['x'=4,'z'=16,'yh'=2,'ch'=4] {'x','yh','ch'}, dimensions={0} | all-to-all | bytes 262144 | tf_op jit(solution)/shard_map/all_to_all | solution.py:335
  65.7 1.1 %shard_map.113 = (bf16[32,40,128]{2,1,0:T(8,128)(2,1)S(1)}, bf16[128,512]{1,0:T(8,128)(2,1)S(1)}, bf16[128,512]{1,0:T(8,128)(2,1)S(1)}) custom-call(bf16[32,16,128]{2,1,0:T(8,128)(2,1)S(1)} %all_to_all.26.got_ref, f32[128,512]{1,0:T(8,128)S(1)} %get-tuple-element.52.z_ref, f32[128,512]{1,0:T(8,128)S(1)} %get-tuple-element.53.gate_ref, ...), custom_call_target="tpu_custom_call" | custom-call | flops 100000000 | bytes 1087488 | tf_op jit(solution)/shard_map/pallas_call | solution.py:19
  66.8 13.2 %all_to_all.27.got_ref = bf16[32,40,128]{2,1,0:T(8,128)(2,1)S(1)} all-to-all(bf16[32,40,128]{2,1,0:T(8,128)(2,1)S(1)} %get-tuple-element.54), channel_id=1, replica_groups=mesh['x'=4,'z'=16,'yh'=2,'ch'=4] {'x','yh','ch'}, dimensions={0} | all-to-all | bytes 655360 | tf_op jit(solution)/shard_map/all_to_all | solution.py:341
  80.0 0.7 shard_map.114
  80.8 8.5 %all_to_all.28.got_ref = bf16[16,24,128]{2,1,0:T(8,128)(2,1)S(1)} all-to-all(bf16[16,24,128]{2,1,0:T(8,128)(2,1)S(1)} %shard_map.114), channel_id=1, replica_groups=mesh['x'=4,'z'=16,'yh'=2,'ch'=4] {'x','ch'}, dimensions={0} | all-to-all | bytes 196608 | tf_op jit(solution)/shard_map/all_to_all | solution.py:343
  89.3 1.0 %shard_map.115 = bf16[32,128]{1,0:T(8,128)(2,1)} custom-call(bf16[16,24,128]{2,1,0:T(8,128)(2,1)S(1)} %all_to_all.28.got_ref, bf16[4,416,128]{2,1,0:T(8,128)(2,1)S(1)} %bitcast.15), custom_call_target="tpu_custom_call" | custom-call | flops 100000000 | bytes 524288 | tf_op jit(solution)/shard_map/pallas_call | solution.py:19
  (12 shorter events, 0.0 us)
Async XLA Ops:
  0.0 0.7 copy-start.3
  1.7 18.4 %copy-start = (bf16[2,128,4,32]{1,3,2,0:T(8,128)(2,1)S(1)}, bf16[2,128,4,32]{1,3,2,0:T(8,128)(2,1)}, u32[]{:S(2)}) copy-start(bf16[2,128,4,32]{1,3,2,0:T(8,128)(2,1)} %param.16) | copy-start | bytes 196612
  1.7 18.4 %copy-start.1 = (bf16[2,128,32]{1,2,0:T(8,128)(2,1)S(1)}, bf16[2,128,32]{1,2,0:T(8,128)(2,1)}, u32[]{:S(2)}) copy-start(bf16[2,128,32]{1,2,0:T(8,128)(2,1)} %param.17) | copy-start | bytes 49156
  1.8 18.4 %copy-start.2 = (bf16[2,32,128]{2,1,0:T(8,128)(2,1)S(1)}, bf16[2,32,128]{2,1,0:T(8,128)(2,1)}, u32[]{:S(2)}) copy-start(bf16[2,32,128]{2,1,0:T(8,128)(2,1)} %param.21) | copy-start | bytes 49156
  1.8 18.4 %copy-start.4 = (f32[2,128]{1,0:T(2,128)S(1)}, f32[2,128]{1,0:T(2,128)}, u32[]{:S(2)}) copy-start(f32[2,128]{1,0:T(2,128)} %gain_ref) | copy-start | bytes 3076
  1.8 18.4 %copy-start.5 = (f32[2,128]{1,0:T(2,128)S(1)}, f32[2,128]{1,0:T(2,128)}, u32[]{:S(2)}) copy-start(f32[2,128]{1,0:T(2,128)} %bias_ref) | copy-start | bytes 3076
  1.8 18.4 %copy-start.6 = (f32[2,32]{1,0:T(2,128)S(1)}, f32[2,32]{1,0:T(2,128)}, u32[]{:S(2)}) copy-start(f32[2,32]{1,0:T(2,128)} %pb_ref) | copy-start | bytes 772
  1.8 18.4 %copy-start.7 = (f32[2,32]{1,0:T(2,128)S(1)}, f32[2,32]{1,0:T(2,128)}, u32[]{:S(2)}) copy-start(f32[2,32]{1,0:T(2,128)} %og_ref) | copy-start | bytes 772
  1.8 18.4 %copy-start.8 = (f32[2,32]{1,0:T(2,128)S(1)}, f32[2,32]{1,0:T(2,128)}, u32[]{:S(2)}) copy-start(f32[2,32]{1,0:T(2,128)} %ob_ref) | copy-start | bytes 772
  1.8 18.4 %copy-start.9 = (s32[128]{0:T(128)S(1)}, s32[128]{0:T(128)}, u32[]{:S(2)}) copy-start(s32[128]{0:T(128)} %param.12) | copy-start | bytes 1540
  1.8 18.4 %copy-start.10 = (s32[128]{0:T(128)S(1)}, s32[128]{0:T(128)}, u32[]{:S(2)}) copy-start(s32[128]{0:T(128)} %param.13) | copy-start | bytes 1540
  1.9 35.4 %all-to-all-start = ((bf16[64,8,128]{2,1,0:T(8,128)(2,1)}), bf16[64,8,128]{2,1,0:T(8,128)(2,1)S(1)}, u32[]{:S(2)}, u32[]{:S(2)}) async-start(bf16[64,8,128]{2,1,0:T(8,128)(2,1)} %shard_map.109), calls=%async_computation | async-start | bytes 262144 | tf_op jit(solution)/shard_map/all_to_all | solution.py:324

commit v9 on v8

--- a/solution.py
+++ b/solution.py
@@ -27,10 +27,6 @@
     )(*ins)
 
 
-def tn(a, b):
-    return lax.dot_general(a, b, (((0,), (0,)), ((), ())), preferred_element_type=f32)
-
-
 def nt(a, b):
     return lax.dot_general(a, b, (((1,), (1,)), ((), ())), preferred_element_type=f32)
 
@@ -49,9 +45,9 @@
     return jnp.concatenate(pieces, axis=1)
 
 
-def permutation():
-    k = lax.broadcasted_iota(jnp.int32, (128, 128), 0)
-    p = lax.broadcasted_iota(jnp.int32, (128, 128), 1)
+def permutation(k_dim=0):
+    k = lax.broadcasted_iota(jnp.int32, (128, 128), k_dim)
+    p = lax.broadcasted_iota(jnp.int32, (128, 128), 1 - k_dim)
     place = (k & 96) | ((k & 1) << 4) | ((k & 31) >> 1)
     return (place == p).astype(f32).astype(bf16)
 
@@ -146,9 +142,19 @@
     )(*args)
 
 
-def columns_of(w_ref):
+def arrange_kernel(w_ref, cols_ref, wo_ref, own_ref, back_ref, scr):
     v = jnp.concatenate([w_ref[q, 384:416, :].astype(f32) for q in range(4)], axis=0)
-    return v[:, 0:6] + v[:, 6:12] + v[:, 12:18]
+    cols_ref[...] = v[:, 0:8] + v[:, 6:14] + v[:, 12:20]
+    for u in range(2):
+        w = jnp.concatenate([w_ref[q, 320 + u * 32 : 352 + u * 32, :] for q in range(4)], axis=0)
+        w = w.astype(f32).T
+        if u == 0:
+            wo_ref[...] = w.astype(bf16)
+        else:
+            scr[...] = w
+    own = pl.multiple_of(lax.axis_index("ch") * 32, 32)
+    own_ref[...] = scr[pl.ds(own, 32), :].astype(bf16)
+    back_ref[...] = permutation(1)
 
 
 def project(n, w_ref, u, pm):
@@ -170,7 +176,7 @@
     return sigmoid(jnp.dot(w, n, preferred_element_type=f32) + cols * same)
 
 
-def first_kernel(got_ref, gain_ref, w_ref, pm_ref, same_ref, out_ref, z_ref, gate_ref):
+def first_kernel(got_ref, gain_ref, cols_ref, w_ref, pm_ref, same_ref, out_ref, z_ref, gate_ref):
     rows = []
     for q in range(4):
         for c in range(4):
@@ -179,7 +185,7 @@
     z0 = jnp.concatenate(rows, axis=0)
     z_ref[...] = z0
     n = norm(z0, gain_ref[:, 0:1], gain_ref[:, 2:3])
-    gate_ref[...] = gates(n, w_ref, 0, columns_of(w_ref)[:, 4:5], same_ref[...])
+    gate_ref[...] = gates(n, w_ref, 0, cols_ref[:, 4:5], same_ref[...])
     for s, v in enumerate(project(n, w_ref, 0, pm_ref[...])):
         v = jnp.swapaxes(jnp.stack(slabs(v), axis=0), 0, 1)
         out_ref[:, s * 16 : s * 16 + 16, :] = v.astype(bf16)
@@ -202,15 +208,14 @@
             out_ref[b * 4 + q] = x[b * 16 : b * 16 + 16]
 
 
-def middle_kernel(got_ref, z_ref, gate_ref, gain_ref, w_ref, pm_ref, out_ref, z1_ref, n1_ref):
+def middle_kernel(got_ref, z_ref, gate_ref, gain_ref, cols_ref, wo_ref, w_ref, pm_ref, out_ref, z1_ref, n1_ref):
     x = jnp.swapaxes(got_ref[...].astype(f32), 0, 1)
     x0 = jnp.concatenate(
         [lanes([x[z][:, d * 32 : d * 32 + 32] for z in range(16)]) for d in range(4)], axis=0
     )
-    cols = columns_of(w_ref)
-    xn = norm(x0, cols[:, 0:1], cols[:, 2:3])
-    w = jnp.concatenate([w_ref[q, 320:352, :] for q in range(4)], axis=0)
-    z1 = (z_ref[...] + gate_ref[...] * tn(w, xn)).astype(bf16)
+    xn = norm(x0, cols_ref[:, 0:1], cols_ref[:, 2:3])
+    y = jnp.dot(wo_ref[...], xn, preferred_element_type=f32)
+    z1 = (z_ref[...] + gate_ref[...] * y).astype(bf16)
     z1_ref[...] = z1
     n1 = norm(z1.astype(f32), gain_ref[:, 1:2], gain_ref[:, 3:4])
     n1_ref[...] = n1
@@ -231,7 +236,7 @@
             out_ref[at, 32:40, :] = marks
 
 
-def incoming_kernel(got_ref, z1_ref, n1_ref, w_ref, same_ref, out_ref):
+def incoming_kernel(got_ref, z1_ref, n1_ref, cols_ref, w_ref, same_ref, out_ref):
     here = lax.axis_index("z")
     right = [
         lanes(
@@ -274,7 +279,7 @@
     same = jnp.dot(
         jnp.broadcast_to(same_ref[...], (8, 512)).astype(bf16), pick, preferred_element_type=f32
     )[0:1]
-    gate = gates(n1, w_ref, 1, columns_of(w_ref)[:, 5:6], same)
+    gate = gates(n1, w_ref, 1, cols_ref[:, 5:6], same)
     for q in range(4):
         zq, gq = (
             lanes([v[q * 32 + c * 8 : q * 32 + c * 8 + 8, 0:32] for c in range(4)]).astype(bf16)
@@ -286,14 +291,11 @@
             out_ref[a * 4 + q, 16:24, :] = gq
 
 
-def last_kernel(got_ref, w_ref, out_ref, ys):
+def last_kernel(got_ref, cols_ref, own_ref, back_ref, out_ref):
     x = jnp.swapaxes(got_ref[:, 0:8, :].astype(f32), 0, 1)
     x1 = jnp.concatenate([x[h * 4 + d] for d in range(4) for h in range(2)], axis=0)
-    cols = columns_of(w_ref)
-    xn = norm(x1, cols[:, 1:2], cols[:, 3:4])
-    w = jnp.concatenate([w_ref[q, 352:384, :] for q in range(4)], axis=0)
-    ys[...] = tn(w, xn)
-    y = ys[pl.ds(pl.multiple_of(lax.axis_index("ch") * 32, 32), 32), :]
+    xn = norm(x1, cols_ref[:, 1:2], cols_ref[:, 3:4])
+    y = jnp.dot(own_ref[...], xn, preferred_element_type=f32)
     home = lax.axis_index("x") * 4
     own = [got_ref[home + s].astype(f32) for s in range(4)]
     z1, gate = (
@@ -303,7 +305,7 @@
         for r in (8, 16)
     )
     out = (z1 + gate * y).astype(bf16)
-    out_ref[...] = nt(out, permutation()).astype(bf16)
+    out_ref[...] = jnp.dot(out, back_ref[...], preferred_element_type=f32).astype(bf16)
 
 
 def body(pair_rep, residue_mask, chain_ids, in_gain, in_bias, w_proj, w_gate, pair_bias, out_gain, out_bias, w_out):
@@ -324,11 +326,20 @@
     got = lax.all_to_all(send, ("z", "ch"), 0, 0, tiled=True)
     packed, gains, pm, same = prepare(*args)
     packed = lax.all_gather(packed, "ch", axis=0)
-    got, packed, gains, pm, same = lax.optimization_barrier((got, packed, gains, pm, same))
+    cols, wo, own, back = call(
+        arrange_kernel,
+        [((128, 8), f32), ((128, 128), bf16), ((32, 128), bf16), ((128, 128), bf16)],
+        [packed],
+        [(128, 128)],
+        flops=1_000_000,
+    )
+    got, packed, gains, pm, same, cols, wo, own, back = lax.optimization_barrier(
+        (got, packed, gains, pm, same, cols, wo, own, back)
+    )
     send, z0, gate = call(
         first_kernel,
         [((32, 32, 128), bf16), ((128, 512), f32), ((128, 512), f32)],
-        [got, gains, packed, pm, same],
+        [got, gains, cols, packed, pm, same],
     )
     got = lax.all_to_all(send, PLANE, 0, 0, tiled=True)
     (send,) = call(outgoing_kernel, [((32, 16, 128), bf16)], [got])
@@ -336,12 +347,12 @@
     send, z1, n1 = call(
         middle_kernel,
         [((32, 40, 128), bf16), ((128, 512), bf16), ((128, 512), bf16)],
-        [got, z0, gate, gains, packed, pm],
+        [got, z0, gate, gains, cols, wo, packed, pm],
     )
     got = lax.all_to_all(send, PLANE, 0, 0, tiled=True)
-    (send,) = call(incoming_kernel, [((16, 24, 128), bf16)], [got, z1, n1, packed, same])
+    (send,) = call(incoming_kernel, [((16, 24, 128), bf16)], [got, z1, n1, cols, packed, same])
     got = lax.all_to_all(send, ("x", "ch"), 0, 0, tiled=True)
-    (out,) = call(last_kernel, [((32, 128), bf16)], [got, packed], [(128, 128)])
+    (out,) = call(last_kernel, [((32, 128), bf16)], [got, cols, own, back])
     return out.reshape(32, 1, 128)
 
 

time: 90.7 us -> 90.6 us (level)
    pallas_call x5 -> x6, Pallas kernels: 4.12 us -> 4.17 us  [call(): pl.pallas_call(kernel, out_shape=[jax.ShapeDtypeStruct(s, d) for s, d in...]
where the time goes in v9:
time: 90.6 us; the launch traced here: 90.2 us
  blocking collectives  56.2 us (62%)
  starting transfers between devices  18.3 us (20%)
  waiting for transfers between devices  9.03 us (10%)
  Pallas kernels  5.66 us (6%)
    all_to_all x3, blocking collectives, body(): got = lax.all_to_all(send, PLANE, 0, 0, tiled=True)  40.4 us
    all_to_all x1, starting transfers between devices, body(): got = lax.all_to_all(send, ('z', 'ch'), 0, 0, tiled=True)  18.3 us
    all_to_all x1, waiting for transfers between devices, body(): got = lax.all_to_all(send, ('z', 'ch'), 0, 0, tiled=True)  9.03 us
    all_to_all x1, blocking collectives, body(): got = lax.all_to_all(send, ('x', 'ch'), 0, 0, tiled=True)  8.52 us
    all_gather x1, blocking collectives, body(): packed = lax.all_gather(packed, 'ch', axis=0)  7.36 us
    pallas_call x6, Pallas kernels, call(): pl.pallas_call(kernel, out_shape=[jax.ShapeDtypeStruct(s, d) for s, d in...  4.17 us
  transfers between devices with their start and end apart: 1, of which 1 were waited for; matrix products, arithmetic and copies ran while one was open for 0% of the time, Pallas kernels for 1%

profile of v9, /device:TPU:1, one launch (start us, length us, event | category | flops | bytes accessed | tf_op | source)
XLA Modules:
  0.0 90.2 jit_solution(10314588621645772480)
XLA Ops:
  0.0 0.7 copy-done.3
  0.7 1.0 %shard_map.109 = bf16[64,8,128]{2,1,0:T(8,128)(2,1)} custom-call(bf16[32,128]{1,0:T(8,128)(2,1)S(1)} %bitcast.19), custom_call_target="tpu_custom_call" | custom-call | tf_op jit(solution)/shard_map/pallas_call | solution.py:68
  1.7 0.0 copy-start
  1.7 0.0 copy-start.1
  1.8 0.0 copy-start.2
  1.8 0.0 copy-start.4
  1.8 0.0 copy-start.5
  1.8 0.0 copy-start.6
  1.8 0.0 copy-start.9
  1.8 0.0 copy-start.10
  1.9 18.3 %all-to-all-start = ((bf16[64,8,128]{2,1,0:T(8,128)(2,1)}), bf16[64,8,128]{2,1,0:T(8,128)(2,1)S(1)}, u32[]{:S(2)}, u32[]{:S(2)}) async-start(bf16[64,8,128]{2,1,0:T(8,128)(2,1)} %shard_map.109), calls=%async_computation | async-start | bytes 262144 | tf_op jit(solution)/shard_map/all_to_all | solution.py:326
  20.3 0.5 shard_map.110
  20.7 7.4 %all-gather = bf16[1664,128]{1,0:T(8,128)(2,1)S(1)} all-gather(bf16[416,128]{1,0:T(8,128)(2,1)S(1)} %get-tuple-element.50), channel_id=2, replica_groups=mesh['x'=4,'z'=16,'yh'=2,'ch'=4] {'ch'}, dimensions={0}, use_global_device_ids=true | all-gather | bytes 532480 | tf_op jit(solution)/shard_map/all_gather | solution.py:328
  28.1 0.1 shard_map.111
  28.2 9.0 %all-to-all-done.got_ref = bf16[64,8,128]{2,1,0:T(8,128)(2,1)S(1)} async-done(((bf16[64,8,128]{2,1,0:T(8,128)(2,1)}), bf16[64,8,128]{2,1,0:T(8,128)(2,1)S(1)}, u32[]{:S(2)}, u32[]{:S(2)}) %all-to-all-start) | async-done | bytes 131104 | tf_op jit(solution)/shard_map/all_to_all | solution.py:326
  37.3 1.0 %shard_map.112 = (bf16[32,32,128]{2,1,0:T(8,128)(2,1)S(1)}, f32[128,512]{1,0:T(8,128)S(1)}, f32[128,512]{1,0:T(8,128)S(1)}) custom-call(bf16[64,8,128]{2,1,0:T(8,128)(2,1)S(1)} %all-to-all-done.got_ref, f32[128,8]{1,0:T(8,128)S(1)} %get-tuple-element.59.gain_ref, f32[128,8]{1,0:T(8,128)S(1)} %get-tuple-element.60.cols_ref, ...), custom_call_target="tpu_custom_call" | custom-call | flops 100000000 | bytes 569344 | tf_op jit(solution)/shard_map/pallas_call | solution.py:19
  38.2 16.0 %all_to_all.25.got_ref = bf16[32,32,128]{2,1,0:T(8,128)(2,1)S(1)} all-to-all(bf16[32,32,128]{2,1,0:T(8,128)(2,1)S(1)} %get-tuple-element.64), channel_id=1, replica_groups=mesh['x'=4,'z'=16,'yh'=2,'ch'=4] {'x','yh','ch'}, dimensions={0} | all-to-all | bytes 524288 | tf_op jit(solution)/shard_map/all_to_all | solution.py:344
  54.2 0.3 shard_map.113
  54.5 11.2 %all_to_all.26.got_ref = bf16[32,16,128]{2,1,0:T(8,128)(2,1)S(1)} all-to-all(bf16[32,16,128]{2,1,0:T(8,128)(2,1)S(1)} %shard_map.113), channel_id=1, replica_groups=mesh['x'=4,'z'=16,'yh'=2,'ch'=4] {'x','yh','ch'}, dimensions={0} | all-to-all | bytes 262144 | tf_op jit(solution)/shard_map/all_to_all | solution.py:346
  65.7 1.1 %shard_map.114 = (bf16[32,40,128]{2,1,0:T(8,128)(2,1)S(1)}, bf16[128,512]{1,0:T(8,128)(2,1)S(1)}, bf16[128,512]{1,0:T(8,128)(2,1)S(1)}) custom-call(bf16[32,16,128]{2,1,0:T(8,128)(2,1)S(1)} %all_to_all.26.got_ref, f32[128,512]{1,0:T(8,128)S(1)} %get-tuple-element.65.z_ref, f32[128,512]{1,0:T(8,128)S(1)} %get-tuple-element.66.gate_ref, ...), custom_call_target="tpu_custom_call" | custom-call | flops 100000000 | bytes 1124352 | tf_op jit(solution)/shard_map/pallas_call | solution.py:19
  66.8 13.2 %all_to_all.27.got_ref = bf16[32,40,128]{2,1,0:T(8,128)(2,1)S(1)} all-to-all(bf16[32,40,128]{2,1,0:T(8,128)(2,1)S(1)} %get-tuple-element.68), channel_id=1, replica_groups=mesh['x'=4,'z'=16,'yh'=2,'ch'=4] {'x','yh','ch'}, dimensions={0} | all-to-all | bytes 655360 | tf_op jit(solution)/shard_map/all_to_all | solution.py:352
  80.0 0.7 shard_map.115
  80.7 8.5 %all_to_all.28.got_ref = bf16[16,24,128]{2,1,0:T(8,128)(2,1)S(1)} all-to-all(bf16[16,24,128]{2,1,0:T(8,128)(2,1)S(1)} %shard_map.115), channel_id=1, replica_groups=mesh['x'=4,'z'=16,'yh'=2,'ch'=4] {'x','ch'}, dimensions={0} | all-to-all | bytes 196608 | tf_op jit(solution)/shard_map/all_to_all | solution.py:354
  89.3 1.0 %shard_map.116 = bf16[32,128]{1,0:T(8,128)(2,1)} custom-call(bf16[16,24,128]{2,1,0:T(8,128)(2,1)S(1)} %all_to_all.28.got_ref, f32[128,8]{1,0:T(8,128)S(1)} %get-tuple-element.60.cols_ref, bf16[32,128]{1,0:T(8,128)(2,1)S(1)} %get-tuple-element.71.own_ref, bf16[128,128]{1,0:T(8,128)(2,1)S(1)} %get-tuple-element.72.back_ref), custom_call_target="tpu_custom_call" | custom-call | flops 100000000 | bytes 143360 | tf_op jit(solution)/shard_map/pallas_call | solution.py:19
  (13 shorter events, 0.0 us)
Async XLA Ops:
  0.0 0.7 copy-start.3
  1.7 18.4 %copy-start = (bf16[2,128,4,32]{1,3,2,0:T(8,128)(2,1)S(1)}, bf16[2,128,4,32]{1,3,2,0:T(8,128)(2,1)}, u32[]{:S(2)}) copy-start(bf16[2,128,4,32]{1,3,2,0:T(8,128)(2,1)} %param.16) | copy-start | bytes 196612
  1.7 18.4 %copy-start.1 = (bf16[2,128,32]{1,2,0:T(8,128)(2,1)S(1)}, bf16[2,128,32]{1,2,0:T(8,128)(2,1)}, u32[]{:S(2)}) copy-start(bf16[2,128,32]{1,2,0:T(8,128)(2,1)} %param.17) | copy-start | bytes 49156
  1.8 18.4 %copy-start.2 = (bf16[2,32,128]{2,1,0:T(8,128)(2,1)S(1)}, bf16[2,32,128]{2,1,0:T(8,128)(2,1)}, u32[]{:S(2)}) copy-start(bf16[2,32,128]{2,1,0:T(8,128)(2,1)} %param.21) | copy-start | bytes 49156
  1.8 18.4 %copy-start.4 = (f32[2,128]{1,0:T(2,128)S(1)}, f32[2,128]{1,0:T(2,128)}, u32[]{:S(2)}) copy-start(f32[2,128]{1,0:T(2,128)} %gain_ref) | copy-start | bytes 3076
  1.8 18.4 %copy-start.5 = (f32[2,128]{1,0:T(2,128)S(1)}, f32[2,128]{1,0:T(2,128)}, u32[]{:S(2)}) copy-start(f32[2,128]{1,0:T(2,128)} %bias_ref) | copy-start | bytes 3076
  1.8 18.4 %copy-start.6 = (f32[2,32]{1,0:T(2,128)S(1)}, f32[2,32]{1,0:T(2,128)}, u32[]{:S(2)}) copy-start(f32[2,32]{1,0:T(2,128)} %pb_ref) | copy-start | bytes 772
  1.8 18.4 %copy-start.7 = (f32[2,32]{1,0:T(2,128)S(1)}, f32[2,32]{1,0:T(2,128)}, u32[]{:S(2)}) copy-start(f32[2,32]{1,0:T(2,128)} %og_ref) | copy-start | bytes 772
  1.8 18.4 %copy-start.8 = (f32[2,32]{1,0:T(2,128)S(1)}, f32[2,32]{1,0:T(2,128)}, u32[]{:S(2)}) copy-start(f32[2,32]{1,0:T(2,128)} %ob_ref) | copy-start | bytes 772
  1.8 18.4 %copy-start.9 = (s32[128]{0:T(128)S(1)}, s32[128]{0:T(128)}, u32[]{:S(2)}) copy-start(s32[128]{0:T(128)} %param.12) | copy-start | bytes 1540
  1.8 18.4 %copy-start.10 = (s32[128]{0:T(128)S(1)}, s32[128]{0:T(128)}, u32[]{:S(2)}) copy-start(s32[128]{0:T(128)} %param.13) | copy-start | bytes 1540
  1.9 35.4 %all-to-all-start = ((bf16[64,8,128]{2,1,0:T(8,128)(2,1)}), bf16[64,8,128]{2,1,0:T(8,128)(2,1)S(1)}, u32[]{:S(2)}, u32[]{:S(2)}) async-start(bf16[64,8,128]{2,1,0:T(8,128)(2,1)} %shard_map.109), calls=%async_computation | async-start | bytes 262144 | tf_op jit(solution)/shard_map/all_to_all | solution.py:326

commit v10 on v9

--- a/solution.py
+++ b/solution.py
@@ -10,6 +10,13 @@
 f32 = jnp.float32
 ROW = ("x", "z", "yh")
 PLANE = ("x", "yh", "ch")
+ALL = ("x", "z", "yh", "ch")
+FIRST_Z = 8
+COLUMNS = [
+    [((x * 16 + (z + FIRST_Z) % 16) * 2 + yh) * 4 + q for z in range(16) for q in range(4)]
+    for x in range(4)
+    for yh in range(2)
+]
 VMEM = pl.BlockSpec(memory_space=pltpu.VMEM)
 HBM = pl.BlockSpec(memory_space=pltpu.HBM)
 
@@ -180,7 +187,9 @@
     rows = []
     for q in range(4):
         for c in range(4):
-            pieces = [got_ref[z * 4 + q].astype(f32)[:, c * 32 : c * 32 + 32] for z in range(16)]
+            pieces = [
+                got_ref[(z - FIRST_Z) % 16 * 4 + q].astype(f32)[:, c * 32 : c * 32 + 32] for z in range(16)
+            ]
             rows.append(lanes(pieces))
     z0 = jnp.concatenate(rows, axis=0)
     z_ref[...] = z0
@@ -323,7 +332,7 @@
         w_out.reshape(64, 128),
     )
     send, *args = lax.optimization_barrier((send, *args))
-    got = lax.all_to_all(send, ("z", "ch"), 0, 0, tiled=True)
+    got = lax.all_to_all(send, ALL, 0, 0, axis_index_groups=COLUMNS, tiled=True)
     packed, gains, pm, same = prepare(*args)
     packed = lax.all_gather(packed, "ch", axis=0)
     cols, wo, own, back = call(

time: 90.6 us -> 84.9 us (0.937)
  waiting for transfers between devices: 9.03 us -> 0.01 us
  starting transfers between devices: 18.3 us -> 21.8 us
    all_to_all x1, waiting for transfers between devices: 9.03 us -> 0.01 us  [body(): got = lax.all_to_all(send, ALL, 0, 0, axis_index_groups=COLUMNS, tiled=True)]
    all_to_all x1, starting transfers between devices: 18.3 us -> 21.8 us  [body(): got = lax.all_to_all(send, ALL, 0, 0, axis_index_groups=COLUMNS, tiled=True)]
  transfers between devices with their start and end apart: 1 -> 1, of which waited for: 1 -> 0; matrix products, arithmetic and copies ran while one was open for 0% -> 0% of each run, Pallas kernels for 1% -> 1%
where the time goes in v10:
time: 84.9 us; the launch traced here: 84.6 us
  blocking collectives  56.1 us (66%)
  starting transfers between devices  21.8 us (26%)
  Pallas kernels  5.66 us (7%)
    all_to_all x3, blocking collectives, body(): got = lax.all_to_all(send, PLANE, 0, 0, tiled=True)  40.1 us
    all_to_all x1, starting transfers between devices, body(): got = lax.all_to_all(send, ALL, 0, 0, axis_index_groups=COLUMNS, tiled=True)  21.8 us
    all_to_all x1, blocking collectives, body(): got = lax.all_to_all(send, ('x', 'ch'), 0, 0, tiled=True)  8.51 us
    all_gather x1, blocking collectives, body(): packed = lax.all_gather(packed, 'ch', axis=0)  7.47 us
    pallas_call x6, Pallas kernels, call(): pl.pallas_call(kernel, out_shape=[jax.ShapeDtypeStruct(s, d) for s, d in...  4.17 us
  transfers between devices with their start and end apart: 1, of which 0 were waited for; matrix products, arithmetic and copies ran while one was open for 0% of the time, Pallas kernels for 1%

profile of v10, /device:TPU:1, one launch (start us, length us, event | category | flops | bytes accessed | tf_op | source)
XLA Modules:
  0.0 84.6 jit_solution(16297055263345204413)
XLA Ops:
  0.0 0.7 copy-done.3
  0.7 1.0 %shard_map.109 = bf16[64,8,128]{2,1,0:T(8,128)(2,1)} custom-call(bf16[32,128]{1,0:T(8,128)(2,1)S(1)} %bitcast.19), custom_call_target="tpu_custom_call" | custom-call | tf_op jit(solution)/shard_map/pallas_call | solution.py:75
  1.7 0.0 copy-start
  1.7 0.0 copy-start.1
  1.8 0.0 copy-start.2
  1.8 0.0 copy-start.4
  1.8 0.0 copy-start.5
  1.8 0.0 copy-start.6
  1.8 0.0 copy-start.7
  1.8 0.0 copy-start.9
  1.8 0.0 copy-start.10
  1.9 21.8 %all-to-all-start = ((bf16[64,8,128]{2,1,0:T(8,128)(2,1)}), bf16[64,8,128]{2,1,0:T(8,128)(2,1)S(1)}, u32[]{:S(2)}, u32[]{:S(2)}) async-start(bf16[64,8,128]{2,1,0:T(8,128)(2,1)} %shard_map.109), calls=%async_computation | async-start | bytes 262144 | tf_op jit(solution)/shard_map/all_to_all | solution.py:335
  23.8 0.5 shard_map.110
  24.2 7.5 %all-gather = bf16[1664,128]{1,0:T(8,128)(2,1)S(1)} all-gather(bf16[416,128]{1,0:T(8,128)(2,1)S(1)} %get-tuple-element.50), channel_id=2, replica_groups=mesh['x'=4,'z'=16,'yh'=2,'ch'=4] {'ch'}, dimensions={0}, use_global_device_ids=true | all-gather | bytes 532480 | tf_op jit(solution)/shard_map/all_gather | solution.py:337
  31.7 0.1 shard_map.111
  31.8 1.0 %shard_map.112 = (bf16[32,32,128]{2,1,0:T(8,128)(2,1)S(1)}, f32[128,512]{1,0:T(8,128)S(1)}, f32[128,512]{1,0:T(8,128)S(1)}) custom-call(bf16[64,8,128]{2,1,0:T(8,128)(2,1)S(1)} %all-to-all-done.got_ref, f32[128,8]{1,0:T(8,128)S(1)} %get-tuple-element.59.gain_ref, f32[128,8]{1,0:T(8,128)S(1)} %get-tuple-element.60.cols_ref, ...), custom_call_target="tpu_custom_call" | custom-call | flops 100000000 | bytes 569344 | tf_op jit(solution)/shard_map/pallas_call | solution.py:26
  32.8 15.8 %all_to_all.25.got_ref = bf16[32,32,128]{2,1,0:T(8,128)(2,1)S(1)} all-to-all(bf16[32,32,128]{2,1,0:T(8,128)(2,1)S(1)} %get-tuple-element.64), channel_id=1, replica_groups=mesh['x'=4,'z'=16,'yh'=2,'ch'=4] {'x','yh','ch'}, dimensions={0} | all-to-all | bytes 524288 | tf_op jit(solution)/shard_map/all_to_all | solution.py:353
  48.6 0.3 shard_map.113
  48.9 11.2 %all_to_all.26.got_ref = bf16[32,16,128]{2,1,0:T(8,128)(2,1)S(1)} all-to-all(bf16[32,16,128]{2,1,0:T(8,128)(2,1)S(1)} %shard_map.113), channel_id=1, replica_groups=mesh['x'=4,'z'=16,'yh'=2,'ch'=4] {'x','yh','ch'}, dimensions={0} | all-to-all | bytes 262144 | tf_op jit(solution)/shard_map/all_to_all | solution.py:355
  60.0 1.1 %shard_map.114 = (bf16[32,40,128]{2,1,0:T(8,128)(2,1)S(1)}, bf16[128,512]{1,0:T(8,128)(2,1)S(1)}, bf16[128,512]{1,0:T(8,128)(2,1)S(1)}) custom-call(bf16[32,16,128]{2,1,0:T(8,128)(2,1)S(1)} %all_to_all.26.got_ref, f32[128,512]{1,0:T(8,128)S(1)} %get-tuple-element.65.z_ref, f32[128,512]{1,0:T(8,128)S(1)} %get-tuple-element.66.gate_ref, ...), custom_call_target="tpu_custom_call" | custom-call | flops 100000000 | bytes 1124352 | tf_op jit(solution)/shard_map/pallas_call | solution.py:26
  61.2 13.2 %all_to_all.27.got_ref = bf16[32,40,128]{2,1,0:T(8,128)(2,1)S(1)} all-to-all(bf16[32,40,128]{2,1,0:T(8,128)(2,1)S(1)} %get-tuple-element.68), channel_id=1, replica_groups=mesh['x'=4,'z'=16,'yh'=2,'ch'=4] {'x','yh','ch'}, dimensions={0} | all-to-all | bytes 655360 | tf_op jit(solution)/shard_map/all_to_all | solution.py:361
  74.4 0.7 shard_map.115
  75.1 8.5 %all_to_all.28.got_ref = bf16[16,24,128]{2,1,0:T(8,128)(2,1)S(1)} all-to-all(bf16[16,24,128]{2,1,0:T(8,128)(2,1)S(1)} %shard_map.115), channel_id=1, replica_groups=mesh['x'=4,'z'=16,'yh'=2,'ch'=4] {'x','ch'}, dimensions={0} | all-to-all | bytes 196608 | tf_op jit(solution)/shard_map/all_to_all | solution.py:363
  83.6 1.0 %shard_map.116 = bf16[32,128]{1,0:T(8,128)(2,1)} custom-call(bf16[16,24,128]{2,1,0:T(8,128)(2,1)S(1)} %all_to_all.28.got_ref, f32[128,8]{1,0:T(8,128)S(1)} %get-tuple-element.60.cols_ref, bf16[32,128]{1,0:T(8,128)(2,1)S(1)} %get-tuple-element.71.own_ref, bf16[128,128]{1,0:T(8,128)(2,1)S(1)} %get-tuple-element.72.back_ref), custom_call_target="tpu_custom_call" | custom-call | flops 100000000 | bytes 143360 | tf_op jit(solution)/shard_map/pallas_call | solution.py:26
  (13 shorter events, 0.0 us)
Async XLA Ops:
  0.0 0.7 copy-start.3
  1.7 21.9 %copy-start = (bf16[2,128,4,32]{1,3,2,0:T(8,128)(2,1)S(1)}, bf16[2,128,4,32]{1,3,2,0:T(8,128)(2,1)}, u32[]{:S(2)}) copy-start(bf16[2,128,4,32]{1,3,2,0:T(8,128)(2,1)} %param.16) | copy-start | bytes 196612
  1.7 21.9 %copy-start.1 = (bf16[2,128,32]{1,2,0:T(8,128)(2,1)S(1)}, bf16[2,128,32]{1,2,0:T(8,128)(2,1)}, u32[]{:S(2)}) copy-start(bf16[2,128,32]{1,2,0:T(8,128)(2,1)} %param.17) | copy-start | bytes 49156
  1.8 21.9 %copy-start.2 = (bf16[2,32,128]{2,1,0:T(8,128)(2,1)S(1)}, bf16[2,32,128]{2,1,0:T(8,128)(2,1)}, u32[]{:S(2)}) copy-start(bf16[2,32,128]{2,1,0:T(8,128)(2,1)} %param.21) | copy-start | bytes 49156
  1.8 21.9 %copy-start.4 = (f32[2,128]{1,0:T(2,128)S(1)}, f32[2,128]{1,0:T(2,128)}, u32[]{:S(2)}) copy-start(f32[2,128]{1,0:T(2,128)} %gain_ref) | copy-start | bytes 3076
  1.8 21.9 %copy-start.5 = (f32[2,128]{1,0:T(2,128)S(1)}, f32[2,128]{1,0:T(2,128)}, u32[]{:S(2)}) copy-start(f32[2,128]{1,0:T(2,128)} %bias_ref) | copy-start | bytes 3076
  1.8 21.9 %copy-start.6 = (f32[2,32]{1,0:T(2,128)S(1)}, f32[2,32]{1,0:T(2,128)}, u32[]{:S(2)}) copy-start(f32[2,32]{1,0:T(2,128)} %pb_ref) | copy-start | bytes 772
  1.8 21.9 %copy-start.7 = (f32[2,32]{1,0:T(2,128)S(1)}, f32[2,32]{1,0:T(2,128)}, u32[]{:S(2)}) copy-start(f32[2,32]{1,0:T(2,128)} %og_ref) | copy-start | bytes 772
  1.8 21.9 %copy-start.8 = (f32[2,32]{1,0:T(2,128)S(1)}, f32[2,32]{1,0:T(2,128)}, u32[]{:S(2)}) copy-start(f32[2,32]{1,0:T(2,128)} %ob_ref) | copy-start | bytes 772
  1.8 21.9 %copy-start.9 = (s32[128]{0:T(128)S(1)}, s32[128]{0:T(128)}, u32[]{:S(2)}) copy-start(s32[128]{0:T(128)} %param.12) | copy-start | bytes 1540
  1.8 21.9 %copy-start.10 = (s32[128]{0:T(128)S(1)}, s32[128]{0:T(128)}, u32[]{:S(2)}) copy-start(s32[128]{0:T(128)} %param.13) | copy-start | bytes 1540
  1.9 30.0 %all-to-all-start = ((bf16[64,8,128]{2,1,0:T(8,128)(2,1)}), bf16[64,8,128]{2,1,0:T(8,128)(2,1)S(1)}, u32[]{:S(2)}, u32[]{:S(2)}) async-start(bf16[64,8,128]{2,1,0:T(8,128)(2,1)} %shard_map.109), calls=%async_computation | async-start | bytes 262144 | tf_op jit(solution)/shard_map/all_to_all | solution.py:335

commit v11 on v10

--- a/solution.py
+++ b/solution.py
@@ -9,13 +9,15 @@
 bf16 = jnp.bfloat16
 f32 = jnp.float32
 ROW = ("x", "z", "yh")
-PLANE = ("x", "yh", "ch")
 ALL = ("x", "z", "yh", "ch")
 FIRST_Z = 8
 COLUMNS = [
     [((x * 16 + (z + FIRST_Z) % 16) * 2 + yh) * 4 + q for z in range(16) for q in range(4)]
     for x in range(4)
     for yh in range(2)
+]
+PLANES = [
+    [((d // 8 * 16 + z) * 2 + d // 4 % 2) * 4 + d % 4 for d in (p ^ 20 for p in range(32))] for z in range(16)
 ]
 VMEM = pl.BlockSpec(memory_space=pltpu.VMEM)
 HBM = pl.BlockSpec(memory_space=pltpu.HBM)
@@ -206,15 +208,15 @@
     same = row == lane
     left, right = [], []
     for q in range(4):
-        left.append(jnp.concatenate([got_ref[a * 4 + q, 0:16, :] for a in range(8)], axis=0))
-        right.append(jnp.concatenate([got_ref[a * 4 + q, 16:32, :] for a in range(8)], axis=0))
+        left.append(jnp.concatenate([got_ref[a * 4 + q ^ 20, 0:16, :] for a in range(8)], axis=0))
+        right.append(jnp.concatenate([got_ref[a * 4 + q ^ 20, 16:32, :] for a in range(8)], axis=0))
     left, right = lanes(left), lanes(right)
     for q in range(4):
         part = right[q * 32 : q * 32 + 32].astype(f32)
         block = jnp.where(same, jnp.concatenate([part] * 4, axis=0), 0.0).astype(bf16)
         x = nt(left, block).astype(bf16)
         for b in range(8):
-            out_ref[b * 4 + q] = x[b * 16 : b * 16 + 16]
+            out_ref[b * 4 + q ^ 20] = x[b * 16 : b * 16 + 16]
 
 
 def middle_kernel(got_ref, z_ref, gate_ref, gain_ref, cols_ref, wo_ref, w_ref, pm_ref, out_ref, z1_ref, n1_ref):
@@ -239,7 +241,7 @@
     for g in range(16):
         marks = jnp.where(first, v[g, 16:24], v[16 + g, 16:24]).astype(bf16)
         for yh in range(2):
-            at = (g // 4) * 8 + yh * 4 + g % 4
+            at = (g // 4 * 8 + yh * 4 + g % 4) ^ 20
             out_ref[at, 0:16, :] = v[g, 0:16].astype(bf16)
             out_ref[at, 16:32, :] = v[16 + g, 0:16].astype(bf16)
             out_ref[at, 32:40, :] = marks
@@ -250,7 +252,7 @@
     right = [
         lanes(
             [
-                jnp.concatenate([got_ref[a * 4 + q, h * 16 : h * 16 + 16, :] for a in range(8)], axis=0)
+                jnp.concatenate([got_ref[a * 4 + q ^ 20, h * 16 : h * 16 + 16, :] for a in range(8)], axis=0)
                 for h in range(2)
             ]
         )
@@ -261,7 +263,7 @@
     wanted = ((row >> 3) == (lane >> 5)) & (((lane >> 4) & 1) == lax.axis_index("yh"))
     parts = []
     for a in range(8):
-        tiles = [got_ref[a * 4 + x, 32:40, :].astype(f32) for x in range(4)]
+        tiles = [got_ref[a * 4 + x ^ 20, 32:40, :].astype(f32) for x in range(4)]
         rows = jnp.concatenate([t[h : h + 1] for h in range(2) for t in tiles], axis=0)
         parts.append(jnp.where(wanted, jnp.concatenate([rows] * 4, axis=0), 0.0).astype(bf16))
     source = lax.broadcasted_iota(jnp.int32, (1024, 128), 0)
@@ -350,15 +352,15 @@
         [((32, 32, 128), bf16), ((128, 512), f32), ((128, 512), f32)],
         [got, gains, cols, packed, pm, same],
     )
-    got = lax.all_to_all(send, PLANE, 0, 0, tiled=True)
+    got = lax.all_to_all(send, ALL, 0, 0, axis_index_groups=PLANES, tiled=True)
     (send,) = call(outgoing_kernel, [((32, 16, 128), bf16)], [got])
-    got = lax.all_to_all(send, PLANE, 0, 0, tiled=True)
+    got = lax.all_to_all(send, ALL, 0, 0, axis_index_groups=PLANES, tiled=True)
     send, z1, n1 = call(
         middle_kernel,
         [((32, 40, 128), bf16), ((128, 512), bf16), ((128, 512), bf16)],
         [got, z0, gate, gains, cols, wo, packed, pm],
     )
-    got = lax.all_to_all(send, PLANE, 0, 0, tiled=True)
+    got = lax.all_to_all(send, ALL, 0, 0, axis_index_groups=PLANES, tiled=True)
     (send,) = call(incoming_kernel, [((16, 24, 128), bf16)], [got, z1, n1, cols, packed, same])
     got = lax.all_to_all(send, ("x", "ch"), 0, 0, tiled=True)
     (out,) = call(last_kernel, [((32, 128), bf16)], [got, cols, own, back])

time: 84.9 us -> 84 us (0.989)
  blocking collectives: 56.1 us -> 55.2 us
    all_to_all x3, blocking collectives: 40.1 us -> 36.3 us  [body(): got = lax.all_to_all(send, ALL, 0, 0, axis_index_groups=PLANES, tiled=True)]
    all_to_all x1, blocking collectives: 8.51 us -> 11.4 us  [body(): got = lax.all_to_all(send, ('x', 'ch'), 0, 0, tiled=True)]
where the time goes in v11:
time: 84 us; the launch traced here: 83.6 us
  blocking collectives  55.2 us (66%)
  starting transfers between devices  21.8 us (26%)
  Pallas kernels  5.66 us (7%)
    all_to_all x3, blocking collectives, body(): got = lax.all_to_all(send, ALL, 0, 0, axis_index_groups=PLANES, tiled=True)  36.3 us
    all_to_all x1, starting transfers between devices, body(): got = lax.all_to_all(send, ALL, 0, 0, axis_index_groups=COLUMNS, tiled=True)  21.8 us
    all_to_all x1, blocking collectives, body(): got = lax.all_to_all(send, ('x', 'ch'), 0, 0, tiled=True)  11.4 us
    all_gather x1, blocking collectives, body(): packed = lax.all_gather(packed, 'ch', axis=0)  7.47 us
    pallas_call x6, Pallas kernels, call(): pl.pallas_call(kernel, out_shape=[jax.ShapeDtypeStruct(s, d) for s, d in...  4.18 us
  transfers between devices with their start and end apart: 1, of which 0 were waited for; matrix products, arithmetic and copies ran while one was open for 0% of the time, Pallas kernels for 1%

profile of v11, /device:TPU:1, one launch (start us, length us, event | category | flops | bytes accessed | tf_op | source)
XLA Modules:
  0.0 83.6 jit_solution(6182825015482883589)
XLA Ops:
  0.0 0.7 copy-done.3
  0.7 1.0 %shard_map.109 = bf16[64,8,128]{2,1,0:T(8,128)(2,1)} custom-call(bf16[32,128]{1,0:T(8,128)(2,1)S(1)} %bitcast.19), custom_call_target="tpu_custom_call" | custom-call | tf_op jit(solution)/shard_map/pallas_call | solution.py:77
  1.7 0.0 copy-start
  1.7 0.0 copy-start.1
  1.8 0.0 copy-start.2
  1.8 0.0 copy-start.4
  1.8 0.0 copy-start.5
  1.8 0.0 copy-start.6
  1.8 0.0 copy-start.7
  1.8 0.0 copy-start.9
  1.8 0.0 copy-start.10
  1.9 21.8 %all-to-all-start = ((bf16[64,8,128]{2,1,0:T(8,128)(2,1)}), bf16[64,8,128]{2,1,0:T(8,128)(2,1)S(1)}, u32[]{:S(2)}, u32[]{:S(2)}) async-start(bf16[64,8,128]{2,1,0:T(8,128)(2,1)} %shard_map.109), calls=%async_computation | async-start | bytes 262144 | tf_op jit(solution)/shard_map/all_to_all | solution.py:337
  23.8 0.5 shard_map.110
  24.2 7.5 %all-gather = bf16[1664,128]{1,0:T(8,128)(2,1)S(1)} all-gather(bf16[416,128]{1,0:T(8,128)(2,1)S(1)} %get-tuple-element.50), channel_id=2, replica_groups=mesh['x'=4,'z'=16,'yh'=2,'ch'=4] {'ch'}, dimensions={0}, use_global_device_ids=true | all-gather | bytes 532480 | tf_op jit(solution)/shard_map/all_gather | solution.py:339
  31.7 0.1 shard_map.111
  31.8 1.0 %shard_map.112 = (bf16[32,32,128]{2,1,0:T(8,128)(2,1)S(1)}, f32[128,512]{1,0:T(8,128)S(1)}, f32[128,512]{1,0:T(8,128)S(1)}) custom-call(bf16[64,8,128]{2,1,0:T(8,128)(2,1)S(1)} %all-to-all-done.got_ref, f32[128,8]{1,0:T(8,128)S(1)} %get-tuple-element.59.gain_ref, f32[128,8]{1,0:T(8,128)S(1)} %get-tuple-element.60.cols_ref, ...), custom_call_target="tpu_custom_call" | custom-call | flops 100000000 | bytes 569344 | tf_op jit(solution)/shard_map/pallas_call | solution.py:28
  32.8 12.6 %all_to_all.25.got_ref = bf16[32,32,128]{2,1,0:T(8,128)(2,1)S(1)} all-to-all(bf16[32,32,128]{2,1,0:T(8,128)(2,1)S(1)} %get-tuple-element.64), channel_id=1, replica_groups={{260,261,262,263,256,257,258,259,388,389,390,391,384,385,386,387,4,5,6,..., dimensions={0} | all-to-all | bytes 524288 | tf_op jit(solution)/shard_map/all_to_all | solution.py:355
  45.4 0.3 shard_map.113
  45.7 11.0 %all_to_all.26.got_ref = bf16[32,16,128]{2,1,0:T(8,128)(2,1)S(1)} all-to-all(bf16[32,16,128]{2,1,0:T(8,128)(2,1)S(1)} %shard_map.113), channel_id=1, replica_groups={{260,261,262,263,256,257,258,259,388,389,390,391,384,385,386,387,4,5,6,..., dimensions={0} | all-to-all | bytes 262144 | tf_op jit(solution)/shard_map/all_to_all | solution.py:357
  56.7 1.1 %shard_map.114 = (bf16[32,40,128]{2,1,0:T(8,128)(2,1)S(1)}, bf16[128,512]{1,0:T(8,128)(2,1)S(1)}, bf16[128,512]{1,0:T(8,128)(2,1)S(1)}) custom-call(bf16[32,16,128]{2,1,0:T(8,128)(2,1)S(1)} %all_to_all.26.got_ref, f32[128,512]{1,0:T(8,128)S(1)} %get-tuple-element.65.z_ref, f32[128,512]{1,0:T(8,128)S(1)} %get-tuple-element.66.gate_ref, ...), custom_call_target="tpu_custom_call" | custom-call | flops 100000000 | bytes 1124352 | tf_op jit(solution)/shard_map/pallas_call | solution.py:28
  57.8 12.8 %all_to_all.27.got_ref = bf16[32,40,128]{2,1,0:T(8,128)(2,1)S(1)} all-to-all(bf16[32,40,128]{2,1,0:T(8,128)(2,1)S(1)} %get-tuple-element.68), channel_id=1, replica_groups={{260,261,262,263,256,257,258,259,388,389,390,391,384,385,386,387,4,5,6,..., dimensions={0} | all-to-all | bytes 655360 | tf_op jit(solution)/shard_map/all_to_all | solution.py:363
  70.6 0.7 shard_map.115
  71.3 11.4 %all_to_all.28.got_ref = bf16[16,24,128]{2,1,0:T(8,128)(2,1)S(1)} all-to-all(bf16[16,24,128]{2,1,0:T(8,128)(2,1)S(1)} %shard_map.115), channel_id=1, replica_groups=mesh['x'=4,'z'=16,'yh'=2,'ch'=4] {'x','ch'}, dimensions={0} | all-to-all | bytes 196608 | tf_op jit(solution)/shard_map/all_to_all | solution.py:365
  82.7 1.0 %shard_map.116 = bf16[32,128]{1,0:T(8,128)(2,1)} custom-call(bf16[16,24,128]{2,1,0:T(8,128)(2,1)S(1)} %all_to_all.28.got_ref, f32[128,8]{1,0:T(8,128)S(1)} %get-tuple-element.60.cols_ref, bf16[32,128]{1,0:T(8,128)(2,1)S(1)} %get-tuple-element.71.own_ref, bf16[128,128]{1,0:T(8,128)(2,1)S(1)} %get-tuple-element.72.back_ref), custom_call_target="tpu_custom_call" | custom-call | flops 100000000 | bytes 143360 | tf_op jit(solution)/shard_map/pallas_call | solution.py:28
  (13 shorter events, 0.0 us)
Async XLA Ops:
  0.0 0.7 copy-start.3
  1.7 21.9 %copy-start = (bf16[2,128,4,32]{1,3,2,0:T(8,128)(2,1)S(1)}, bf16[2,128,4,32]{1,3,2,0:T(8,128)(2,1)}, u32[]{:S(2)}) copy-start(bf16[2,128,4,32]{1,3,2,0:T(8,128)(2,1)} %param.16) | copy-start | bytes 196612
  1.7 21.9 %copy-start.1 = (bf16[2,128,32]{1,2,0:T(8,128)(2,1)S(1)}, bf16[2,128,32]{1,2,0:T(8,128)(2,1)}, u32[]{:S(2)}) copy-start(bf16[2,128,32]{1,2,0:T(8,128)(2,1)} %param.17) | copy-start | bytes 49156
  1.8 21.9 %copy-start.2 = (bf16[2,32,128]{2,1,0:T(8,128)(2,1)S(1)}, bf16[2,32,128]{2,1,0:T(8,128)(2,1)}, u32[]{:S(2)}) copy-start(bf16[2,32,128]{2,1,0:T(8,128)(2,1)} %param.21) | copy-start | bytes 49156
  1.8 21.9 %copy-start.4 = (f32[2,128]{1,0:T(2,128)S(1)}, f32[2,128]{1,0:T(2,128)}, u32[]{:S(2)}) copy-start(f32[2,128]{1,0:T(2,128)} %gain_ref) | copy-start | bytes 3076
  1.8 21.9 %copy-start.5 = (f32[2,128]{1,0:T(2,128)S(1)}, f32[2,128]{1,0:T(2,128)}, u32[]{:S(2)}) copy-start(f32[2,128]{1,0:T(2,128)} %bias_ref) | copy-start | bytes 3076
  1.8 21.9 %copy-start.6 = (f32[2,32]{1,0:T(2,128)S(1)}, f32[2,32]{1,0:T(2,128)}, u32[]{:S(2)}) copy-start(f32[2,32]{1,0:T(2,128)} %pb_ref) | copy-start | bytes 772
  1.8 21.9 %copy-start.7 = (f32[2,32]{1,0:T(2,128)S(1)}, f32[2,32]{1,0:T(2,128)}, u32[]{:S(2)}) copy-start(f32[2,32]{1,0:T(2,128)} %og_ref) | copy-start | bytes 772
  1.8 21.9 %copy-start.8 = (f32[2,32]{1,0:T(2,128)S(1)}, f32[2,32]{1,0:T(2,128)}, u32[]{:S(2)}) copy-start(f32[2,32]{1,0:T(2,128)} %ob_ref) | copy-start | bytes 772
  1.8 21.9 %copy-start.9 = (s32[128]{0:T(128)S(1)}, s32[128]{0:T(128)}, u32[]{:S(2)}) copy-start(s32[128]{0:T(128)} %param.12) | copy-start | bytes 1540
  1.8 21.9 %copy-start.10 = (s32[128]{0:T(128)S(1)}, s32[128]{0:T(128)}, u32[]{:S(2)}) copy-start(s32[128]{0:T(128)} %param.13) | copy-start | bytes 1540
  1.9 30.0 %all-to-all-start = ((bf16[64,8,128]{2,1,0:T(8,128)(2,1)}), bf16[64,8,128]{2,1,0:T(8,128)(2,1)S(1)}, u32[]{:S(2)}, u32[]{:S(2)}) async-start(bf16[64,8,128]{2,1,0:T(8,128)(2,1)} %shard_map.109), calls=%async_computation | async-start | bytes 262144 | tf_op jit(solution)/shard_map/all_to_all | solution.py:337

commit v12 on v11

--- a/solution.py
+++ b/solution.py
@@ -18,6 +18,11 @@
 ]
 PLANES = [
     [((d // 8 * 16 + z) * 2 + d // 4 % 2) * 4 + d % 4 for d in (p ^ 20 for p in range(32))] for z in range(16)
+]
+LINES = [
+    [((d // 4 * 16 + z) * 2 + yh) * 4 + d % 4 for d in (p ^ 8 for p in range(16))]
+    for z in range(16)
+    for yh in range(2)
 ]
 VMEM = pl.BlockSpec(memory_space=pltpu.VMEM)
 HBM = pl.BlockSpec(memory_space=pltpu.HBM)
@@ -297,17 +302,17 @@
             for v in (z1, gate)
         )
         for a in range(4):
-            out_ref[a * 4 + q, 0:8, :] = x[a]
-            out_ref[a * 4 + q, 8:16, :] = zq
-            out_ref[a * 4 + q, 16:24, :] = gq
+            out_ref[a * 4 + q ^ 8, 0:8, :] = x[a]
+            out_ref[a * 4 + q ^ 8, 8:16, :] = zq
+            out_ref[a * 4 + q ^ 8, 16:24, :] = gq
 
 
 def last_kernel(got_ref, cols_ref, own_ref, back_ref, out_ref):
     x = jnp.swapaxes(got_ref[:, 0:8, :].astype(f32), 0, 1)
-    x1 = jnp.concatenate([x[h * 4 + d] for d in range(4) for h in range(2)], axis=0)
+    x1 = jnp.concatenate([x[h * 4 + d, g : g + 8] for d in range(4) for h in range(2) for g in (8, 0)], axis=0)
     xn = norm(x1, cols_ref[:, 1:2], cols_ref[:, 3:4])
     y = jnp.dot(own_ref[...], xn, preferred_element_type=f32)
-    home = lax.axis_index("x") * 4
+    home = (lax.axis_index("x") ^ 2) * 4
     own = [got_ref[home + s].astype(f32) for s in range(4)]
     z1, gate = (
         jnp.concatenate(
@@ -362,7 +367,7 @@
     )
     got = lax.all_to_all(send, ALL, 0, 0, axis_index_groups=PLANES, tiled=True)
     (send,) = call(incoming_kernel, [((16, 24, 128), bf16)], [got, z1, n1, cols, packed, same])
-    got = lax.all_to_all(send, ("x", "ch"), 0, 0, tiled=True)
+    got = lax.all_to_all(send, ALL, 0, 0, axis_index_groups=LINES, tiled=True)
     (out,) = call(last_kernel, [((32, 128), bf16)], [got, cols, own, back])
     return out.reshape(32, 1, 128)
 

time: 84 us -> 82.3 us (0.980)
  blocking collectives: 55.2 us -> 53.5 us
    all_to_all x1, blocking collectives: 11.4 us -> 9.65 us  [body(): got = lax.all_to_all(send, ALL, 0, 0, axis_index_groups=LINES, tiled=True)]
where the time goes in v12:
time: 82.3 us; the launch traced here: 81.9 us
  blocking collectives  53.5 us (65%)
  starting transfers between devices  21.8 us (26%)
  Pallas kernels  5.66 us (7%)
    all_to_all x3, blocking collectives, body(): got = lax.all_to_all(send, ALL, 0, 0, axis_index_groups=PLANES, tiled=True)  36.3 us
    all_to_all x1, starting transfers between devices, body(): got = lax.all_to_all(send, ALL, 0, 0, axis_index_groups=COLUMNS, tiled=True)  21.8 us
    all_to_all x1, blocking collectives, body(): got = lax.all_to_all(send, ALL, 0, 0, axis_index_groups=LINES, tiled=True)  9.65 us
    all_gather x1, blocking collectives, body(): packed = lax.all_gather(packed, 'ch', axis=0)  7.47 us
    pallas_call x6, Pallas kernels, call(): pl.pallas_call(kernel, out_shape=[jax.ShapeDtypeStruct(s, d) for s, d in...  4.18 us
  transfers between devices with their start and end apart: 1, of which 0 were waited for; matrix products, arithmetic and copies ran while one was open for 0% of the time, Pallas kernels for 1%

profile of v12, /device:TPU:1, one launch (start us, length us, event | category | flops | bytes accessed | tf_op | source)
XLA Modules:
  0.0 81.9 jit_solution(11104686617950814544)
XLA Ops:
  0.0 0.7 copy-done.3
  0.7 1.0 %shard_map.109 = bf16[64,8,128]{2,1,0:T(8,128)(2,1)} custom-call(bf16[32,128]{1,0:T(8,128)(2,1)S(1)} %bitcast.19), custom_call_target="tpu_custom_call" | custom-call | tf_op jit(solution)/shard_map/pallas_call | solution.py:82
  1.7 0.0 copy-start
  1.7 0.0 copy-start.1
  1.8 0.0 copy-start.2
  1.8 0.0 copy-start.4
  1.8 0.0 copy-start.5
  1.8 0.0 copy-start.6
  1.8 0.0 copy-start.7
  1.8 0.0 copy-start.8
  1.8 0.0 copy-start.10
  1.9 21.8 %all-to-all-start = ((bf16[64,8,128]{2,1,0:T(8,128)(2,1)}), bf16[64,8,128]{2,1,0:T(8,128)(2,1)S(1)}, u32[]{:S(2)}, u32[]{:S(2)}) async-start(bf16[64,8,128]{2,1,0:T(8,128)(2,1)} %shard_map.109), calls=%async_computation | async-start | bytes 262144 | tf_op jit(solution)/shard_map/all_to_all | solution.py:342
  23.8 0.5 shard_map.110
  24.2 7.5 %all-gather = bf16[1664,128]{1,0:T(8,128)(2,1)S(1)} all-gather(bf16[416,128]{1,0:T(8,128)(2,1)S(1)} %get-tuple-element.50), channel_id=2, replica_groups=mesh['x'=4,'z'=16,'yh'=2,'ch'=4] {'ch'}, dimensions={0}, use_global_device_ids=true | all-gather | bytes 532480 | tf_op jit(solution)/shard_map/all_gather | solution.py:344
  31.7 0.1 shard_map.111
  31.8 1.0 %shard_map.112 = (bf16[32,32,128]{2,1,0:T(8,128)(2,1)S(1)}, f32[128,512]{1,0:T(8,128)S(1)}, f32[128,512]{1,0:T(8,128)S(1)}) custom-call(bf16[64,8,128]{2,1,0:T(8,128)(2,1)S(1)} %all-to-all-done.got_ref, f32[128,8]{1,0:T(8,128)S(1)} %get-tuple-element.59.gain_ref, f32[128,8]{1,0:T(8,128)S(1)} %get-tuple-element.60.cols_ref, ...), custom_call_target="tpu_custom_call" | custom-call | flops 100000000 | bytes 569344 | tf_op jit(solution)/shard_map/pallas_call | solution.py:33
  32.8 12.6 %all_to_all.25.got_ref = bf16[32,32,128]{2,1,0:T(8,128)(2,1)S(1)} all-to-all(bf16[32,32,128]{2,1,0:T(8,128)(2,1)S(1)} %get-tuple-element.64), channel_id=1, replica_groups={{260,261,262,263,256,257,258,259,388,389,390,391,384,385,386,387,4,5,6,..., dimensions={0} | all-to-all | bytes 524288 | tf_op jit(solution)/shard_map/all_to_all | solution.py:360
  45.4 0.3 shard_map.113
  45.7 11.0 %all_to_all.26.got_ref = bf16[32,16,128]{2,1,0:T(8,128)(2,1)S(1)} all-to-all(bf16[32,16,128]{2,1,0:T(8,128)(2,1)S(1)} %shard_map.113), channel_id=1, replica_groups={{260,261,262,263,256,257,258,259,388,389,390,391,384,385,386,387,4,5,6,..., dimensions={0} | all-to-all | bytes 262144 | tf_op jit(solution)/shard_map/all_to_all | solution.py:362
  56.7 1.1 %shard_map.114 = (bf16[32,40,128]{2,1,0:T(8,128)(2,1)S(1)}, bf16[128,512]{1,0:T(8,128)(2,1)S(1)}, bf16[128,512]{1,0:T(8,128)(2,1)S(1)}) custom-call(bf16[32,16,128]{2,1,0:T(8,128)(2,1)S(1)} %all_to_all.26.got_ref, f32[128,512]{1,0:T(8,128)S(1)} %get-tuple-element.65.z_ref, f32[128,512]{1,0:T(8,128)S(1)} %get-tuple-element.66.gate_ref, ...), custom_call_target="tpu_custom_call" | custom-call | flops 100000000 | bytes 1124352 | tf_op jit(solution)/shard_map/pallas_call | solution.py:33
  57.8 12.8 %all_to_all.27.got_ref = bf16[32,40,128]{2,1,0:T(8,128)(2,1)S(1)} all-to-all(bf16[32,40,128]{2,1,0:T(8,128)(2,1)S(1)} %get-tuple-element.68), channel_id=1, replica_groups={{260,261,262,263,256,257,258,259,388,389,390,391,384,385,386,387,4,5,6,..., dimensions={0} | all-to-all | bytes 655360 | tf_op jit(solution)/shard_map/all_to_all | solution.py:368
  70.6 0.7 shard_map.115
  71.3 9.7 %all_to_all.28.got_ref = bf16[16,24,128]{2,1,0:T(8,128)(2,1)S(1)} all-to-all(bf16[16,24,128]{2,1,0:T(8,128)(2,1)S(1)} %shard_map.115), channel_id=1, replica_groups={{256,257,258,259,384,385,386,387,0,1,2,3,128,129,130,131},{260,261,262,..., dimensions={0} | all-to-all | bytes 196608 | tf_op jit(solution)/shard_map/all_to_all | solution.py:370
  81.0 1.0 %shard_map.116 = bf16[32,128]{1,0:T(8,128)(2,1)} custom-call(bf16[16,24,128]{2,1,0:T(8,128)(2,1)S(1)} %all_to_all.28.got_ref, f32[128,8]{1,0:T(8,128)S(1)} %get-tuple-element.60.cols_ref, bf16[32,128]{1,0:T(8,128)(2,1)S(1)} %get-tuple-element.71.own_ref, bf16[128,128]{1,0:T(8,128)(2,1)S(1)} %get-tuple-element.72.back_ref), custom_call_target="tpu_custom_call" | custom-call | flops 100000000 | bytes 143360 | tf_op jit(solution)/shard_map/pallas_call | solution.py:33
  (13 shorter events, 0.0 us)
Async XLA Ops:
  0.0 0.7 copy-start.3
  1.7 21.9 %copy-start = (bf16[2,128,4,32]{1,3,2,0:T(8,128)(2,1)S(1)}, bf16[2,128,4,32]{1,3,2,0:T(8,128)(2,1)}, u32[]{:S(2)}) copy-start(bf16[2,128,4,32]{1,3,2,0:T(8,128)(2,1)} %param.16) | copy-start | bytes 196612
  1.7 21.9 %copy-start.1 = (bf16[2,128,32]{1,2,0:T(8,128)(2,1)S(1)}, bf16[2,128,32]{1,2,0:T(8,128)(2,1)}, u32[]{:S(2)}) copy-start(bf16[2,128,32]{1,2,0:T(8,128)(2,1)} %param.17) | copy-start | bytes 49156
  1.8 21.9 %copy-start.2 = (bf16[2,32,128]{2,1,0:T(8,128)(2,1)S(1)}, bf16[2,32,128]{2,1,0:T(8,128)(2,1)}, u32[]{:S(2)}) copy-start(bf16[2,32,128]{2,1,0:T(8,128)(2,1)} %param.21) | copy-start | bytes 49156
  1.8 21.9 %copy-start.4 = (f32[2,128]{1,0:T(2,128)S(1)}, f32[2,128]{1,0:T(2,128)}, u32[]{:S(2)}) copy-start(f32[2,128]{1,0:T(2,128)} %gain_ref) | copy-start | bytes 3076
  1.8 21.9 %copy-start.5 = (f32[2,128]{1,0:T(2,128)S(1)}, f32[2,128]{1,0:T(2,128)}, u32[]{:S(2)}) copy-start(f32[2,128]{1,0:T(2,128)} %bias_ref) | copy-start | bytes 3076
  1.8 21.9 %copy-start.6 = (f32[2,32]{1,0:T(2,128)S(1)}, f32[2,32]{1,0:T(2,128)}, u32[]{:S(2)}) copy-start(f32[2,32]{1,0:T(2,128)} %pb_ref) | copy-start | bytes 772
  1.8 21.9 %copy-start.7 = (f32[2,32]{1,0:T(2,128)S(1)}, f32[2,32]{1,0:T(2,128)}, u32[]{:S(2)}) copy-start(f32[2,32]{1,0:T(2,128)} %og_ref) | copy-start | bytes 772
  1.8 21.9 %copy-start.8 = (f32[2,32]{1,0:T(2,128)S(1)}, f32[2,32]{1,0:T(2,128)}, u32[]{:S(2)}) copy-start(f32[2,32]{1,0:T(2,128)} %ob_ref) | copy-start | bytes 772
  1.8 21.9 %copy-start.9 = (s32[128]{0:T(128)S(1)}, s32[128]{0:T(128)}, u32[]{:S(2)}) copy-start(s32[128]{0:T(128)} %param.12) | copy-start | bytes 1540
  1.8 21.9 %copy-start.10 = (s32[128]{0:T(128)S(1)}, s32[128]{0:T(128)}, u32[]{:S(2)}) copy-start(s32[128]{0:T(128)} %param.13) | copy-start | bytes 1540
  1.9 30.0 %all-to-all-start = ((bf16[64,8,128]{2,1,0:T(8,128)(2,1)}), bf16[64,8,128]{2,1,0:T(8,128)(2,1)S(1)}, u32[]{:S(2)}, u32[]{:S(2)}) async-start(bf16[64,8,128]{2,1,0:T(8,128)(2,1)} %shard_map.109), calls=%async_computation | async-start | bytes 262144 | tf_op jit(solution)/shard_map/all_to_all | solution.py:342
